TPU v7x, 32 devices: a whole 2x2x4 slice. The times are simulated.
32 devices in a mesh: hour: 2 (over y), stn: 4 (over x, core), tchunk: 4 (over z).
Axes of the slice: x: 2, y: 2, z: 4, core: 2. Of those that a mesh axis runs over, the one named last changes fastest.
Arguments:
- raw_data: float32 [576, 32768], P('stn', ('hour', 'tchunk')), parts along dimension 1, may hold values from -500 to 500, as said below
- station_group: int32 [576], P('stn'), may hold values from 0 to 15
- partner_blocks: int32 [4, 3], P('stn'), may hold values from -1 to 3, as said below
Outputs:
- cross_spectra: float32 [8, 3, 512, 512], P(('hour', 'stn'), None, 'tchunk'), parts along dimension 0
There are 2 independent parts, one for each index of `hour`. A program takes and returns all parts, laid end to end along the dimension named above; an argument that names none is the same for every part. Nothing has to cross between parts.
Inputs may be any that keep to these rules, and one draw needn't show every extreme that they name: `raw_data`: recorded ground motion. `partner_blocks`: row b holds distinct blocks other than b in its first entries and -1 in the rest; every row has at least one partner and some row has 3.
All inputs are finite; a program needn't handle non-finite values.
Results may differ from a plain program's by a relative error of at most 0.0079.
Values may be sent and summed in bfloat16 or wider, within the bound.
No kernel may reach another device: no remote copies, remote signals or barrier semaphores. Data moves between devices by JAX's collectives and lax.ppermute only.
A program may use at most 128 MiB of HBM per device.

v0:
```python
import math

import jax
import jax.numpy as jnp
from jax import lax
from jax.sharding import PartitionSpec as P

SEG_DEV = 2
SEGLEN = 4096
HOP = 2048
NBIN = 512
RB = 128
RAMH = 10
SMOOTH = 8
SUB = 16
MAXP = 3


EPS_MEAN = 1e-06
LEVEL = 0.05


def with_halo(cells, sides, width):
    for axis, dim in sides:
        count = lax.axis_size(axis)
        ends = count - 1
        head = lax.slice_in_dim(cells, 0, width, axis=dim)
        tail = lax.slice_in_dim(cells, cells.shape[dim] - width, cells.shape[dim], axis=dim)
        cells = jnp.concatenate(
            [
                lax.ppermute(tail, axis, [(i, (i + 1) % count) for i in range(ends)]),
                cells,
                lax.ppermute(head, axis, [((i + 1) % count, i) for i in range(ends)]),
            ],
            axis=dim,
        )
    return cells


def from_behind(block, axis, distance):
    devices = range(lax.axis_size(axis))
    route = [(i - distance, i) for i in devices if i - distance in devices]
    return lax.ppermute(block, axis, route)


def dft_table():
    sample = jnp.arange(SEGLEN, dtype=jnp.int32)
    frequency = jnp.arange(1, NBIN + 1, dtype=jnp.int32)
    phases = sample[:, None] * frequency[None, :] % SEGLEN
    angles = phases.astype(jnp.float32) * (2.0 * math.pi / SEGLEN)
    taper_window = 0.5 - 0.5 * jnp.cos(sample.astype(jnp.float32) * (2.0 * math.pi / SEGLEN))
    matrix = jnp.concatenate(
        [taper_window[:, None] * jnp.cos(angles), -taper_window[:, None] * jnp.sin(angles)], axis=1
    )
    return matrix.astype(jnp.bfloat16)


def smooth_table():
    bin_index = jnp.arange(NBIN, dtype=jnp.int32)
    nearby = (jnp.abs(bin_index[:, None] - bin_index[None, :]) <= SMOOTH).astype(jnp.float32)
    return nearby / jnp.sum(nearby, axis=0, keepdims=True)


def whiten(spectra, smoother):
    real_part = spectra[:, :NBIN]
    imag_part = spectra[:, NBIN:]
    powers = real_part * real_part + imag_part * imag_part
    smooth = jnp.dot(powers, smoother, precision=lax.Precision.HIGHEST)
    floor_level = jnp.mean(powers, axis=1, keepdims=True) + 1e-06
    divisor = jnp.sqrt(smooth + LEVEL * floor_level)
    return jnp.concatenate([real_part / divisor, imag_part / divisor], axis=1).astype(jnp.bfloat16)


def cross_terms(mine, others):
    real_part = mine[:, :, 0]
    imag_part = mine[:, :, 1]
    left_side = jnp.stack(
        [jnp.stack([real_part, imag_part], 2), jnp.stack([imag_part, -real_part], 2)], 0
    )
    product = jnp.einsum(
        "oqsck,mrsck->mkoqr", left_side, others, preferred_element_type=jnp.float32
    )
    return product.reshape(product.shape[0], product.shape[1], -1)


def picker(partner_row, chosen, piece):
    count_rows = piece.shape[0]
    picked = []
    for column in range(partner_row.shape[0]):
        offset = partner_row[column]
        inside = (offset >= 0) & (offset < count_rows)
        chosen_piece = lax.dynamic_index_in_dim(
            piece, jnp.clip(offset, 0, count_rows - 1), 0, keepdims=False
        )
        picked.append(jnp.where(inside, chosen_piece, chosen[column]))
    return jnp.stack(picked, 0)


def body(raw_data, station_group, partner_blocks):
    stations, samples = raw_data.shape
    slabs = lax.axis_size("tchunk")
    slab_index = lax.axis_index("tchunk")
    blocks_here = samples // RB
    total_blocks = blocks_here * slabs
    pieces = raw_data.reshape(stations, blocks_here, RB)
    block_sums = jnp.sum(jnp.abs(pieces), axis=2)
    padded = with_halo(block_sums, (("tchunk", 1),), RAMH)
    window = padded[:, 0:blocks_here]
    for offset in range(1, 2 * RAMH):
        window = window + padded[:, offset : offset + blocks_here]
    global_block = slab_index * blocks_here + jnp.arange(blocks_here, dtype=jnp.int32)
    counted = (
        jnp.minimum(global_block + RAMH, total_blocks) - jnp.maximum(global_block - RAMH, 0)
    ).astype(jnp.float32)
    running = window / (RB * counted)
    normalized = (
        (pieces / (running[:, :, None] + EPS_MEAN)).reshape(stations, samples).astype(jnp.bfloat16)
    )
    following = from_behind(normalized[:, :HOP], "tchunk", -1)
    extended = jnp.concatenate([normalized, following], axis=1).reshape(stations, SEG_DEV + 1, HOP)
    segments = jnp.concatenate([extended[:, :-1], extended[:, 1:]], axis=2).reshape(
        stations * SEG_DEV, SEGLEN
    )
    spectra = jnp.dot(segments, dft_table(), preferred_element_type=jnp.float32)
    whitened = whiten(spectra, smooth_table())
    member = (station_group[None, :] == jnp.arange(SUB, dtype=jnp.int32)[:, None]).astype(
        jnp.bfloat16
    )
    beam_sums = jnp.dot(
        member, whitened.reshape(stations, SEG_DEV * 2 * NBIN), preferred_element_type=jnp.float32
    )
    beam_sums = beam_sums.astype(jnp.bfloat16).reshape(SUB, SEG_DEV, 2, NBIN)
    count_segments = SEG_DEV * slabs - 1
    live_segment = slab_index * SEG_DEV + jnp.arange(SEG_DEV, dtype=jnp.int32) < count_segments
    beam_sums = jnp.where(live_segment[None, :, None, None], beam_sums, jnp.zeros_like(beam_sums))
    partner_row = partner_blocks[0]
    spread = lax.all_to_all(beam_sums, "tchunk", split_axis=3, concat_axis=1, tiled=True)
    nothing = jnp.zeros((MAXP,) + spread.shape, jnp.bfloat16)
    others = picker(partner_row, nothing, lax.all_gather(spread[None], "stn", axis=0, tiled=True))
    stacked = cross_terms(spread, others)
    return (stacked / count_segments)[None]


def solution(mesh):
    placed = (P("stn", ("hour", "tchunk")), P("stn"), P("stn", None))
    return jax.shard_map(
        body,
        mesh=mesh,
        in_specs=placed,
        out_specs=P(("hour", "stn"), None, "tchunk", None),
        check_vma=False,
    )
```

profile of v0, /device:TPU:0, one launch (start us, length us, event | category | flops | bytes accessed | tf_op | source)
XLA Modules:
  0.0 111.9 jit_solution(16296220445079391815)
XLA Ops:
  0.0 1.9 %abs_bitcast_fusion = f32[18,8,32,128]{3,1,2,0:T(8,128)S(1)} fusion(f32[144,4096]{1,0:T(8,128)} %param.3), kind=kLoop, calls=%fused_computation.20 | loop fusion | flops 589824 | bytes 4718592
  1.9 0.4 copy.36
  2.3 0.7 reduce_sum.27
  3.1 5.1 %collective-permute-start = (f32[144,10]{1,0:T(8,128)S(1)}, f32[144,10]{1,0:T(8,128)S(1)}, u32[]{:S(2)}, u32[]{:S(2)}) collective-permute-start(f32[144,10]{1,0:T(8,128)S(1)} %get-tuple-element.12), channel_id=1, source_target_pairs={{0,1},{1,2},{2,3},{4,5},{5,6},{6,7},{8,9},{9,10},{10,11},{12,13},{... | collective-permute-start | bytes 17288 | tf_op jit(solution)/shard_map/ppermute | solution.py:31
  8.1 1.3 %collective-permute-start.1 = (f32[144,10]{1,0:T(8,128)S(1)}, f32[144,10]{1,0:T(8,128)S(1)}, u32[]{:S(2)}, u32[]{:S(2)}) collective-permute-start(f32[144,10]{1,0:T(8,128)S(1)} %get-tuple-element.13), channel_id=1, source_target_pairs={{1,0},{2,1},{3,2},{5,4},{6,5},{7,6},{9,8},{10,9},{11,10},{13,12},{... | collective-permute-start | bytes 17288 | tf_op jit(solution)/shard_map/ppermute | solution.py:33
  9.4 0.7 multiply_subtract_fusion
  10.1 0.6 iota_add_fusion
  10.7 3.7 %collective-permute-done.1 = f32[144,10]{1,0:T(8,128)S(1)} collective-permute-done((f32[144,10]{1,0:T(8,128)S(1)}, f32[144,10]{1,0:T(8,128)S(1)}, u32[]{:S(2)}, u32[]{:S(2)}) %collective-permute-start.1) | collective-permute-done | bytes 5792 | tf_op jit(solution)/shard_map/ppermute | solution.py:33
  14.4 0.8 fusion.18
  15.2 0.7 div.51
  15.9 2.2 %fusion.11 = bf16[144,4096]{1,0:T(8,128)(2,1)S(1)} fusion(f32[144,4096]{1,0:T(8,128)S(1)} %copy-done, f32[18,8,32,128]{3,2,1,0:T(8,128)S(1)} %bitcast.41), kind=kLoop, calls=%fused_computation.18 | loop fusion | flops 1179648 | bytes 5898240 | tf_op jit(solution)/shard_map/convert_element_type | solution.py:117
  18.1 1.5 %collective-permute-start.2 = (bf16[144,2048]{1,0:T(8,128)(2,1)S(1)}, bf16[144,2048]{1,0:T(8,128)(2,1)S(1)}, u32[]{:S(2)}, u32[]{:S(2)}) collective-permute-start(bf16[144,2048]{1,0:T(8,128)(2,1)S(1)} %slice.183), channel_id=1, source_target_pairs={{1,0},{2,1},{3,2},{5,4},{6,5},{7,6},{9,8},{10,9},{11,10},{13,12},{... | collective-permute-start | bytes 1769480 | tf_op jit(solution)/shard_map/ppermute | solution.py:43
  19.6 36.3 %multiply_convert_fusion.1 = (bf16[4096,512]{1,0:T(8,128)(2,1)}, bf16[4096,512]{1,0:T(8,128)(2,1)}) fusion(s32[512]{0:T(512)S(1)} %copy-done.2, f32[4096]{0:T(1024)S(1)} %get-tuple-element.21, f32[4096]{0:T(1024)S(1)} %copy-done.1), kind=kLoop, calls=%fused_computation.11 | loop fusion | flops 37748736 | bytes 8423424 | tf_op jit(solution)/shard_map/convert.2
  56.0 1.4 %pad_maximum_fusion.1 = bf16[144,6144]{1,0:T(8,128)(2,1)} fusion(bf16[144,2048]{1,0:T(8,128)(2,1)S(1)} %collective-permute-done.2, bf16[144,4096]{1,0:T(8,128)(2,1)S(1)} %fusion.11), kind=kLoop, calls=%fused_computation.22 | loop fusion | flops 3538944 | bytes 3538944 | tf_op jit(solution)/shard_map/concatenate | solution.py:120
  57.4 4.6 %reshape.108 = bf16[144,3,2048]{2,1,0:T(4,128)(2,1)S(1)} reshape(bf16[144,6144]{1,0:T(8,128)(2,1)} %pad_maximum_fusion.1) | data formatting | bytes 3538944 | tf_op jit(solution)/shard_map/reshape | solution.py:120
  62.1 1.6 %fusion.50 = (bf16[144,2,2048]{2,1,0:T(2,128)(2,1)S(1)}, bf16[144,2,2048]{2,1,0:T(2,128)(2,1)S(1)}) fusion(bf16[144,3,2048]{2,1,0:T(4,128)(2,1)S(1)} %reshape.108), kind=kLoop, calls=%fused_computation.115 | loop fusion | bytes 4718592 | tf_op jit(solution)/shard_map/slice | solution.py:121
  63.7 3.0 %pad_maximum_fusion = bf16[144,2,4096]{2,1,0:T(2,128)(2,1)S(1)} fusion(bf16[144,2,2048]{2,1,0:T(2,128)(2,1)S(1)} %get-tuple-element.6, bf16[144,2,2048]{2,1,0:T(2,128)(2,1)S(1)} %get-tuple-element.5), kind=kLoop, calls=%fused_computation.19 | loop fusion | flops 4718592 | bytes 4718592 | tf_op jit(solution)/shard_map/concatenate | solution.py:121
  66.7 2.4 %reshape.109 = bf16[288,4096]{1,0:T(8,128)(2,1)} reshape(bf16[144,2,4096]{2,1,0:T(2,128)(2,1)S(1)} %pad_maximum_fusion) | data formatting | bytes 4718592 | tf_op jit(solution)/shard_map/reshape | solution.py:121
  69.1 6.7 %fusion.3 = f32[288,1024]{1,0:T(8,128)S(1)} fusion(bf16[288,4096]{1,0:T(8,128)(2,1)} %reshape.109, bf16[4096,512]{1,0:T(8,128)(2,1)} %get-tuple-element.17, bf16[4096,512]{1,0:T(8,128)(2,1)} %get-tuple-element.16), kind=kOutput, calls=%fused_computation.6 | convolution fusion | flops 2432696320 | bytes 11927552 | tf_op jit(solution)/shard_map/dot_general | solution.py:124
  76.0 1.4 %divide_convert_fusion.1 = (bf16[288,512]{1,0:T(8,128)(2,1)S(1)}, bf16[288,512]{1,0:T(8,128)(2,1)S(1)}) fusion(f32[288,1024]{1,0:T(8,128)S(1)} %fusion.3, f32[288]{0:T(512)S(1)} %add_multiply_fusion, f32[512]{0:T(512)S(1)} %convert_reduce_fusion), kind=kOutput, calls=%fused_computation.31 | convolution fusion | flops 908460032 | bytes 2953216 | tf_op jit(solution)/shard_map/dot_general | solution.py:68
  78.3 0.4 copy.22
  78.7 0.5 fusion.54
  79.2 1.2 %reshape.114 = bf16[4,2,4096]{2,1,0:T(2,128)(2,1)} reshape(bf16[512,2,2,16]{3,2,1,0:T(2,128)(2,1)S(1)} %fusion.54) | data formatting | bytes 131072
  80.4 6.0 %all-to-all-start = ((bf16[4,2,4096]{2,1,0:T(2,128)(2,1)}), bf16[4,2,4096]{2,1,0:T(2,128)(2,1)S(1)}, u32[]{:S(2)}, u32[]{:S(2)}) async-start(bf16[4,2,4096]{2,1,0:T(2,128)(2,1)} %reshape.114), calls=%async_computation | async-start | bytes 131072 | tf_op jit(solution)/shard_map/all_to_all | solution.py:137
  86.3 0.6 fusion.53
  93.0 0.4 copy.23
  93.5 5.8 %all_gather.3 = bf16[4,16,8,2,128]{4,2,3,1,0:T(8,128)(2,1)S(1)} all-gather(bf16[1,16,8,2,128]{4,2,3,1,0:T(8,128)(2,1)S(1)} %bitcast.45), channel_id=1, replica_groups=mesh['hour'=2,'stn'=4,'tchunk'=4] {'stn'}, dimensions={0}, use_global_device_ids=true | all-gather | bytes 327680 | tf_op jit(solution)/shard_map/all_gather | solution.py:139
  99.3 1.5 %copy.30 = bf16[2,16,8,2,128,1]{1,2,3,0,5,4:T(8,128)(2,1)S(1)} copy(bf16[2,16,8,2,128,1]{4,2,3,1,0,5:T(8,128)(2,1)S(1)} %maximum_bitcast_fusion.1) | data formatting | bytes 262144 | tf_op jit(solution)/shard_map/stack | solution.py:77
  100.8 1.1 copy.29
  101.9 3.3 %fusion.10 = f32[3,128,2,16,16]{3,4,2,0,1:T(8,128)} fusion(bf16[3,16,8,2,128,1]{1,2,3,5,0,4:T(8,128)(2,1)S(1)} %copy.29, bf16[2,16,8,2,128,1]{1,2,3,0,5,4:T(8,128)(2,1)S(1)} %copy.30), kind=kOutput, calls=%fused_computation.16 | convolution fusion | flops 6488064 | bytes 1114112 | tf_op jit(solution)/shard_map/oqsck,mrsck->mkoqr/dot_general | solution.py:80
  105.3 5.5 %copy.27 = f32[3,128,2,16,16]{1,4,3,2,0:T(8,128)S(1)} copy(f32[3,128,2,16,16]{3,4,2,0,1:T(8,128)} %fusion.10) | data formatting | bytes 1572864 | tf_op jit(solution)/shard_map/div | solution.py:141
  110.8 1.1 %copy.28 = f32[1,3,128,512]{3,2,1,0:T(8,128)} copy(f32[1,3,128,512]{2,3,1,0:T(8,128)S(1)} %bitcast.42) | data formatting | bytes 1572864 | tf_op jit(solution)/shard_map/div | solution.py:141
  (30 shorter events, 1.8 us)
Async XLA Ops:
  3.0 12.9 %copy-start = (f32[144,4096]{1,0:T(8,128)S(1)}, f32[144,4096]{1,0:T(8,128)}, u32[]{:S(2)}) copy-start(f32[144,4096]{1,0:T(8,128)} %param.3) | copy-start | bytes 7077892
  3.1 7.6 %collective-permute-start = (f32[144,10]{1,0:T(8,128)S(1)}, f32[144,10]{1,0:T(8,128)S(1)}, u32[]{:S(2)}, u32[]{:S(2)}) collective-permute-start(f32[144,10]{1,0:T(8,128)S(1)} %get-tuple-element.12), channel_id=1, source_target_pairs={{0,1},{1,2},{2,3},{4,5},{5,6},{6,7},{8,9},{9,10},{10,11},{12,13},{... | collective-permute-start | bytes 17288 | tf_op jit(solution)/shard_map/ppermute | solution.py:31
  8.1 6.2 %collective-permute-start.1 = (f32[144,10]{1,0:T(8,128)S(1)}, f32[144,10]{1,0:T(8,128)S(1)}, u32[]{:S(2)}, u32[]{:S(2)}) collective-permute-start(f32[144,10]{1,0:T(8,128)S(1)} %get-tuple-element.13), channel_id=1, source_target_pairs={{1,0},{2,1},{3,2},{5,4},{6,5},{7,6},{9,8},{10,9},{11,10},{13,12},{... | collective-permute-start | bytes 17288 | tf_op jit(solution)/shard_map/ppermute | solution.py:33
  15.8 3.7 %copy-start.1 = (f32[4096]{0:T(1024)S(1)}, f32[4096]{0:T(1024)}, u32[]{:S(2)}) copy-start(f32[4096]{0:T(1024)} %get-tuple-element.22) | copy-start | bytes 49156
  15.8 3.7 %copy-start.2 = (s32[512]{0:T(512)S(1)}, s32[512]{0:T(512)}, u32[]{:S(2)}) copy-start(s32[512]{0:T(512)} %iota_add_fusion) | copy-start | bytes 6148
  18.1 37.9 %collective-permute-start.2 = (bf16[144,2048]{1,0:T(8,128)(2,1)S(1)}, bf16[144,2048]{1,0:T(8,128)(2,1)S(1)}, u32[]{:S(2)}, u32[]{:S(2)}) collective-permute-start(bf16[144,2048]{1,0:T(8,128)(2,1)S(1)} %slice.183), channel_id=1, source_target_pairs={{1,0},{2,1},{3,2},{5,4},{6,5},{7,6},{9,8},{10,9},{11,10},{13,12},{... | collective-permute-start | bytes 1769480 | tf_op jit(solution)/shard_map/ppermute | solution.py:43
  77.4 0.7 copy-start.4
  77.4 8.9 %copy-start.3 = (s32[1,3]{1,0:T(1,128)S(1)}, s32[1,3]{1,0:T(1,128)}, u32[]{:S(2)}) copy-start(s32[1,3]{1,0:T(1,128)} %param.5) | copy-start | bytes 40
  80.4 12.3 %all-to-all-start = ((bf16[4,2,4096]{2,1,0:T(2,128)(2,1)}), bf16[4,2,4096]{2,1,0:T(2,128)(2,1)S(1)}, u32[]{:S(2)}, u32[]{:S(2)}) async-start(bf16[4,2,4096]{2,1,0:T(2,128)(2,1)} %reshape.114), calls=%async_computation | async-start | bytes 131072 | tf_op jit(solution)/shard_map/all_to_all | solution.py:137
where the time goes:
time: 112 us
  other arithmetic  48.4 us (43%)
  local copies, waits for them, and re-layouts  22.7 us (20%)
  starting transfers between devices  13.8 us (12%)
  matrix products  11.6 us (10%)
  between operations  5.95 us (5%)
  blocking collectives  5.79 us (5%)
  waiting for transfers between devices  3.69 us (3%)
    another operation x1, other arithmetic  36.3 us
    dot_general x1, matrix products, body(): spectra = jnp.dot(segments, dft_table(), preferred_element_type=jnp.float32)  6.69 us
    div x2, local copies, waits for them, and re-layouts, body(): return (stacked / count_segments)[None]  6.64 us
    all_to_all x1, starting transfers between devices, body(): lax.all_to_all(beam_sums, 'tchunk', split_axis=3, concat_axis=1, tiled=True)  5.97 us
    all_gather x1, blocking collectives, body(): lax.all_gather(spread[None], 'stn', axis=0, tiled=True)  5.79 us
    ppermute x1, starting transfers between devices, with_halo(): lax.ppermute(tail, axis, [(i, (i + 1) % count) for i in range(ends)])  5.06 us
    reshape x1, local copies, waits for them, and re-layouts, body(): jnp.concatenate([normalized, following], axis=1)  4.64 us
    ppermute x1, waiting for transfers between devices, with_halo(): lax.ppermute(head, axis, [((i + 1) % count, i) for i in range(ends)])  3.68 us
  transfers between devices with their start and end apart: 4, of which 1 were waited for; matrix products, arithmetic and copies ran while one was open for 34% of the time, Pallas kernels for 0%

commit v1 on v0

v1 whole, which is shorter than its diff:
```python
import functools
import math

import jax
import jax.numpy as jnp
import ml_dtypes
import numpy as np
from jax import lax
from jax.experimental import pallas as pl
from jax.experimental.pallas import tpu as pltpu
from jax.sharding import PartitionSpec as P

SEG_DEV = 2
SEGLEN = 4096
HOP = 2048
NBIN = 512
RB = 128
RAMH = 10
SMOOTH = 8
SUB = 16
MAXP = 3

EPS_MEAN = 1e-06
LEVEL = 0.05

BF16 = jnp.bfloat16
F32 = jnp.float32
VMEM = pl.BlockSpec(memory_space=pltpu.VMEM)
SMEM = pl.BlockSpec(memory_space=pltpu.SMEM)
MIB = 1 << 20


def dft_table():
    sample = np.arange(SEGLEN, dtype=np.int32)
    frequency = np.arange(1, NBIN + 1, dtype=np.int32)
    phases = sample[:, None] * frequency[None, :] % SEGLEN
    turn = np.arange(SEGLEN, dtype=np.float64) * (2.0 * math.pi / SEGLEN)
    taper = (0.5 - 0.5 * np.cos(turn))[:, None]
    matrix = np.concatenate([taper * np.cos(turn)[phases], -taper * np.sin(turn)[phases]], axis=1)
    return matrix.astype(np.float32).astype(ml_dtypes.bfloat16)


def smooth_tables():
    bin_index = np.arange(NBIN)
    nearby = np.abs(bin_index[:, None] - bin_index[None, :]) <= SMOOTH
    scale = 1.0 / np.sum(nearby, axis=0, keepdims=True)
    return nearby.astype(ml_dtypes.bfloat16), scale.astype(np.float32)


def neighbour_swap(first, second, axis):
    count = lax.axis_size(axis)
    out = []
    for block, start in ((first, 0), (second, 1)):
        pairs = [(i, i + 1) for i in range(start, count - 1, 2)]
        out.append(lax.ppermute(block, axis, pairs + [(j, i) for i, j in pairs]))
    return out


def swapped(block, axis, mask):
    return lax.ppermute(block, axis, [(i, i ^ mask) for i in range(lax.axis_size(axis))])


def call(kernel, out_shape, operands, specs=None, flops=0, limit=16, **more):
    moved = sum(math.prod(a.shape) * a.dtype.itemsize for a in list(operands) + jax.tree.leaves(out_shape))
    more.setdefault("out_specs", jax.tree.map(lambda _: VMEM, out_shape))
    return pl.pallas_call(
        kernel,
        out_shape=out_shape,
        in_specs=specs or [VMEM] * len(operands),
        compiler_params=pltpu.CompilerParams(vmem_limit_bytes=limit * MIB),
        cost_estimate=pl.CostEstimate(flops=flops, bytes_accessed=moved, transcendentals=0),
        **more,
    )(*operands)


def sums_kernel(steps, place, raw, sums, to_even, to_odd, held):
    step = pl.program_id(0)
    rows, samples = raw.shape
    lane = lax.broadcasted_iota(jnp.int32, (rows, RB), 1)
    total = jnp.zeros((rows, RB), F32)
    for b in range(samples // RB):
        here = jnp.sum(jnp.abs(raw[:, b * RB : (b + 1) * RB]), axis=1, keepdims=True)
        total = jnp.where(lane == b, here, total)
    held[pl.ds(step * rows, rows), :] = total

    @pl.when(step == steps - 1)
    def _():
        blocks = samples // RB
        whole = held[...]
        sums[...] = whole[:, :blocks]
        flipped = jnp.transpose(whole)
        head = flipped[: blocks // 2]
        tail = flipped[blocks // 2 : blocks]
        even = place[0] % 2 == 0
        to_even[...] = jnp.where(even, tail, head)
        to_odd[...] = jnp.where(even, head, tail)


def exact_dot(left, right, dims):
    return lax.dot_general(left, right, (dims, ((), ())), precision=lax.Precision.HIGHEST, preferred_element_type=F32)


def normalize_kernel(
    slabs, place, raw, sums, from_even, from_odd, table, normal, to_even, to_odd, keep_right, keep_left
):
    stations, blocks = sums.shape
    half_blocks = from_even.shape[0]
    even = place[0] % 2 == 0
    left = jnp.where(even, from_odd[...], from_even[...])
    right = jnp.where(even, from_even[...], from_odd[...])

    def band(rows, first):
        source = lax.broadcasted_iota(jnp.int32, (rows, blocks), 0) + first
        target = lax.broadcasted_iota(jnp.int32, (rows, blocks), 1)
        return ((source >= target - RAMH) & (source < target + RAMH)).astype(F32)

    window = exact_dot(sums[...], band(blocks, 0), ((1,), (0,)))
    window += exact_dot(left, band(half_blocks, -half_blocks), ((0,), (0,)))
    window += exact_dot(right, band(half_blocks, blocks), ((0,), (0,)))
    block = lax.broadcasted_iota(jnp.int32, (stations, blocks), 1) + place[0] * blocks
    counted = jnp.minimum(block + RAMH, slabs * blocks) - jnp.maximum(block - RAMH, 0)
    factor = 1.0 / (window / (RB * counted.astype(F32)) + EPS_MEAN)
    for b in range(blocks):
        here = pl.ds(b * RB, RB)
        normal[:, here] = (raw[:, here] * factor[:, b : b + 1]).astype(BF16)

    half = stations // 2

    def crossing(first, second):
        return jnp.dot(normal[:, first : first + HOP], table[second : second + HOP, :], preferred_element_type=F32)

    ahead = crossing(HOP, 0)
    keep_right[...] = ahead[:half]
    for_right = ahead[half:].astype(BF16)
    behind = crossing(0, HOP)
    keep_left[...] = behind[half:]
    for_left = behind[:half].astype(BF16)

    @pl.when(even)
    def _():
        to_even[...] = for_right
        to_odd[...] = for_left

    @pl.when(jnp.logical_not(even))
    def _():
        to_even[...] = for_left
        to_odd[...] = for_right


def whiten(spectra, nearby, scale):
    real_part = spectra[:, :NBIN]
    imag_part = spectra[:, NBIN:]
    powers = real_part * real_part + imag_part * imag_part
    high = powers.astype(BF16)
    low = (powers - high.astype(F32)).astype(BF16)
    smooth = jnp.dot(high, nearby, preferred_element_type=F32) + jnp.dot(low, nearby, preferred_element_type=F32)
    floor_level = jnp.sum(powers, axis=1, keepdims=True) * (1.0 / NBIN) + 1e-06
    inverse = lax.rsqrt(smooth * scale + LEVEL * floor_level)
    return (real_part * inverse).astype(BF16), (imag_part * inverse).astype(BF16)


def members(group, count):
    shape = (count, group.shape[1])
    return (lax.broadcasted_iota(jnp.int32, shape, 0) == group).astype(BF16)


def own_kernel(normal, table, group, nearby, scale, beams):
    spectra = jnp.dot(normal[...], table[...], preferred_element_type=F32)
    member = members(group[...], SUB)
    for part, white in enumerate(whiten(spectra, nearby[...], scale[...])):
        beams[part * SUB : (part + 1) * SUB, :] = jnp.dot(member, white, preferred_element_type=F32).astype(BF16)


def crossing_kernel(place, keep_right, keep_left, from_even, from_odd, own, group, nearby, scale, *out):
    half = keep_right.shape[0]
    held = out[-1]
    even = place[0] % 2 == 0
    got_even = from_even[...].astype(F32)
    got_odd = from_odd[...].astype(F32)
    ahead = keep_right[...] + jnp.where(even, got_even, got_odd)
    behind = keep_left[...] + jnp.where(even, got_odd, got_even)
    spectra = jnp.concatenate([ahead, behind], axis=0)
    station = lax.broadcasted_iota(jnp.int32, group.shape, 1)
    member = members(group[...] + jnp.where(station < half, 0, SUB), 2 * SUB)
    held[: 2 * SUB, :] = own[...]
    for part, white in enumerate(whiten(spectra, nearby[...], scale[...])):
        sums = jnp.dot(member, white, preferred_element_type=F32).astype(BF16)
        for side in range(2):
            row = (2 + 2 * side + part) * SUB
            held[row : row + SUB, :] = sums[side * SUB : (side + 1) * SUB]
    pieces = len(out) - 1
    if pieces > 1:
        width = NBIN // pieces
        for mask in range(pieces):
            start = pl.multiple_of((place[0] ^ mask) * width, width)
            out[mask][...] = held[:, pl.ds(start, width)]
    else:
        out[0][...] = held[...]


def cross_kernel(segments, place, partners, *refs):
    blocks, out, mine, others = refs[:-3], refs[-3], refs[-2], refs[-1]
    slot = pl.program_id(0)
    width = out.shape[1]
    lane = lax.broadcasted_iota(jnp.int32, (SUB, SUB * SUB), 1)
    row = lax.broadcasted_iota(jnp.int32, (SUB, SUB * SUB), 0)
    spread = (lane // SUB == row).astype(BF16)
    tiled = (lane % SUB == row).astype(BF16)
    count = (segments + 1) // 2

    def grown(piece, pattern):
        return lax.dot_general(piece, pattern, (((0,), (0,)), ((), ())), preferred_element_type=F32)

    def segment(block, s, part):
        source = block.at[s // 2]
        if s % 2 == 0:
            return source[part * SUB : (part + 1) * SUB, :]
        ahead = source[(2 + part) * SUB : (3 + part) * SUB, :].astype(F32)
        behind = block[s // 2 + 1, (4 + part) * SUB : (5 + part) * SUB, :].astype(F32)
        return (ahead + behind).astype(BF16)

    partner = partners[0, slot]

    @pl.when(slot == 0)
    def _():
        own = blocks[0]
        for s in range(segments):
            for part in range(2):
                mine[s, part] = grown(segment(own, s, part), spread)

    @pl.when(partner < 0)
    def _():
        out[...] = jnp.zeros_like(out)

    @pl.when(partner >= 0)
    def _():
        which = partner ^ place[1]
        for index in range(1, len(blocks)):
            @pl.when(which == index)
            def _(index=index):
                others[...] = blocks[index][...]
        real_sum = jnp.zeros((width, SUB * SUB), F32)
        imag_sum = jnp.zeros((width, SUB * SUB), F32)
        for s in range(segments):
            a, b = mine[s, 0], mine[s, 1]
            c, d = grown(segment(others, s, 0), tiled), grown(segment(others, s, 1), tiled)
            real_sum += a * c + b * d
            imag_sum += b * c - a * d
        out[0, :, : SUB * SUB] = real_sum * (1.0 / segments)
        out[0, :, SUB * SUB :] = imag_sum * (1.0 / segments)


def body(raw_data, station_group, partner_blocks):
    stations, samples = raw_data.shape
    slabs = lax.axis_size("tchunk")
    count_blocks = lax.axis_size("stn")
    me = lax.axis_index("tchunk")
    place = jnp.stack([me, lax.axis_index("stn")]).astype(jnp.int32)
    blocks = samples // RB
    half = stations // 2
    table = jnp.asarray(dft_table())
    nearby, scale = (jnp.asarray(t) for t in smooth_tables())
    group = station_group[None, :]
    shape = jax.ShapeDtypeStruct

    steps = 3
    halo = shape((blocks // 2, stations), F32)
    sums, even, odd = call(
        functools.partial(sums_kernel, steps),
        (shape((stations, blocks), F32), halo, halo),
        (place, raw_data),
        specs=[SMEM, pl.BlockSpec((stations // steps, samples), lambda i: (i, 0))],
        out_specs=[pl.BlockSpec((stations, blocks), lambda i: (0, 0))]
        + [pl.BlockSpec(halo.shape, lambda i: (0, 0))] * 2,
        grid=(steps,),
        scratch_shapes=[pltpu.VMEM((stations, RB), F32)],
        flops=2 * stations * samples,
    )
    even, odd = neighbour_swap(even, odd, "tchunk")
    sent = shape((half, 2 * NBIN), BF16)
    kept = shape((half, 2 * NBIN), F32)
    normal, even, odd, keep_right, keep_left = call(
        functools.partial(normalize_kernel, slabs),
        (shape((stations, samples), BF16), sent, sent, kept, kept),
        (place, raw_data, sums, even, odd, table),
        specs=[SMEM] + [VMEM] * 5,
        flops=4 * stations * samples * NBIN,
        limit=32,
    )
    even, odd = neighbour_swap(even, odd, "tchunk")
    own = call(
        own_kernel,
        shape((2 * SUB, NBIN), BF16),
        (normal, table, group, nearby, scale),
        flops=4 * stations * samples * NBIN,
        limit=32,
    )
    direct = slabs <= 8 and slabs & (slabs - 1) == 0 and NBIN // slabs % 128 == 0
    width = NBIN // slabs
    rows = 6 * SUB
    pieces = call(
        crossing_kernel,
        tuple([shape((rows, width), BF16)] * slabs) if direct else (shape((rows, NBIN), BF16),),
        (place, keep_right, keep_left, even, odd, own, group, nearby, scale),
        specs=[SMEM] + [VMEM] * 8,
        scratch_shapes=[pltpu.VMEM((rows, NBIN), BF16)],
        flops=8 * stations * NBIN * NBIN,
        limit=32,
    )
    if direct:
        received = [pieces[0]] + [swapped(pieces[m], "tchunk", m) for m in range(1, slabs)]
        order = jnp.arange(slabs) ^ me
        mine = jnp.stack(received, 0)[order]
    else:
        mine = jnp.moveaxis(pieces[0].reshape(rows, slabs, width), 1, 0)
        mine = lax.all_to_all(mine, "tchunk", split_axis=0, concat_axis=0, tiled=True)
    segments = SEG_DEV * slabs - 1
    if count_blocks <= 4 and count_blocks & (count_blocks - 1) == 0:
        others = [mine] + [swapped(mine, "stn", m) for m in range(1, count_blocks)]
    else:
        gathered = lax.all_gather(mine, "stn", axis=0)
        others = [lax.dynamic_index_in_dim(gathered, place[1] ^ m, 0, keepdims=False) for m in range(count_blocks)]
    out = call(
        functools.partial(cross_kernel, segments),
        shape((MAXP, width, 2 * SUB * SUB), F32),
        (place, partner_blocks, *others),
        specs=[SMEM, SMEM] + [VMEM] * count_blocks,
        out_specs=pl.BlockSpec((1, width, 2 * SUB * SUB), lambda i: (i, 0, 0)),
        grid=(MAXP,),
        scratch_shapes=[pltpu.VMEM((segments, 2, width, SUB * SUB), F32), pltpu.VMEM(mine.shape, BF16)],
        flops=MAXP * segments * width * SUB * SUB * 8,
        limit=32,
    )
    return out[None]


def solution(mesh):
    placed = (P("stn", ("hour", "tchunk")), P("stn"), P("stn", None))
    return jax.shard_map(
        body,
        mesh=mesh,
        in_specs=placed,
        out_specs=P(("hour", "stn"), None, "tchunk", None),
        check_vma=False,
    )
```

time: 112 us -> 45.9 us (0.41)
  other arithmetic: 48.4 us -> 0.1 us
  local copies, waits for them, and re-layouts: 22.7 us -> 5.64 us
  matrix products: 11.6 us -> 0 us
  Pallas kernels: 0 us -> 10.4 us
  waiting for transfers between devices: 3.69 us -> 10.8 us
  between operations: 5.95 us -> 0.13 us
  blocking collectives: 5.79 us -> 0 us
  starting transfers between devices: 13.8 us -> 18.3 us
    another operation x4 -> x2, other arithmetic: 36.4 us -> 0.09 us  [the longest x1 0.07 us: body(): place = jnp.stack([me, lax.axis_index('stn')]).astype(jnp.int32)]
    dot_general x4 -> x0, matrix products: 11.6 us -> none  [the longest x1 6.69 us: body(): spectra = jnp.dot(segments, dft_table(), preferred_element_type=jnp.float32)]
    ppermute x3 -> x10, starting transfers between devices: 7.83 us -> 18.3 us  [the longest x4 9.52 us: neighbour_swap(): out.append(lax.ppermute(block, axis, pairs + [(j, i) for i, j in pairs]))]
    pallas_call x0 -> x5, Pallas kernels: none -> 10.4 us  [call(): pl.pallas_call(kernel, out_shape=out_shape, in_specs=specs or [VMEM] * le...]
    reshape x4 -> x0, local copies, waits for them, and re-layouts: 7.49 us -> none  [the longest x1 4.64 us: body(): jnp.concatenate([normalized, following], axis=1)]
    div x3 -> x0, local copies, waits for them, and re-layouts: 7.31 us -> none  [the longest x2 6.64 us: body(): return (stacked / count_segments)[None]]
    ppermute x3 -> x10, waiting for transfers between devices: 3.69 us -> 10.8 us  [the longest x6 9.23 us: swapped(): lax.ppermute(block, axis, [(i, i ^ mask) for i in range(lax.axis_size(axi...]
    all_to_all x1 -> x0, starting transfers between devices: 5.97 us -> none  [body(): lax.all_to_all(beam_sums, 'tchunk', split_axis=3, concat_axis=1, tiled=True)]
  transfers between devices with their start and end apart: 4 -> 10, of which waited for: 1 -> 6; matrix products, arithmetic and copies ran while one was open for 34% -> 0% of each run, Pallas kernels for 0% -> 4%
where the time goes in v1:
time: 45.9 us; the launch traced here: 45.4 us
  starting transfers between devices  18.3 us (40%)
  waiting for transfers between devices  10.8 us (24%)
  Pallas kernels  10.4 us (23%)
  local copies, waits for them, and re-layouts  5.64 us (12%)
    pallas_call x5, Pallas kernels, call(): pl.pallas_call(kernel, out_shape=out_shape, in_specs=specs or [VMEM] * le...  10.4 us
    ppermute x4, starting transfers between devices, neighbour_swap(): out.append(lax.ppermute(block, axis, pairs + [(j, i) for i, j in pairs]))  9.52 us
    ppermute x6, waiting for transfers between devices, swapped(): lax.ppermute(block, axis, [(i, i ^ mask) for i in range(lax.axis_size(axi...  9.23 us
    ppermute x6, starting transfers between devices, swapped(): lax.ppermute(block, axis, [(i, i ^ mask) for i in range(lax.axis_size(axi...  8.82 us
    unnamed x16, local copies, waits for them, and re-layouts  5.07 us
    ppermute x4, waiting for transfers between devices, neighbour_swap(): out.append(lax.ppermute(block, axis, pairs + [(j, i) for i, j in pairs]))  1.61 us
  transfers between devices with their start and end apart: 10, of which 6 were waited for; matrix products, arithmetic and copies ran while one was open for 0% of the time, Pallas kernels for 4%

profile of v1, /device:TPU:0, one launch (start us, length us, event | category | flops | bytes accessed | tf_op | source)
XLA Modules:
  0.0 45.4 jit_solution(4476337700941308750)
XLA Ops:
  0.0 0.1 pad_add_fusion.place
  0.1 1.7 %copy-done.2 = f32[144,4096]{1,0:T(8,128)S(1)} copy-done((f32[144,4096]{1,0:T(8,128)S(1)}, f32[144,4096]{1,0:T(8,128)}, u32[]{:S(2)}) %copy-start.2) | copy-done | bytes 2359320
  1.7 1.5 %shard_map.64 = (f32[144,32]{1,0:T(8,128)S(1)}, f32[16,144]{1,0:T(8,128)S(1)}, f32[16,144]{1,0:T(8,128)S(1)}) custom-call(s32[2]{0:T(128)S(1)} %pad_add_fusion.place, f32[144,4096]{1,0:T(8,128)S(1)} %copy-done.2), custom_call_target="tpu_custom_call" | custom-call | flops 1179648 | bytes 2396168 | tf_op jit(solution)/shard_map/pallas_call | solution.py:66
  3.2 3.1 %collective-permute-start = (f32[16,144]{1,0:T(8,128)S(1)}, f32[16,144]{1,0:T(8,128)S(1)}, u32[]{:S(2)}, u32[]{:S(2)}) collective-permute-start(f32[16,144]{1,0:T(8,128)S(1)} %get-tuple-element.18), channel_id=1, source_target_pairs={{0,1},{2,3},{1,0},{3,2},{4,5},{6,7},{5,4},{7,6},{8,9},{10,11},{9,8... | collective-permute-start | bytes 27656 | tf_op jit(solution)/shard_map/ppermute | solution.py:55
  6.3 0.7 %collective-permute-start.1 = (f32[16,144]{1,0:T(8,128)S(1)}, f32[16,144]{1,0:T(8,128)S(1)}, u32[]{:S(2)}, u32[]{:S(2)}) collective-permute-start(f32[16,144]{1,0:T(8,128)S(1)} %get-tuple-element.19), channel_id=1, source_target_pairs={{1,2},{2,1},{5,6},{6,5},{9,10},{10,9},{13,14},{14,13},{17,18},{18,... | collective-permute-start | bytes 27656 | tf_op jit(solution)/shard_map/ppermute | solution.py:55
  7.0 1.1 %collective-permute-done.from_even = f32[16,144]{1,0:T(8,128)S(1)} collective-permute-done((f32[16,144]{1,0:T(8,128)S(1)}, f32[16,144]{1,0:T(8,128)S(1)}, u32[]{:S(2)}, u32[]{:S(2)}) %collective-permute-start) | collective-permute-done | bytes 9248 | tf_op jit(solution)/shard_map/ppermute | solution.py:55
  8.0 0.0 collective-permute-done.1.from_odd
  8.0 0.0 copy-done.3
  8.0 3.4 %copy-done = bf16[4096,1024]{1,0:T(8,128)(2,1)S(1)} copy-done((bf16[4096,1024]{1,0:T(8,128)(2,1)S(1)}, bf16[4096,1024]{1,0:T(8,128)(2,1)}, u32[]{:S(2)}) %copy-start) | copy-done | bytes 8388632
  11.4 3.1 %shard_map.65 = (bf16[144,4096]{1,0:T(8,128)(2,1)S(1)}, bf16[72,1024]{1,0:T(8,128)(2,1)S(1)}, bf16[72,1024]{1,0:T(8,128)(2,1)S(1)}, f32[72,1024]{1,0:T(8,128)S(1)}, f32[72,1024]{1,0:T(8,128)S(1)}) custom-call(s32[2]{0:T(128)S(1)} %pad_add_fusion.place, f32[144,4096]{1,0:T(8,128)S(1)} %copy-done.3, f32[144,32]{1,0:T(8,128)S(1)} %get-tuple-element.17.sums, ...), custom_call_target="tpu_custom_call" | custom-call | flops 1207959552 | bytes 12849160 | tf_op jit(solution)/shard_map/pallas_call | solution.py:66
  14.5 5.1 %collective-permute-start.2 = (bf16[72,1024]{1,0:T(8,128)(2,1)S(1)}, bf16[72,1024]{1,0:T(8,128)(2,1)S(1)}, u32[]{:S(2)}, u32[]{:S(2)}) collective-permute-start(bf16[72,1024]{1,0:T(8,128)(2,1)S(1)} %get-tuple-element.22), channel_id=1, source_target_pairs={{0,1},{2,3},{1,0},{3,2},{4,5},{6,7},{5,4},{7,6},{8,9},{10,11},{9,8... | collective-permute-start | bytes 442376 | tf_op jit(solution)/shard_map/ppermute | solution.py:55
  19.6 0.7 %collective-permute-start.3 = (bf16[72,1024]{1,0:T(8,128)(2,1)S(1)}, bf16[72,1024]{1,0:T(8,128)(2,1)S(1)}, u32[]{:S(2)}, u32[]{:S(2)}) collective-permute-start(bf16[72,1024]{1,0:T(8,128)(2,1)S(1)} %get-tuple-element.23), channel_id=1, source_target_pairs={{1,2},{2,1},{5,6},{6,5},{9,10},{10,9},{13,14},{14,13},{17,18},{18,... | collective-permute-start | bytes 442376 | tf_op jit(solution)/shard_map/ppermute | solution.py:55
  20.3 0.0 copy-done.1
  20.3 0.0 copy-start.7
  20.3 1.8 %shard_map.66.own = bf16[32,512]{1,0:T(8,128)(2,1)S(1)} custom-call(bf16[144,4096]{1,0:T(8,128)(2,1)S(1)} %get-tuple-element.24.normal, bf16[4096,1024]{1,0:T(8,128)(2,1)S(1)} %copy-done.1, s32[1,144]{1,0:T(1,128)S(1)} %bitcast.11, bf16[512,512]{1,0:T(8,128)(2,1)S(1)} %copy-done.4, f32[1,512]{1,0:T(1,128)S(1)} %copy-done.5), custom_call_target="tpu_custom_call" | custom-call | flops 1207959552 | bytes 10127936 | tf_op jit(solution)/shard_map/pallas_call | solution.py:66
  22.2 0.5 %collective-permute-done.2.from_even = bf16[72,1024]{1,0:T(8,128)(2,1)S(1)} collective-permute-done((bf16[72,1024]{1,0:T(8,128)(2,1)S(1)}, bf16[72,1024]{1,0:T(8,128)(2,1)S(1)}, u32[]{:S(2)}, u32[]{:S(2)}) %collective-permute-start.2) | collective-permute-done | bytes 147488 | tf_op jit(solution)/shard_map/ppermute | solution.py:55
  22.7 0.0 collective-permute-done.3.from_odd
  22.7 1.1 %shard_map.67 = (bf16[96,128]{1,0:T(8,128)(2,1)S(1)}, bf16[96,128]{1,0:T(8,128)(2,1)S(1)}, bf16[96,128]{1,0:T(8,128)(2,1)S(1)}, bf16[96,128]{1,0:T(8,128)(2,1)S(1)}) custom-call(s32[2]{0:T(128)S(1)} %pad_add_fusion.place, f32[72,1024]{1,0:T(8,128)S(1)} %get-tuple-element.20.keep_right, f32[72,1024]{1,0:T(8,128)S(1)} %get-tuple-element.21.keep_left, ...), custom_call_target="tpu_custom_call" | custom-call | flops 301989888 | bytes 1542728 | tf_op jit(solution)/shard_map/pallas_call | solution.py:66
  23.9 4.0 %collective-permute-start.4 = (bf16[96,128]{1,0:T(8,128)(2,1)S(1)}, bf16[96,128]{1,0:T(8,128)(2,1)S(1)}, u32[]{:S(2)}, u32[]{:S(2)}) collective-permute-start(bf16[96,128]{1,0:T(8,128)(2,1)S(1)} %get-tuple-element.26), channel_id=1, source_target_pairs={{0,1},{1,0},{2,3},{3,2},{4,5},{5,4},{6,7},{7,6},{8,9},{9,8},{10,11... | collective-permute-start | bytes 73736 | tf_op jit(solution)/shard_map/ppermute | solution.py:60
  27.8 1.5 %collective-permute-start.5 = (bf16[96,128]{1,0:T(8,128)(2,1)S(1)}, bf16[96,128]{1,0:T(8,128)(2,1)S(1)}, u32[]{:S(2)}, u32[]{:S(2)}) collective-permute-start(bf16[96,128]{1,0:T(8,128)(2,1)S(1)} %get-tuple-element.27), channel_id=1, source_target_pairs={{0,2},{1,3},{2,0},{3,1},{4,6},{5,7},{6,4},{7,5},{8,10},{9,11},{10,... | collective-permute-start | bytes 73736 | tf_op jit(solution)/shard_map/ppermute | solution.py:60
  29.4 1.4 %collective-permute-start.6 = (bf16[96,128]{1,0:T(8,128)(2,1)S(1)}, bf16[96,128]{1,0:T(8,128)(2,1)S(1)}, u32[]{:S(2)}, u32[]{:S(2)}) collective-permute-start(bf16[96,128]{1,0:T(8,128)(2,1)S(1)} %get-tuple-element.28), channel_id=1, source_target_pairs={{0,3},{1,2},{2,1},{3,0},{4,7},{5,6},{6,5},{7,4},{8,11},{9,10},{10,... | collective-permute-start | bytes 73736 | tf_op jit(solution)/shard_map/ppermute | solution.py:60
  30.7 0.0 collective-permute-done.4
  30.8 1.8 %collective-permute-done.5 = bf16[96,128]{1,0:T(8,128)(2,1)S(1)} collective-permute-done((bf16[96,128]{1,0:T(8,128)(2,1)S(1)}, bf16[96,128]{1,0:T(8,128)(2,1)S(1)}, u32[]{:S(2)}, u32[]{:S(2)}) %collective-permute-start.5) | collective-permute-done | bytes 24608 | tf_op jit(solution)/shard_map/ppermute | solution.py:60
  32.6 2.4 %collective-permute-done.6 = bf16[96,128]{1,0:T(8,128)(2,1)S(1)} collective-permute-done((bf16[96,128]{1,0:T(8,128)(2,1)S(1)}, bf16[96,128]{1,0:T(8,128)(2,1)S(1)}, u32[]{:S(2)}, u32[]{:S(2)}) %collective-permute-start.6) | collective-permute-done | bytes 24608 | tf_op jit(solution)/shard_map/ppermute | solution.py:60
  35.0 0.6 %gather_fusion = bf16[4,96,128]{2,1,0:T(8,128)(2,1)S(1)} fusion(bf16[4,96,128]{2,1,0:T(8,128)(2,1)S(1)} %pad_maximum_fusion, s32[1024]{0:T(1024)S(1)} %pad_clamp_fusion), kind=kCustom, calls=%fused_computation | custom fusion | bytes 196624 | tf_op jit(solution)/shard_map/gather | solution.py:313
  35.6 0.1 collective-permute-start.7
  35.7 1.6 %collective-permute-start.8 = (bf16[4,96,128]{2,1,0:T(8,128)(2,1)S(1)}, bf16[4,96,128]{2,1,0:T(8,128)(2,1)S(1)}, u32[]{:S(2)}, u32[]{:S(2)}) collective-permute-start(bf16[4,96,128]{2,1,0:T(8,128)(2,1)S(1)} %gather_fusion), channel_id=1, source_target_pairs={{0,8},{4,12},{8,0},{12,4},{1,9},{5,13},{9,1},{13,5},{2,10},{6,14},... | collective-permute-start | bytes 294920 | tf_op jit(solution)/shard_map/ppermute | solution.py:60
  37.2 0.3 collective-permute-start.9
  37.5 0.0 collective-permute-done.7.refs_1_
  37.5 3.8 %collective-permute-done.8.refs_2_ = bf16[4,96,128]{2,1,0:T(8,128)(2,1)S(1)} collective-permute-done((bf16[4,96,128]{2,1,0:T(8,128)(2,1)S(1)}, bf16[4,96,128]{2,1,0:T(8,128)(2,1)S(1)}, u32[]{:S(2)}, u32[]{:S(2)}) %collective-permute-start.8) | collective-permute-done | bytes 98336 | tf_op jit(solution)/shard_map/ppermute | solution.py:60
  41.3 1.2 %collective-permute-done.9.refs_3_ = bf16[4,96,128]{2,1,0:T(8,128)(2,1)S(1)} collective-permute-done((bf16[4,96,128]{2,1,0:T(8,128)(2,1)S(1)}, bf16[4,96,128]{2,1,0:T(8,128)(2,1)S(1)}, u32[]{:S(2)}, u32[]{:S(2)}) %collective-permute-start.9) | collective-permute-done | bytes 98336 | tf_op jit(solution)/shard_map/ppermute | solution.py:60
  42.5 2.9 %shard_map.68 = f32[3,128,512]{2,1,0:T(8,128)} custom-call(s32[2]{0:T(128)S(1)} %pad_add_fusion.place, s32[1,3]{1,0:T(1,128)S(1)} %copy-done.7, bf16[4,96,128]{2,1,0:T(8,128)(2,1)S(1)} %gather_fusion, bf16[4,96,128]{2,1,0:T(8,128)(2,1)S(1)} %collective-permute-done.7.refs_1_, bf16[4,96,128]{2,1,0:T(8,128)(2,1)S(1)} %collective-permute-done.8.refs_2_, ...), custom_call_target="tpu_custom_call" | custom-call | flops 5505024 | bytes 1179668 | tf_op jit(solution)/shard_map/pallas_call | solution.py:66
  (14 shorter events, 0.0 us)
Async XLA Ops:
  0.1 1.7 %copy-start.2 = (f32[144,4096]{1,0:T(8,128)S(1)}, f32[144,4096]{1,0:T(8,128)}, u32[]{:S(2)}) copy-start(f32[144,4096]{1,0:T(8,128)} %raw.3) | copy-start | bytes 7077892
  1.7 6.3 %copy-start.3 = (f32[144,4096]{1,0:T(8,128)S(1)}, f32[144,4096]{1,0:T(8,128)}, u32[]{:S(2)}) copy-start(f32[144,4096]{1,0:T(8,128)} %raw.3) | copy-start | bytes 7077892
  3.2 4.8 %collective-permute-start = (f32[16,144]{1,0:T(8,128)S(1)}, f32[16,144]{1,0:T(8,128)S(1)}, u32[]{:S(2)}, u32[]{:S(2)}) collective-permute-start(f32[16,144]{1,0:T(8,128)S(1)} %get-tuple-element.18), channel_id=1, source_target_pairs={{0,1},{2,3},{1,0},{3,2},{4,5},{6,7},{5,4},{7,6},{8,9},{10,11},{9,8... | collective-permute-start | bytes 27656 | tf_op jit(solution)/shard_map/ppermute | solution.py:55
  6.3 1.7 %collective-permute-start.1 = (f32[16,144]{1,0:T(8,128)S(1)}, f32[16,144]{1,0:T(8,128)S(1)}, u32[]{:S(2)}, u32[]{:S(2)}) collective-permute-start(f32[16,144]{1,0:T(8,128)S(1)} %get-tuple-element.19), channel_id=1, source_target_pairs={{1,2},{2,1},{5,6},{6,5},{9,10},{10,9},{13,14},{14,13},{17,18},{18,... | collective-permute-start | bytes 27656 | tf_op jit(solution)/shard_map/ppermute | solution.py:55
  8.0 3.4 %copy-start = (bf16[4096,1024]{1,0:T(8,128)(2,1)S(1)}, bf16[4096,1024]{1,0:T(8,128)(2,1)}, u32[]{:S(2)}) copy-start(bf16[4096,1024]{1,0:T(8,128)(2,1)} %constant.17.clone.table) | copy-start | bytes 25165828
  11.4 8.9 %copy-start.1 = (bf16[4096,1024]{1,0:T(8,128)(2,1)S(1)}, bf16[4096,1024]{1,0:T(8,128)(2,1)}, u32[]{:S(2)}) copy-start(bf16[4096,1024]{1,0:T(8,128)(2,1)} %constant.17.clone.table) | copy-start | bytes 25165828
  11.4 8.9 %copy-start.4 = (bf16[512,512]{1,0:T(8,128)(2,1)S(1)}, bf16[512,512]{1,0:T(8,128)(2,1)}, u32[]{:S(2)}) copy-start(bf16[512,512]{1,0:T(8,128)(2,1)} %constant.18.clone.nearby) | copy-start | bytes 1572868
  11.4 8.9 %copy-start.5 = (f32[1,512]{1,0:T(1,128)S(1)}, f32[1,512]{1,0:T(1,128)}, u32[]{:S(2)}) copy-start(f32[1,512]{1,0:T(1,128)} %constant.19.clone.scale) | copy-start | bytes 6148
  11.4 8.9 %copy-start.6 = (s32[144]{0:T(256)S(1)}, s32[144]{0:T(256)}, u32[]{:S(2)}) copy-start(s32[144]{0:T(256)} %param.7) | copy-start | bytes 1732
  14.5 8.2 %collective-permute-start.2 = (bf16[72,1024]{1,0:T(8,128)(2,1)S(1)}, bf16[72,1024]{1,0:T(8,128)(2,1)S(1)}, u32[]{:S(2)}, u32[]{:S(2)}) collective-permute-start(bf16[72,1024]{1,0:T(8,128)(2,1)S(1)} %get-tuple-element.22), channel_id=1, source_target_pairs={{0,1},{2,3},{1,0},{3,2},{4,5},{6,7},{5,4},{7,6},{8,9},{10,11},{9,8... | collective-permute-start | bytes 442376 | tf_op jit(solution)/shard_map/ppermute | solution.py:55
  19.6 3.1 %collective-permute-start.3 = (bf16[72,1024]{1,0:T(8,128)(2,1)S(1)}, bf16[72,1024]{1,0:T(8,128)(2,1)S(1)}, u32[]{:S(2)}, u32[]{:S(2)}) collective-permute-start(bf16[72,1024]{1,0:T(8,128)(2,1)S(1)} %get-tuple-element.23), channel_id=1, source_target_pairs={{1,2},{2,1},{5,6},{6,5},{9,10},{10,9},{13,14},{14,13},{17,18},{18,... | collective-permute-start | bytes 442376 | tf_op jit(solution)/shard_map/ppermute | solution.py:55
  20.3 22.2 %copy-start.7 = (s32[1,3]{1,0:T(1,128)S(1)}, s32[1,3]{1,0:T(1,128)}, u32[]{:S(2)}) copy-start(s32[1,3]{1,0:T(1,128)} %partners.1) | copy-start | bytes 40
  23.9 6.9 %collective-permute-start.4 = (bf16[96,128]{1,0:T(8,128)(2,1)S(1)}, bf16[96,128]{1,0:T(8,128)(2,1)S(1)}, u32[]{:S(2)}, u32[]{:S(2)}) collective-permute-start(bf16[96,128]{1,0:T(8,128)(2,1)S(1)} %get-tuple-element.26), channel_id=1, source_target_pairs={{0,1},{1,0},{2,3},{3,2},{4,5},{5,4},{6,7},{7,6},{8,9},{9,8},{10,11... | collective-permute-start | bytes 73736 | tf_op jit(solution)/shard_map/ppermute | solution.py:60
  27.8 4.7 %collective-permute-start.5 = (bf16[96,128]{1,0:T(8,128)(2,1)S(1)}, bf16[96,128]{1,0:T(8,128)(2,1)S(1)}, u32[]{:S(2)}, u32[]{:S(2)}) collective-permute-start(bf16[96,128]{1,0:T(8,128)(2,1)S(1)} %get-tuple-element.27), channel_id=1, source_target_pairs={{0,2},{1,3},{2,0},{3,1},{4,6},{5,7},{6,4},{7,5},{8,10},{9,11},{10,... | collective-permute-start | bytes 73736 | tf_op jit(solution)/shard_map/ppermute | solution.py:60
  29.4 5.6 %collective-permute-start.6 = (bf16[96,128]{1,0:T(8,128)(2,1)S(1)}, bf16[96,128]{1,0:T(8,128)(2,1)S(1)}, u32[]{:S(2)}, u32[]{:S(2)}) collective-permute-start(bf16[96,128]{1,0:T(8,128)(2,1)S(1)} %get-tuple-element.28), channel_id=1, source_target_pairs={{0,3},{1,2},{2,1},{3,0},{4,7},{5,6},{6,5},{7,4},{8,11},{9,10},{10,... | collective-permute-start | bytes 73736 | tf_op jit(solution)/shard_map/ppermute | solution.py:60
  35.6 1.9 %collective-permute-start.7 = (bf16[4,96,128]{2,1,0:T(8,128)(2,1)S(1)}, bf16[4,96,128]{2,1,0:T(8,128)(2,1)S(1)}, u32[]{:S(2)}, u32[]{:S(2)}) collective-permute-start(bf16[4,96,128]{2,1,0:T(8,128)(2,1)S(1)} %gather_fusion), channel_id=1, source_target_pairs={{0,4},{4,0},{8,12},{12,8},{1,5},{5,1},{9,13},{13,9},{2,6},{6,2},{1... | collective-permute-start | bytes 294920 | tf_op jit(solution)/shard_map/ppermute | solution.py:60
  35.7 5.7 %collective-permute-start.8 = (bf16[4,96,128]{2,1,0:T(8,128)(2,1)S(1)}, bf16[4,96,128]{2,1,0:T(8,128)(2,1)S(1)}, u32[]{:S(2)}, u32[]{:S(2)}) collective-permute-start(bf16[4,96,128]{2,1,0:T(8,128)(2,1)S(1)} %gather_fusion), channel_id=1, source_target_pairs={{0,8},{4,12},{8,0},{12,4},{1,9},{5,13},{9,1},{13,5},{2,10},{6,14},... | collective-permute-start | bytes 294920 | tf_op jit(solution)/shard_map/ppermute | solution.py:60
  37.2 5.3 %collective-permute-start.9 = (bf16[4,96,128]{2,1,0:T(8,128)(2,1)S(1)}, bf16[4,96,128]{2,1,0:T(8,128)(2,1)S(1)}, u32[]{:S(2)}, u32[]{:S(2)}) collective-permute-start(bf16[4,96,128]{2,1,0:T(8,128)(2,1)S(1)} %gather_fusion), channel_id=1, source_target_pairs={{0,12},{4,8},{8,4},{12,0},{1,13},{5,9},{9,5},{13,1},{2,14},{6,10},... | collective-permute-start | bytes 294920 | tf_op jit(solution)/shard_map/ppermute | solution.py:60

commit v2 on v1

v2 whole, which is shorter than its diff:
```python
import functools
import math

import jax
import jax.numpy as jnp
import ml_dtypes
import numpy as np
from jax import lax
from jax.experimental import pallas as pl
from jax.experimental.pallas import tpu as pltpu
from jax.sharding import PartitionSpec as P

SEG_DEV = 2
SEGLEN = 4096
HOP = 2048
NBIN = 512
RB = 128
RAMH = 10
SMOOTH = 8
SUB = 16
MAXP = 3

EPS_MEAN = 1e-06
LEVEL = 0.05

BF16 = jnp.bfloat16
F32 = jnp.float32
VMEM = pl.BlockSpec(memory_space=pltpu.VMEM)
HBM = pl.BlockSpec(memory_space=pltpu.HBM)
SMEM = pl.BlockSpec(memory_space=pltpu.SMEM)
MIB = 1 << 20


def dft_tables():
    sample = np.arange(HOP, dtype=np.int32)
    frequency = np.arange(1, NBIN + 1, dtype=np.int32)
    turn = np.arange(SEGLEN, dtype=np.float64) * (2.0 * math.pi / SEGLEN)
    phases = sample[:, None] * frequency[None, :] % SEGLEN
    matrix = np.concatenate([np.cos(turn)[phases], -np.sin(turn)[phases]], axis=1)
    taper = (0.5 - 0.5 * np.cos(turn)).reshape(2, HOP)
    sign = np.concatenate([(-1.0) ** frequency] * 2)[None, :]
    matrix = matrix.astype(np.float32).astype(ml_dtypes.bfloat16)
    return matrix, taper.astype(np.float32), sign.astype(np.float32)


def smooth_tables():
    bin_index = np.arange(NBIN)
    nearby = np.abs(bin_index[:, None] - bin_index[None, :]) <= SMOOTH
    scale = 1.0 / np.sum(nearby, axis=0, keepdims=True)
    return nearby.astype(ml_dtypes.bfloat16), scale.astype(np.float32)


def neighbour_swap(first, second):
    blocks, slabs = lax.axis_size("stn"), lax.axis_size("tchunk")
    inner = [(i, i ^ 1) for i in range(slabs - slabs % 2)]
    outer = [(i, i + 1) for i in range(1, slabs - 1, 2)]
    outer += [(j, i) for i, j in outer]
    pairs = [[(b * slabs + i, b * slabs + j) for b in range(blocks) for i, j in part] for part in (inner, outer)]
    if blocks % 2 == 0 and slabs % 2 == 0:
        pairs[1] += [(b * slabs + i, (b ^ 1) * slabs + i) for b in range(blocks) for i in (0, slabs - 1)]
    return [lax.ppermute(block, ("stn", "tchunk"), part) for block, part in zip((first, second), pairs)]


def swapped(block, axis, mask):
    return lax.ppermute(block, axis, [(i, i ^ mask) for i in range(lax.axis_size(axis))])


def call(kernel, out_shape, operands, specs=None, flops=0, limit=16, **more):
    moved = sum(math.prod(a.shape) * a.dtype.itemsize for a in list(operands) + jax.tree.leaves(out_shape))
    more.setdefault("out_specs", jax.tree.map(lambda _: VMEM, out_shape))
    return pl.pallas_call(
        kernel,
        out_shape=out_shape,
        in_specs=specs or [VMEM] * len(operands),
        compiler_params=pltpu.CompilerParams(vmem_limit_bytes=limit * MIB),
        cost_estimate=pl.CostEstimate(flops=flops, bytes_accessed=moved, transcendentals=0),
        **more,
    )(*operands)


def sums_kernel(place, source, raw, sums, to_even, to_odd, held, arrived):
    chunks = arrived.shape[0]
    stations, samples = raw.shape
    rows = stations // chunks
    blocks = samples // RB
    copies = []
    for step in range(chunks):
        here = pl.ds(step * rows, rows)
        copies.append(pltpu.make_async_copy(source.at[here], raw.at[here], arrived.at[step]))
        copies[-1].start()
    lane = lax.broadcasted_iota(jnp.int32, (rows, RB), 1)
    for step in range(chunks):
        copies[step].wait()
        here = pl.ds(step * rows, rows)
        total = jnp.zeros((rows, RB), F32)
        for b in range(blocks):
            amount = jnp.sum(jnp.abs(raw[here, b * RB : (b + 1) * RB]), axis=1, keepdims=True)
            total = jnp.where(lane == b, amount, total)
        held[here, :] = total
    whole = held[...]
    sums[...] = whole[:, :blocks]
    flipped = jnp.transpose(whole)
    head = flipped[: blocks // 2]
    tail = flipped[blocks // 2 : blocks]
    even = place[0] % 2 == 0
    to_even[...] = jnp.where(even, tail, head)
    to_odd[...] = jnp.where(even, head, tail)


def exact_dot(left, right, dims):
    return lax.dot_general(left, right, (dims, ((), ())), precision=lax.Precision.HIGHEST, preferred_element_type=F32)


def band(rows, blocks, first):
    source = lax.broadcasted_iota(jnp.int32, (rows, blocks), 0) + first
    target = lax.broadcasted_iota(jnp.int32, (rows, blocks), 1)
    return ((source >= target - RAMH) & (source < target + RAMH)).astype(F32)


def scale_blocks(raw, factor, taper, some, normal, windowed):
    for place, b in enumerate(some):
        here = pl.ds(place * RB, RB)
        scaled = (raw[:, b * RB : (b + 1) * RB] * factor[:, b : b + 1]).astype(BF16)
        normal[:, here] = scaled
        hop, inside = divmod(b * RB, HOP)
        weight = taper[1 - hop : 2 - hop, inside : inside + RB]
        windowed[:, here] = (scaled.astype(F32) * weight).astype(BF16)


def middle_kernel(raw, sums, source, taper, table, normal, ahead, behind, windowed, arrived):
    copy = pltpu.make_async_copy(source, table, arrived)
    copy.start()
    blocks = sums.shape[1]
    window = exact_dot(sums[...], band(blocks, blocks, 0), ((1,), (0,)))
    factor = 1.0 / (window * (1.0 / (2 * RAMH * RB)) + EPS_MEAN)
    scale_blocks(raw, factor, taper, range(RAMH, blocks - RAMH + 1), normal, windowed)
    copy.wait()
    split = HOP - RAMH * RB
    rest = windowed.shape[1] - split
    ahead[...] = jnp.dot(windowed[:, split:], table[:rest, :], preferred_element_type=F32)
    behind[...] = jnp.dot(windowed[:, :split], table[HOP - split :, :], preferred_element_type=F32)


def normalize_kernel(
    slabs, place, raw, sums, from_even, from_odd, table, taper, sign, ahead, behind,
    normal, to_even, to_odd, keep_right, keep_left, windowed,
):
    stations, blocks = sums.shape
    half_blocks = from_even.shape[0]
    even = place[0] % 2 == 0
    left = jnp.where(even, from_odd[...], from_even[...])
    right = jnp.where(even, from_even[...], from_odd[...])
    left = jnp.where(place[0] > 0, left, 0.0)
    right = jnp.where(place[0] < slabs - 1, right, 0.0)
    window = exact_dot(sums[...], band(blocks, blocks, 0), ((1,), (0,)))
    window += exact_dot(left, band(half_blocks, blocks, -half_blocks), ((0,), (0,)))
    window += exact_dot(right, band(half_blocks, blocks, blocks), ((0,), (0,)))
    block = lax.broadcasted_iota(jnp.int32, (stations, blocks), 1) + place[0] * blocks
    counted = jnp.minimum(block + RAMH, slabs * blocks) - jnp.maximum(block - RAMH, 0)
    factor = 1.0 / (window / (RB * counted.astype(F32)) + EPS_MEAN)
    outer = [*range(RAMH), *range(blocks - RAMH + 1, blocks)]
    scale_blocks(raw, factor, taper, outer, normal, windowed)

    half = stations // 2
    width = NBIN // 2
    split = RAMH * RB
    rest = windowed.shape[1] - split

    def keep(to_right, to_left):
        for n in range(table.shape[1] // width):
            here = pl.ds(n * width, width)
            right_part = jnp.dot(windowed[:, split:], table[HOP - rest :, here], preferred_element_type=F32)
            right_part += ahead[:, here]
            keep_right[:, here] = right_part[:half]
            to_right[:, here] = right_part[half:].astype(BF16)
            left_part = jnp.dot(windowed[:, :split], table[:split, here], preferred_element_type=F32)
            left_part = (left_part + behind[:, here]) * sign[:, here]
            keep_left[:, here] = left_part[half:]
            to_left[:, here] = left_part[:half].astype(BF16)

    @pl.when(even)
    def _():
        keep(to_even, to_odd)

    @pl.when(jnp.logical_not(even))
    def _():
        keep(to_odd, to_even)


def whiten(spectra, nearby, scale):
    real_part = spectra[:, :NBIN]
    imag_part = spectra[:, NBIN:]
    powers = real_part * real_part + imag_part * imag_part
    high = powers.astype(BF16)
    low = (powers - high.astype(F32)).astype(BF16)
    smooth = jnp.dot(high, nearby, preferred_element_type=F32) + jnp.dot(low, nearby, preferred_element_type=F32)
    floor_level = jnp.sum(powers, axis=1, keepdims=True) * (1.0 / NBIN) + 1e-06
    inverse = lax.rsqrt(smooth * scale + LEVEL * floor_level)
    return (real_part * inverse).astype(BF16), (imag_part * inverse).astype(BF16)


def members(group, count):
    shape = (count, group.shape[1])
    return (lax.broadcasted_iota(jnp.int32, shape, 0) == group).astype(BF16)


def own_kernel(outer, middle, table, taper, sign, group, nearby, scale, beams, windowed):
    stations = outer.shape[0]
    first = RAMH * RB
    last = first + middle.shape[1]
    parts = ((outer, 0, 0, first), (middle, 0, first, HOP), (middle, HOP - first, HOP, last), (outer, first, last, 2 * HOP))
    for source, start, low, high in parts:
        hop, inside = divmod(low, HOP)
        here = source[:, start : start + high - low].astype(F32) * taper[hop : hop + 1, inside : inside + high - low]
        windowed[hop * stations : (hop + 1) * stations, inside : inside + high - low] = here.astype(BF16)
    both = jnp.dot(windowed[...], table[...], preferred_element_type=F32)
    spectra = both[:stations] + both[stations:] * sign[...]
    member = members(group[...], SUB)
    for part, white in enumerate(whiten(spectra, nearby[...], scale[...])):
        beams[part * SUB : (part + 1) * SUB, :] = jnp.dot(member, white, preferred_element_type=F32).astype(BF16)


def crossing_kernel(place, keep_right, keep_left, from_even, from_odd, own, group, nearby, scale, *out):
    half = keep_right.shape[0]
    held = out[-1]
    even = place[0] % 2 == 0
    got_even = from_even[...].astype(F32)
    got_odd = from_odd[...].astype(F32)
    ahead = keep_right[...] + jnp.where(even, got_even, got_odd)
    behind = keep_left[...] + jnp.where(even, got_odd, got_even)
    spectra = jnp.concatenate([ahead, behind], axis=0)
    station = lax.broadcasted_iota(jnp.int32, group.shape, 1)
    member = members(group[...] + jnp.where(station < half, 0, SUB), 2 * SUB)
    held[: 2 * SUB, :] = own[...]
    for part, white in enumerate(whiten(spectra, nearby[...], scale[...])):
        sums = jnp.dot(member, white, preferred_element_type=F32).astype(BF16)
        for side in range(2):
            row = (2 + 2 * side + part) * SUB
            held[row : row + SUB, :] = sums[side * SUB : (side + 1) * SUB]
    pieces = len(out) - 1
    if pieces > 1:
        width = NBIN // pieces
        for mask in range(pieces):
            start = pl.multiple_of((place[0] ^ mask) * width, width)
            out[mask][...] = held[:, pl.ds(start, width)]
    else:
        out[0][...] = held[...]


def cross_kernel(segments, slabs, place, partners, *refs):
    blocks, (out, mine, others, held) = refs[:-4], refs[-4:]
    slot = pl.program_id(0)
    width = out.shape[1]
    partner = partners[0, slot]

    def pick(target, block):
        for m in range(slabs):
            held[place[0] ^ m] = block[m * 6 * SUB : (m + 1) * 6 * SUB, :]
        for s in range(segments):
            source = held.at[s // 2]
            for part in range(2):
                if s % 2 == 0:
                    target[s, part] = source[part * SUB : (part + 1) * SUB, :].astype(F32)
                else:
                    ahead = source[(2 + part) * SUB : (3 + part) * SUB, :].astype(F32)
                    behind = held[s // 2 + 1, (4 + part) * SUB : (5 + part) * SUB, :].astype(F32)
                    target[s, part] = (ahead + behind).astype(BF16).astype(F32)

    @pl.when(slot == 0)
    def _():
        pick(mine, blocks[0])

    @pl.when(partner < 0)
    def _():
        out[...] = jnp.zeros_like(out)

    @pl.when(partner >= 0)
    def _():
        which = partner ^ place[1]
        for index in range(1, len(blocks)):
            @pl.when(which == index)
            def _(index=index):
                pick(others, blocks[index])
        real, imag = [], []
        for q in range(SUB):
            real_sum = jnp.zeros((SUB, width), F32)
            imag_sum = jnp.zeros((SUB, width), F32)
            for s in range(segments):
                a, b = mine[s, 0, q : q + 1, :], mine[s, 1, q : q + 1, :]
                c, d = others[s, 0], others[s, 1]
                real_sum += a * c + b * d
                imag_sum += b * c - a * d
            real.append(real_sum * (1.0 / segments))
            imag.append(imag_sum * (1.0 / segments))
        half = SUB * SUB
        out[0, :, :half] = jnp.transpose(jnp.concatenate(real, axis=0))
        out[0, :, half:] = jnp.transpose(jnp.concatenate(imag, axis=0))


def body(raw_data, station_group, partner_blocks):
    stations, samples = raw_data.shape
    slabs = lax.axis_size("tchunk")
    count_blocks = lax.axis_size("stn")
    me = lax.axis_index("tchunk")
    place = jnp.stack([me, lax.axis_index("stn")]).astype(jnp.int32)
    blocks = samples // RB
    half = stations // 2
    table, taper, sign = (jnp.asarray(t) for t in dft_tables())
    nearby, scale = (jnp.asarray(t) for t in smooth_tables())
    group = station_group[None, :]
    shape = jax.ShapeDtypeStruct

    halo = shape((blocks // 2, stations), F32)
    in_hbm = [pltpu.with_memory_space_constraint(a, pltpu.HBM) for a in (raw_data, table)]
    raw, sums, even, odd = call(
        sums_kernel,
        (shape(raw_data.shape, F32), shape((stations, blocks), F32), halo, halo),
        (place, in_hbm[0]),
        specs=[SMEM, HBM],
        scratch_shapes=[pltpu.VMEM((stations, RB), F32), pltpu.SemaphoreType.DMA((6,))],
        flops=2 * stations * samples,
    )
    even, odd = neighbour_swap(even, odd)
    sent = shape((half, 2 * NBIN), BF16)
    kept = shape((half, 2 * NBIN), F32)
    inner = (blocks - 2 * RAMH + 1) * RB
    partial = shape((stations, 2 * NBIN), F32)
    table, middle, ahead, behind = call(
        middle_kernel,
        (shape(table.shape, BF16), shape((stations, inner), BF16), partial, partial),
        (raw, sums, in_hbm[1], taper),
        specs=[VMEM, VMEM, HBM, VMEM],
        scratch_shapes=[pltpu.VMEM((stations, inner), BF16), pltpu.SemaphoreType.DMA],
        flops=4 * stations * inner * NBIN,
    )
    edge = shape((stations, samples - inner), BF16)
    outer, even, odd, keep_right, keep_left = call(
        functools.partial(normalize_kernel, slabs),
        (edge, sent, sent, kept, kept),
        (place, raw, sums, even, odd, table, taper, sign, ahead, behind),
        specs=[SMEM] + [VMEM] * 9,
        scratch_shapes=[pltpu.VMEM(edge.shape, BF16)],
        flops=4 * stations * samples * NBIN,
        limit=16,
    )
    even, odd = neighbour_swap(even, odd)
    own = call(
        own_kernel,
        shape((2 * SUB, NBIN), BF16),
        (outer, middle, table, taper, sign, group, nearby, scale),
        scratch_shapes=[pltpu.VMEM((2 * stations, HOP), BF16)],
        flops=4 * stations * samples * NBIN,
        limit=32,
    )
    direct = slabs <= 8 and slabs & (slabs - 1) == 0 and NBIN // slabs % 128 == 0
    width = NBIN // slabs
    rows = 6 * SUB
    pieces = call(
        crossing_kernel,
        tuple([shape((rows, width), BF16)] * slabs) if direct else (shape((rows, NBIN), BF16),),
        (place, keep_right, keep_left, even, odd, own, group, nearby, scale),
        specs=[SMEM] + [VMEM] * 8,
        scratch_shapes=[pltpu.VMEM((rows, NBIN), BF16)],
        flops=8 * stations * NBIN * NBIN,
        limit=32,
    )
    if direct:
        order = sorted(range(1, slabs), key=lambda m: (m % 2 == 0, m))
        received = {m: swapped(pieces[m], "tchunk", m) for m in order}
        mine = jnp.concatenate([pieces[0]] + [received[m] for m in range(1, slabs)], axis=0)
    else:
        mine = pieces[0].reshape(rows, slabs, width).swapaxes(0, 1)
        mine = lax.all_to_all(mine, "tchunk", split_axis=0, concat_axis=0, tiled=True)
        mine = mine[jnp.arange(slabs) ^ me].reshape(slabs * rows, width)
    segments = SEG_DEV * slabs - 1
    if count_blocks == 4:
        across = swapped(mine, "stn", 2)
        others = [mine, swapped(mine, "stn", 1), across, swapped(across, "stn", 1)]
    else:
        gathered = lax.all_gather(mine, "stn", axis=0)
        others = [lax.dynamic_index_in_dim(gathered, place[1] ^ m, 0, keepdims=False) for m in range(count_blocks)]
    out = call(
        functools.partial(cross_kernel, segments, slabs),
        shape((MAXP, width, 2 * SUB * SUB), F32),
        (place, partner_blocks, *others),
        specs=[SMEM, SMEM] + [VMEM] * count_blocks,
        out_specs=pl.BlockSpec((1, width, 2 * SUB * SUB), lambda i: (i, 0, 0)),
        grid=(MAXP,),
        scratch_shapes=[pltpu.VMEM((segments, 2, SUB, width), F32)] * 2 + [pltpu.VMEM((slabs, rows, width), BF16)],
        flops=MAXP * segments * width * SUB * SUB * 8,
        limit=32,
    )
    return out[None]


def solution(mesh):
    placed = (P("stn", ("hour", "tchunk")), P("stn"), P("stn", None))
    return jax.shard_map(
        body,
        mesh=mesh,
        in_specs=placed,
        out_specs=P(("hour", "stn"), None, "tchunk", None),
        check_vma=False,
    )
```

time: 45.9 us -> 37 us (0.81)
  starting transfers between devices: 18.3 us -> 12.3 us
  local copies, waits for them, and re-layouts: 5.64 us -> 0.78 us
  Pallas kernels: 10.4 us -> 13.7 us
  waiting for transfers between devices: 10.8 us -> 9.88 us
    unnamed x16 -> x17, local copies, waits for them, and re-layouts: 5.07 us -> 0.77 us
    pallas_call x5 -> x6, Pallas kernels: 10.4 us -> 13.7 us  [call(): pl.pallas_call(kernel, out_shape=out_shape, in_specs=specs or [VMEM] * le...]
    ppermute x4, starting transfers between devices: 9.52 us -> 6.32 us  [neighbour_swap(): lax.ppermute(block, ('stn', 'tchunk'), part)]
    ppermute x6, starting transfers between devices: 8.82 us -> 5.95 us  [swapped(): lax.ppermute(block, axis, [(i, i ^ mask) for i in range(lax.axis_size(axi...]
    ppermute x6, waiting for transfers between devices: 9.23 us -> 8.5 us  [swapped(): lax.ppermute(block, axis, [(i, i ^ mask) for i in range(lax.axis_size(axi...]
    gather x1 -> x0, local copies, waits for them, and re-layouts: 0.57 us -> none  [body(): mine = jnp.stack(received, 0)[order]]
  transfers between devices with their start and end apart: 10 -> 10, of which waited for: 6 -> 5; matrix products, arithmetic and copies ran while one was open for 0% -> 0% of each run, Pallas kernels for 4% -> 13%
where the time goes in v2:
time: 37 us; the launch traced here: 36.8 us
  Pallas kernels  13.7 us (37%)
  starting transfers between devices  12.3 us (33%)
  waiting for transfers between devices  9.88 us (27%)
  local copies, waits for them, and re-layouts  0.78 us (2%)
    pallas_call x6, Pallas kernels, call(): pl.pallas_call(kernel, out_shape=out_shape, in_specs=specs or [VMEM] * le...  13.7 us
    ppermute x6, waiting for transfers between devices, swapped(): lax.ppermute(block, axis, [(i, i ^ mask) for i in range(lax.axis_size(axi...  8.5 us
    ppermute x4, starting transfers between devices, neighbour_swap(): lax.ppermute(block, ('stn', 'tchunk'), part)  6.32 us
    ppermute x6, starting transfers between devices, swapped(): lax.ppermute(block, axis, [(i, i ^ mask) for i in range(lax.axis_size(axi...  5.95 us
    ppermute x4, waiting for transfers between devices, neighbour_swap(): lax.ppermute(block, ('stn', 'tchunk'), part)  1.39 us
    unnamed x17, local copies, waits for them, and re-layouts  0.77 us
  transfers between devices with their start and end apart: 10, of which 5 were waited for; matrix products, arithmetic and copies ran while one was open for 0% of the time, Pallas kernels for 13%

profile of v2, /device:TPU:0, one launch (start us, length us, event | category | flops | bytes accessed | tf_op | source)
XLA Modules:
  0.0 36.8 jit_solution(6023108042174071386)
XLA Ops:
  0.0 0.1 pad_add_fusion.place
  0.1 2.7 %shard_map.82 = (f32[144,4096]{1,0:T(8,128)S(1)}, f32[144,32]{1,0:T(8,128)S(1)}, f32[16,144]{1,0:T(8,128)S(1)}, f32[16,144]{1,0:T(8,128)S(1)}) custom-call(s32[2]{0:T(128)S(1)} %pad_add_fusion.place, f32[144,4096]{1,0:T(8,128)} %source.2), custom_call_target="tpu_custom_call" | custom-call | flops 1179648 | bytes 4755464 | tf_op jit(solution)/shard_map/pallas_call | solution.py:71
  2.8 3.1 %collective-permute-start = (f32[16,144]{1,0:T(8,128)S(1)}, f32[16,144]{1,0:T(8,128)S(1)}, u32[]{:S(2)}, u32[]{:S(2)}) collective-permute-start(f32[16,144]{1,0:T(8,128)S(1)} %get-tuple-element.24), channel_id=1, source_target_pairs={{0,1},{1,0},{2,3},{3,2},{4,5},{5,4},{6,7},{7,6},{8,9},{9,8},{10,11... | collective-permute-start | bytes 27656 | tf_op jit(solution)/shard_map/ppermute | solution.py:61
  5.9 0.0 collective-permute-start.1
  5.9 0.7 %copy-done.1 = f32[2,2048]{1,0:T(2,128)S(1)} copy-done((f32[2,2048]{1,0:T(2,128)S(1)}, f32[2,2048]{1,0:T(2,128)}, u32[]{:S(2)}) %copy-start.1) | copy-done | bytes 16408
  6.6 3.0 %shard_map.83 = (bf16[2048,1024]{1,0:T(8,128)(2,1)S(1)}, bf16[144,1664]{1,0:T(8,128)(2,1)S(1)}, f32[144,1024]{1,0:T(8,128)S(1)}, f32[144,1024]{1,0:T(8,128)S(1)}) custom-call(f32[144,4096]{1,0:T(8,128)S(1)} %get-tuple-element.22.raw, f32[144,32]{1,0:T(8,128)S(1)} %get-tuple-element.23.sums, bf16[2048,1024]{1,0:T(8,128)(2,1)} %constant.17.clone.source, ...), custom_call_target="tpu_custom_call" | custom-call | flops 490733568 | bytes 12441600 | tf_op jit(solution)/shard_map/pallas_call | solution.py:71
  9.6 0.0 copy-start
  9.6 0.0 copy-start.2
  9.6 0.0 copy-start.4
  9.6 0.0 copy-start.5
  9.7 0.0 collective-permute-done.from_even
  9.7 0.0 collective-permute-done.1.from_odd
  9.7 2.6 %shard_map.84 = (bf16[144,2432]{1,0:T(8,128)(2,1)S(1)}, bf16[72,1024]{1,0:T(8,128)(2,1)S(1)}, bf16[72,1024]{1,0:T(8,128)(2,1)S(1)}, f32[72,1024]{1,0:T(8,128)S(1)}, f32[72,1024]{1,0:T(8,128)S(1)}) custom-call(s32[2]{0:T(128)S(1)} %pad_add_fusion.place, f32[144,4096]{1,0:T(8,128)S(1)} %get-tuple-element.22.raw, f32[144,32]{1,0:T(8,128)S(1)} %get-tuple-element.23.sums, ...), custom_call_target="tpu_custom_call" | custom-call | flops 1207959552 | bytes 9375752 | tf_op jit(solution)/shard_map/pallas_call | solution.py:71
  12.3 0.0 copy-start.6
  12.3 3.2 %collective-permute-start.2 = (bf16[72,1024]{1,0:T(8,128)(2,1)S(1)}, bf16[72,1024]{1,0:T(8,128)(2,1)S(1)}, u32[]{:S(2)}, u32[]{:S(2)}) collective-permute-start(bf16[72,1024]{1,0:T(8,128)(2,1)S(1)} %get-tuple-element.31), channel_id=1, source_target_pairs={{0,1},{1,0},{2,3},{3,2},{4,5},{5,4},{6,7},{7,6},{8,9},{9,8},{10,11... | collective-permute-start | bytes 442376 | tf_op jit(solution)/shard_map/ppermute | solution.py:61
  15.5 0.0 collective-permute-start.3
  15.5 1.9 %shard_map.85.own = bf16[32,512]{1,0:T(8,128)(2,1)S(1)} custom-call(bf16[144,2432]{1,0:T(8,128)(2,1)S(1)} %get-tuple-element.33.outer, bf16[144,1664]{1,0:T(8,128)(2,1)S(1)} %get-tuple-element.34.middle, bf16[2048,1024]{1,0:T(8,128)(2,1)S(1)} %get-tuple-element.26.table, f32[2,2048]{1,0:T(2,128)S(1)} %copy-done.2, f32[1,1024]{1,0:T(1,128)S(1)} %copy-done.3, ...), custom_call_target="tpu_custom_call" | custom-call | flops 1207959552 | bytes 5954112 | tf_op jit(solution)/shard_map/pallas_call | solution.py:71
  17.4 1.4 %collective-permute-done.2.from_even = bf16[72,1024]{1,0:T(8,128)(2,1)S(1)} collective-permute-done((bf16[72,1024]{1,0:T(8,128)(2,1)S(1)}, bf16[72,1024]{1,0:T(8,128)(2,1)S(1)}, u32[]{:S(2)}, u32[]{:S(2)}) %collective-permute-start.2) | collective-permute-done | bytes 147488 | tf_op jit(solution)/shard_map/ppermute | solution.py:61
  18.8 0.0 collective-permute-done.3.from_odd
  18.8 1.1 %shard_map.86 = (bf16[96,128]{1,0:T(8,128)(2,1)S(1)}, bf16[96,128]{1,0:T(8,128)(2,1)S(1)}, bf16[96,128]{1,0:T(8,128)(2,1)S(1)}, bf16[96,128]{1,0:T(8,128)(2,1)S(1)}) custom-call(s32[2]{0:T(128)S(1)} %pad_add_fusion.place, f32[72,1024]{1,0:T(8,128)S(1)} %get-tuple-element.29.keep_right, f32[72,1024]{1,0:T(8,128)S(1)} %get-tuple-element.30.keep_left, ...), custom_call_target="tpu_custom_call" | custom-call | flops 301989888 | bytes 1542728 | tf_op jit(solution)/shard_map/pallas_call | solution.py:71
  19.9 2.0 %collective-permute-start.4 = (bf16[96,128]{1,0:T(8,128)(2,1)S(1)}, bf16[96,128]{1,0:T(8,128)(2,1)S(1)}, u32[]{:S(2)}, u32[]{:S(2)}) collective-permute-start(bf16[96,128]{1,0:T(8,128)(2,1)S(1)} %get-tuple-element.36), channel_id=1, source_target_pairs={{0,1},{1,0},{2,3},{3,2},{4,5},{5,4},{6,7},{7,6},{8,9},{9,8},{10,11... | collective-permute-start | bytes 73736 | tf_op jit(solution)/shard_map/ppermute | solution.py:65
  21.9 0.9 %collective-permute-start.5 = (bf16[96,128]{1,0:T(8,128)(2,1)S(1)}, bf16[96,128]{1,0:T(8,128)(2,1)S(1)}, u32[]{:S(2)}, u32[]{:S(2)}) collective-permute-start(bf16[96,128]{1,0:T(8,128)(2,1)S(1)} %get-tuple-element.37), channel_id=1, source_target_pairs={{0,2},{1,3},{2,0},{3,1},{4,6},{5,7},{6,4},{7,5},{8,10},{9,11},{10,... | collective-permute-start | bytes 73736 | tf_op jit(solution)/shard_map/ppermute | solution.py:65
  22.9 1.5 %collective-permute-start.6 = (bf16[96,128]{1,0:T(8,128)(2,1)S(1)}, bf16[96,128]{1,0:T(8,128)(2,1)S(1)}, u32[]{:S(2)}, u32[]{:S(2)}) collective-permute-start(bf16[96,128]{1,0:T(8,128)(2,1)S(1)} %get-tuple-element.38), channel_id=1, source_target_pairs={{0,3},{1,2},{2,1},{3,0},{4,7},{5,6},{6,5},{7,4},{8,11},{9,10},{10,... | collective-permute-start | bytes 73736 | tf_op jit(solution)/shard_map/ppermute | solution.py:65
  24.4 0.0 collective-permute-done.4
  24.4 2.5 %collective-permute-done.5 = bf16[96,128]{1,0:T(8,128)(2,1)S(1)} collective-permute-done((bf16[96,128]{1,0:T(8,128)(2,1)S(1)}, bf16[96,128]{1,0:T(8,128)(2,1)S(1)}, u32[]{:S(2)}, u32[]{:S(2)}) %collective-permute-start.5) | collective-permute-done | bytes 24608 | tf_op jit(solution)/shard_map/ppermute | solution.py:65
  26.9 1.6 %collective-permute-done.6 = bf16[96,128]{1,0:T(8,128)(2,1)S(1)} collective-permute-done((bf16[96,128]{1,0:T(8,128)(2,1)S(1)}, bf16[96,128]{1,0:T(8,128)(2,1)S(1)}, u32[]{:S(2)}, u32[]{:S(2)}) %collective-permute-start.6) | collective-permute-done | bytes 24608 | tf_op jit(solution)/shard_map/ppermute | solution.py:65
  28.5 1.5 %collective-permute-start.8 = (bf16[384,128]{1,0:T(8,128)(2,1)S(1)}, bf16[384,128]{1,0:T(8,128)(2,1)S(1)}, u32[]{:S(2)}, u32[]{:S(2)}) collective-permute-start(bf16[384,128]{1,0:T(8,128)(2,1)S(1)} %constant_dynamic-update-slice_fusion.refs_0_), channel_id=1, source_target_pairs={{0,8},{4,12},{8,0},{12,4},{1,9},{5,13},{9,1},{13,5},{2,10},{6,14},... | collective-permute-start | bytes 294920 | tf_op jit(solution)/shard_map/ppermute | solution.py:65
  30.0 0.0 collective-permute-start.7
  30.0 3.1 %collective-permute-done.8.refs_2_ = bf16[384,128]{1,0:T(8,128)(2,1)S(1)} collective-permute-done((bf16[384,128]{1,0:T(8,128)(2,1)S(1)}, bf16[384,128]{1,0:T(8,128)(2,1)S(1)}, u32[]{:S(2)}, u32[]{:S(2)}) %collective-permute-start.8) | collective-permute-done | bytes 98336 | tf_op jit(solution)/shard_map/ppermute | solution.py:65
  33.1 0.0 collective-permute-start.9
  33.1 1.3 %collective-permute-done.9.refs_3_ = bf16[384,128]{1,0:T(8,128)(2,1)S(1)} collective-permute-done((bf16[384,128]{1,0:T(8,128)(2,1)S(1)}, bf16[384,128]{1,0:T(8,128)(2,1)S(1)}, u32[]{:S(2)}, u32[]{:S(2)}) %collective-permute-start.9) | collective-permute-done | bytes 98336 | tf_op jit(solution)/shard_map/ppermute | solution.py:65
  34.4 2.4 %shard_map.87 = f32[3,128,512]{2,1,0:T(8,128)} custom-call(s32[2]{0:T(128)S(1)} %pad_add_fusion.place, s32[1,3]{1,0:T(1,128)S(1)} %copy-done.6, bf16[384,128]{1,0:T(8,128)(2,1)S(1)} %constant_dynamic-update-slice_fusion.refs_0_, bf16[384,128]{1,0:T(8,128)(2,1)S(1)} %collective-permute-done.7.refs_1_, bf16[384,128]{1,0:T(8,128)(2,1)S(1)} %collective-permute-done.8.refs_2_, ...), custom_call_target="tpu_custom_call" | custom-call | flops 5505024 | bytes 1179668 | tf_op jit(solution)/shard_map/pallas_call | solution.py:71
  (13 shorter events, 0.0 us)
Async XLA Ops:
  0.1 9.6 %copy-start.3 = (f32[1,1024]{1,0:T(1,128)S(1)}, f32[1,1024]{1,0:T(1,128)}, u32[]{:S(2)}) copy-start(f32[1,1024]{1,0:T(1,128)} %constant.19.clone.sign) | copy-start | bytes 12292
  2.8 6.9 %collective-permute-start = (f32[16,144]{1,0:T(8,128)S(1)}, f32[16,144]{1,0:T(8,128)S(1)}, u32[]{:S(2)}, u32[]{:S(2)}) collective-permute-start(f32[16,144]{1,0:T(8,128)S(1)} %get-tuple-element.24), channel_id=1, source_target_pairs={{0,1},{1,0},{2,3},{3,2},{4,5},{5,4},{6,7},{7,6},{8,9},{9,8},{10,11... | collective-permute-start | bytes 27656 | tf_op jit(solution)/shard_map/ppermute | solution.py:61
  5.9 3.8 %collective-permute-start.1 = (f32[16,144]{1,0:T(8,128)S(1)}, f32[16,144]{1,0:T(8,128)S(1)}, u32[]{:S(2)}, u32[]{:S(2)}) collective-permute-start(f32[16,144]{1,0:T(8,128)S(1)} %get-tuple-element.25), channel_id=1, source_target_pairs={{1,2},{2,1},{5,6},{6,5},{9,10},{10,9},{13,14},{14,13},{0,4},{3,7},... | collective-permute-start | bytes 27656 | tf_op jit(solution)/shard_map/ppermute | solution.py:61
  5.9 0.7 %copy-start.1 = (f32[2,2048]{1,0:T(2,128)S(1)}, f32[2,2048]{1,0:T(2,128)}, u32[]{:S(2)}) copy-start(f32[2,2048]{1,0:T(2,128)} %constant.18.clone.taper) | copy-start | bytes 49156
  9.6 5.9 %copy-start = (bf16[512,512]{1,0:T(8,128)(2,1)S(1)}, bf16[512,512]{1,0:T(8,128)(2,1)}, u32[]{:S(2)}) copy-start(bf16[512,512]{1,0:T(8,128)(2,1)} %constant.20.clone.nearby) | copy-start | bytes 1572868
  9.6 5.9 %copy-start.2 = (f32[2,2048]{1,0:T(2,128)S(1)}, f32[2,2048]{1,0:T(2,128)}, u32[]{:S(2)}) copy-start(f32[2,2048]{1,0:T(2,128)} %constant.18.clone.taper) | copy-start | bytes 49156
  9.6 5.9 %copy-start.4 = (f32[1,512]{1,0:T(1,128)S(1)}, f32[1,512]{1,0:T(1,128)}, u32[]{:S(2)}) copy-start(f32[1,512]{1,0:T(1,128)} %constant.21.clone.scale) | copy-start | bytes 6148
  9.6 5.9 %copy-start.5 = (s32[144]{0:T(256)S(1)}, s32[144]{0:T(256)}, u32[]{:S(2)}) copy-start(s32[144]{0:T(256)} %param.9) | copy-start | bytes 1732
  12.3 22.1 %copy-start.6 = (s32[1,3]{1,0:T(1,128)S(1)}, s32[1,3]{1,0:T(1,128)}, u32[]{:S(2)}) copy-start(s32[1,3]{1,0:T(1,128)} %partners.1) | copy-start | bytes 40
  12.3 6.5 %collective-permute-start.2 = (bf16[72,1024]{1,0:T(8,128)(2,1)S(1)}, bf16[72,1024]{1,0:T(8,128)(2,1)S(1)}, u32[]{:S(2)}, u32[]{:S(2)}) collective-permute-start(bf16[72,1024]{1,0:T(8,128)(2,1)S(1)} %get-tuple-element.31), channel_id=1, source_target_pairs={{0,1},{1,0},{2,3},{3,2},{4,5},{5,4},{6,7},{7,6},{8,9},{9,8},{10,11... | collective-permute-start | bytes 442376 | tf_op jit(solution)/shard_map/ppermute | solution.py:61
  15.5 3.3 %collective-permute-start.3 = (bf16[72,1024]{1,0:T(8,128)(2,1)S(1)}, bf16[72,1024]{1,0:T(8,128)(2,1)S(1)}, u32[]{:S(2)}, u32[]{:S(2)}) collective-permute-start(bf16[72,1024]{1,0:T(8,128)(2,1)S(1)} %get-tuple-element.32), channel_id=1, source_target_pairs={{1,2},{2,1},{5,6},{6,5},{9,10},{10,9},{13,14},{14,13},{0,4},{3,7},... | collective-permute-start | bytes 442376 | tf_op jit(solution)/shard_map/ppermute | solution.py:61
  19.9 4.5 %collective-permute-start.4 = (bf16[96,128]{1,0:T(8,128)(2,1)S(1)}, bf16[96,128]{1,0:T(8,128)(2,1)S(1)}, u32[]{:S(2)}, u32[]{:S(2)}) collective-permute-start(bf16[96,128]{1,0:T(8,128)(2,1)S(1)} %get-tuple-element.36), channel_id=1, source_target_pairs={{0,1},{1,0},{2,3},{3,2},{4,5},{5,4},{6,7},{7,6},{8,9},{9,8},{10,11... | collective-permute-start | bytes 73736 | tf_op jit(solution)/shard_map/ppermute | solution.py:65
  21.9 5.0 %collective-permute-start.5 = (bf16[96,128]{1,0:T(8,128)(2,1)S(1)}, bf16[96,128]{1,0:T(8,128)(2,1)S(1)}, u32[]{:S(2)}, u32[]{:S(2)}) collective-permute-start(bf16[96,128]{1,0:T(8,128)(2,1)S(1)} %get-tuple-element.37), channel_id=1, source_target_pairs={{0,2},{1,3},{2,0},{3,1},{4,6},{5,7},{6,4},{7,5},{8,10},{9,11},{10,... | collective-permute-start | bytes 73736 | tf_op jit(solution)/shard_map/ppermute | solution.py:65
  22.9 5.6 %collective-permute-start.6 = (bf16[96,128]{1,0:T(8,128)(2,1)S(1)}, bf16[96,128]{1,0:T(8,128)(2,1)S(1)}, u32[]{:S(2)}, u32[]{:S(2)}) collective-permute-start(bf16[96,128]{1,0:T(8,128)(2,1)S(1)} %get-tuple-element.38), channel_id=1, source_target_pairs={{0,3},{1,2},{2,1},{3,0},{4,7},{5,6},{6,5},{7,4},{8,11},{9,10},{10,... | collective-permute-start | bytes 73736 | tf_op jit(solution)/shard_map/ppermute | solution.py:65
  28.5 4.6 %collective-permute-start.8 = (bf16[384,128]{1,0:T(8,128)(2,1)S(1)}, bf16[384,128]{1,0:T(8,128)(2,1)S(1)}, u32[]{:S(2)}, u32[]{:S(2)}) collective-permute-start(bf16[384,128]{1,0:T(8,128)(2,1)S(1)} %constant_dynamic-update-slice_fusion.refs_0_), channel_id=1, source_target_pairs={{0,8},{4,12},{8,0},{12,4},{1,9},{5,13},{9,1},{13,5},{2,10},{6,14},... | collective-permute-start | bytes 294920 | tf_op jit(solution)/shard_map/ppermute | solution.py:65
  30.0 3.1 %collective-permute-start.7 = (bf16[384,128]{1,0:T(8,128)(2,1)S(1)}, bf16[384,128]{1,0:T(8,128)(2,1)S(1)}, u32[]{:S(2)}, u32[]{:S(2)}) collective-permute-start(bf16[384,128]{1,0:T(8,128)(2,1)S(1)} %constant_dynamic-update-slice_fusion.refs_0_), channel_id=1, source_target_pairs={{0,4},{4,0},{8,12},{12,8},{1,5},{5,1},{9,13},{13,9},{2,6},{6,2},{1... | collective-permute-start | bytes 294920 | tf_op jit(solution)/shard_map/ppermute | solution.py:65
  33.1 1.3 %collective-permute-start.9 = (bf16[384,128]{1,0:T(8,128)(2,1)S(1)}, bf16[384,128]{1,0:T(8,128)(2,1)S(1)}, u32[]{:S(2)}, u32[]{:S(2)}) collective-permute-start(bf16[384,128]{1,0:T(8,128)(2,1)S(1)} %collective-permute-done.8.refs_2_), channel_id=1, source_target_pairs={{0,4},{4,0},{8,12},{12,8},{1,5},{5,1},{9,13},{13,9},{2,6},{6,2},{1... | collective-permute-start | bytes 294920 | tf_op jit(solution)/shard_map/ppermute | solution.py:65

commit v3 on v2

--- a/solution.py
+++ b/solution.py
@@ -27,7 +27,6 @@
 F32 = jnp.float32
 VMEM = pl.BlockSpec(memory_space=pltpu.VMEM)
 HBM = pl.BlockSpec(memory_space=pltpu.HBM)
-SMEM = pl.BlockSpec(memory_space=pltpu.SMEM)
 MIB = 1 << 20
 
 
@@ -38,9 +37,8 @@
     phases = sample[:, None] * frequency[None, :] % SEGLEN
     matrix = np.concatenate([np.cos(turn)[phases], -np.sin(turn)[phases]], axis=1)
     taper = (0.5 - 0.5 * np.cos(turn)).reshape(2, HOP)
-    sign = np.concatenate([(-1.0) ** frequency] * 2)[None, :]
     matrix = matrix.astype(np.float32).astype(ml_dtypes.bfloat16)
-    return matrix, taper.astype(np.float32), sign.astype(np.float32)
+    return matrix, taper.astype(np.float32)
 
 
 def smooth_tables():
@@ -78,8 +76,8 @@
     )(*operands)
 
 
-def sums_kernel(place, source, raw, sums, to_even, to_odd, held, arrived):
-    chunks = arrived.shape[0]
+def sums_kernel(source, taper_source, raw, sums, to_even, to_odd, taper, held, arrived):
+    chunks = arrived.shape[0] - 1
     stations, samples = raw.shape
     rows = stations // chunks
     blocks = samples // RB
@@ -88,6 +86,8 @@
         here = pl.ds(step * rows, rows)
         copies.append(pltpu.make_async_copy(source.at[here], raw.at[here], arrived.at[step]))
         copies[-1].start()
+    copies.append(pltpu.make_async_copy(taper_source, taper, arrived.at[chunks]))
+    copies[-1].start()
     lane = lax.broadcasted_iota(jnp.int32, (rows, RB), 1)
     for step in range(chunks):
         copies[step].wait()
@@ -102,9 +102,10 @@
     flipped = jnp.transpose(whole)
     head = flipped[: blocks // 2]
     tail = flipped[blocks // 2 : blocks]
-    even = place[0] % 2 == 0
+    even = lax.axis_index("tchunk") % 2 == 0
     to_even[...] = jnp.where(even, tail, head)
     to_odd[...] = jnp.where(even, head, tail)
+    copies[-1].wait()
 
 
 def exact_dot(left, right, dims):
@@ -115,6 +116,11 @@
     source = lax.broadcasted_iota(jnp.int32, (rows, blocks), 0) + first
     target = lax.broadcasted_iota(jnp.int32, (rows, blocks), 1)
     return ((source >= target - RAMH) & (source < target + RAMH)).astype(F32)
+
+
+def alternating():
+    column = lax.broadcasted_iota(jnp.int32, (1, 2 * NBIN), 1)
+    return jnp.where(column % 2 == 0, -1.0, 1.0)
 
 
 def scale_blocks(raw, factor, taper, some, normal, windowed):
@@ -142,20 +148,21 @@
 
 
 def normalize_kernel(
-    slabs, place, raw, sums, from_even, from_odd, table, taper, sign, ahead, behind,
+    slabs, raw, sums, from_even, from_odd, table, taper, ahead, behind,
     normal, to_even, to_odd, keep_right, keep_left, windowed,
 ):
     stations, blocks = sums.shape
     half_blocks = from_even.shape[0]
-    even = place[0] % 2 == 0
+    me = lax.axis_index("tchunk")
+    even = me % 2 == 0
     left = jnp.where(even, from_odd[...], from_even[...])
     right = jnp.where(even, from_even[...], from_odd[...])
-    left = jnp.where(place[0] > 0, left, 0.0)
-    right = jnp.where(place[0] < slabs - 1, right, 0.0)
+    left = jnp.where(me > 0, left, 0.0)
+    right = jnp.where(me < slabs - 1, right, 0.0)
     window = exact_dot(sums[...], band(blocks, blocks, 0), ((1,), (0,)))
     window += exact_dot(left, band(half_blocks, blocks, -half_blocks), ((0,), (0,)))
     window += exact_dot(right, band(half_blocks, blocks, blocks), ((0,), (0,)))
-    block = lax.broadcasted_iota(jnp.int32, (stations, blocks), 1) + place[0] * blocks
+    block = lax.broadcasted_iota(jnp.int32, (stations, blocks), 1) + me * blocks
     counted = jnp.minimum(block + RAMH, slabs * blocks) - jnp.maximum(block - RAMH, 0)
     factor = 1.0 / (window / (RB * counted.astype(F32)) + EPS_MEAN)
     outer = [*range(RAMH), *range(blocks - RAMH + 1, blocks)]
@@ -165,6 +172,8 @@
     width = NBIN // 2
     split = RAMH * RB
     rest = windowed.shape[1] - split
+
+    sign = alternating()
 
     def keep(to_right, to_left):
         for n in range(table.shape[1] // width):
@@ -174,7 +183,7 @@
             keep_right[:, here] = right_part[:half]
             to_right[:, here] = right_part[half:].astype(BF16)
             left_part = jnp.dot(windowed[:, :split], table[:split, here], preferred_element_type=F32)
-            left_part = (left_part + behind[:, here]) * sign[:, here]
+            left_part = (left_part + behind[:, here]) * sign[:, n * width : (n + 1) * width]
             keep_left[:, here] = left_part[half:]
             to_left[:, here] = left_part[:half].astype(BF16)
 
@@ -204,7 +213,7 @@
     return (lax.broadcasted_iota(jnp.int32, shape, 0) == group).astype(BF16)
 
 
-def own_kernel(outer, middle, table, taper, sign, group, nearby, scale, beams, windowed):
+def own_kernel(outer, middle, table, taper, group, nearby, scale, beams, windowed):
     stations = outer.shape[0]
     first = RAMH * RB
     last = first + middle.shape[1]
@@ -214,16 +223,17 @@
         here = source[:, start : start + high - low].astype(F32) * taper[hop : hop + 1, inside : inside + high - low]
         windowed[hop * stations : (hop + 1) * stations, inside : inside + high - low] = here.astype(BF16)
     both = jnp.dot(windowed[...], table[...], preferred_element_type=F32)
-    spectra = both[:stations] + both[stations:] * sign[...]
+    spectra = both[:stations] + both[stations:] * alternating()
     member = members(group[...], SUB)
     for part, white in enumerate(whiten(spectra, nearby[...], scale[...])):
         beams[part * SUB : (part + 1) * SUB, :] = jnp.dot(member, white, preferred_element_type=F32).astype(BF16)
 
 
-def crossing_kernel(place, keep_right, keep_left, from_even, from_odd, own, group, nearby, scale, *out):
+def crossing_kernel(keep_right, keep_left, from_even, from_odd, own, group, nearby, scale, *out):
     half = keep_right.shape[0]
     held = out[-1]
-    even = place[0] % 2 == 0
+    me = lax.axis_index("tchunk")
+    even = me % 2 == 0
     got_even = from_even[...].astype(F32)
     got_odd = from_odd[...].astype(F32)
     ahead = keep_right[...] + jnp.where(even, got_even, got_odd)
@@ -241,46 +251,42 @@
     if pieces > 1:
         width = NBIN // pieces
         for mask in range(pieces):
-            start = pl.multiple_of((place[0] ^ mask) * width, width)
+            start = pl.multiple_of((me ^ mask) * width, width)
             out[mask][...] = held[:, pl.ds(start, width)]
     else:
         out[0][...] = held[...]
 
 
-def cross_kernel(segments, slabs, place, partners, *refs):
-    blocks, (out, mine, others, held) = refs[:-4], refs[-4:]
-    slot = pl.program_id(0)
+def cross_kernel(segments, slabs, partners, *refs):
+    blocks, (out, mine, others, held, done, finished) = refs[:-6], refs[-6:]
+    me, home = lax.axis_index("tchunk"), lax.axis_index("stn")
     width = out.shape[1]
-    partner = partners[0, slot]
-
-    def pick(target, block):
-        for m in range(slabs):
-            held[place[0] ^ m] = block[m * 6 * SUB : (m + 1) * 6 * SUB, :]
+    rows = 6 * SUB
+
+    def spread(target):
         for s in range(segments):
-            source = held.at[s // 2]
+            source, after = held.at[s // 2], held.at[s // 2 + 1]
             for part in range(2):
                 if s % 2 == 0:
                     target[s, part] = source[part * SUB : (part + 1) * SUB, :].astype(F32)
                 else:
                     ahead = source[(2 + part) * SUB : (3 + part) * SUB, :].astype(F32)
-                    behind = held[s // 2 + 1, (4 + part) * SUB : (5 + part) * SUB, :].astype(F32)
+                    behind = after[(4 + part) * SUB : (5 + part) * SUB, :].astype(F32)
                     target[s, part] = (ahead + behind).astype(BF16).astype(F32)
 
-    @pl.when(slot == 0)
-    def _():
-        pick(mine, blocks[0])
-
-    @pl.when(partner < 0)
-    def _():
-        out[...] = jnp.zeros_like(out)
-
-    @pl.when(partner >= 0)
-    def _():
-        which = partner ^ place[1]
-        for index in range(1, len(blocks)):
-            @pl.when(which == index)
-            def _(index=index):
-                pick(others, blocks[index])
+    for m in range(slabs):
+        held[me ^ m] = blocks[0][m * rows : (m + 1) * rows, :]
+    spread(mine)
+    copies = []
+    for slot in range(MAXP):
+        partner = partners[0:1, slot : slot + 1]
+        for m in range(slabs):
+            chosen = jnp.zeros((rows, width), F32)
+            for index in range(1, len(blocks)):
+                here = blocks[index][m * rows : (m + 1) * rows, :].astype(F32)
+                chosen = jnp.where(partner == home ^ index, here, chosen)
+            held[me ^ m] = chosen.astype(BF16)
+        spread(others)
         real, imag = [], []
         for q in range(SUB):
             real_sum = jnp.zeros((SUB, width), F32)
@@ -293,31 +299,34 @@
             real.append(real_sum * (1.0 / segments))
             imag.append(imag_sum * (1.0 / segments))
         half = SUB * SUB
-        out[0, :, :half] = jnp.transpose(jnp.concatenate(real, axis=0))
-        out[0, :, half:] = jnp.transpose(jnp.concatenate(imag, axis=0))
+        done[slot, :, :half] = jnp.transpose(jnp.concatenate(real, axis=0))
+        done[slot, :, half:] = jnp.transpose(jnp.concatenate(imag, axis=0))
+        copies.append(pltpu.make_async_copy(done.at[slot], out.at[slot], finished.at[slot]))
+        copies[-1].start()
+    for copy in copies:
+        copy.wait()
 
 
 def body(raw_data, station_group, partner_blocks):
     stations, samples = raw_data.shape
     slabs = lax.axis_size("tchunk")
     count_blocks = lax.axis_size("stn")
-    me = lax.axis_index("tchunk")
-    place = jnp.stack([me, lax.axis_index("stn")]).astype(jnp.int32)
+    me, home = lax.axis_index("tchunk"), lax.axis_index("stn")
     blocks = samples // RB
     half = stations // 2
-    table, taper, sign = (jnp.asarray(t) for t in dft_tables())
+    table, taper = (jnp.asarray(t) for t in dft_tables())
     nearby, scale = (jnp.asarray(t) for t in smooth_tables())
     group = station_group[None, :]
     shape = jax.ShapeDtypeStruct
 
     halo = shape((blocks // 2, stations), F32)
-    in_hbm = [pltpu.with_memory_space_constraint(a, pltpu.HBM) for a in (raw_data, table)]
-    raw, sums, even, odd = call(
+    in_hbm = [pltpu.with_memory_space_constraint(a, pltpu.HBM) for a in (raw_data, taper, table)]
+    raw, sums, even, odd, taper = call(
         sums_kernel,
-        (shape(raw_data.shape, F32), shape((stations, blocks), F32), halo, halo),
-        (place, in_hbm[0]),
-        specs=[SMEM, HBM],
-        scratch_shapes=[pltpu.VMEM((stations, RB), F32), pltpu.SemaphoreType.DMA((6,))],
+        (shape(raw_data.shape, F32), shape((stations, blocks), F32), halo, halo, shape(taper.shape, F32)),
+        in_hbm[:2],
+        specs=[HBM, HBM],
+        scratch_shapes=[pltpu.VMEM((stations, RB), F32), pltpu.SemaphoreType.DMA((4,))],
         flops=2 * stations * samples,
     )
     even, odd = neighbour_swap(even, odd)
@@ -328,7 +337,7 @@
     table, middle, ahead, behind = call(
         middle_kernel,
         (shape(table.shape, BF16), shape((stations, inner), BF16), partial, partial),
-        (raw, sums, in_hbm[1], taper),
+        (raw, sums, in_hbm[2], taper),
         specs=[VMEM, VMEM, HBM, VMEM],
         scratch_shapes=[pltpu.VMEM((stations, inner), BF16), pltpu.SemaphoreType.DMA],
         flops=4 * stations * inner * NBIN,
@@ -337,8 +346,7 @@
     outer, even, odd, keep_right, keep_left = call(
         functools.partial(normalize_kernel, slabs),
         (edge, sent, sent, kept, kept),
-        (place, raw, sums, even, odd, table, taper, sign, ahead, behind),
-        specs=[SMEM] + [VMEM] * 9,
+        (raw, sums, even, odd, table, taper, ahead, behind),
         scratch_shapes=[pltpu.VMEM(edge.shape, BF16)],
         flops=4 * stations * samples * NBIN,
         limit=16,
@@ -347,7 +355,7 @@
     own = call(
         own_kernel,
         shape((2 * SUB, NBIN), BF16),
-        (outer, middle, table, taper, sign, group, nearby, scale),
+        (outer, middle, table, taper, group, nearby, scale),
         scratch_shapes=[pltpu.VMEM((2 * stations, HOP), BF16)],
         flops=4 * stations * samples * NBIN,
         limit=32,
@@ -358,8 +366,7 @@
     pieces = call(
         crossing_kernel,
         tuple([shape((rows, width), BF16)] * slabs) if direct else (shape((rows, NBIN), BF16),),
-        (place, keep_right, keep_left, even, odd, own, group, nearby, scale),
-        specs=[SMEM] + [VMEM] * 8,
+        (keep_right, keep_left, even, odd, own, group, nearby, scale),
         scratch_shapes=[pltpu.VMEM((rows, NBIN), BF16)],
         flops=8 * stations * NBIN * NBIN,
         limit=32,
@@ -378,15 +385,15 @@
         others = [mine, swapped(mine, "stn", 1), across, swapped(across, "stn", 1)]
     else:
         gathered = lax.all_gather(mine, "stn", axis=0)
-        others = [lax.dynamic_index_in_dim(gathered, place[1] ^ m, 0, keepdims=False) for m in range(count_blocks)]
+        others = [lax.dynamic_index_in_dim(gathered, home ^ m, 0, keepdims=False) for m in range(count_blocks)]
+    result = (MAXP, width, 2 * SUB * SUB)
     out = call(
         functools.partial(cross_kernel, segments, slabs),
-        shape((MAXP, width, 2 * SUB * SUB), F32),
-        (place, partner_blocks, *others),
-        specs=[SMEM, SMEM] + [VMEM] * count_blocks,
-        out_specs=pl.BlockSpec((1, width, 2 * SUB * SUB), lambda i: (i, 0, 0)),
-        grid=(MAXP,),
-        scratch_shapes=[pltpu.VMEM((segments, 2, SUB, width), F32)] * 2 + [pltpu.VMEM((slabs, rows, width), BF16)],
+        shape(result, F32),
+        (partner_blocks, *others),
+        out_specs=HBM,
+        scratch_shapes=[pltpu.VMEM((segments, 2, SUB, width), F32)] * 2
+        + [pltpu.VMEM((slabs, rows, width), BF16), pltpu.VMEM(result, F32), pltpu.SemaphoreType.DMA((MAXP,))],
         flops=MAXP * segments * width * SUB * SUB * 8,
         limit=32,
     )

time: 37 us -> 33.8 us (0.914)
  Pallas kernels: 13.7 us -> 11.3 us
  local copies, waits for them, and re-layouts: 0.78 us -> 0.05 us
    pallas_call x6, Pallas kernels: 13.7 us -> 11.3 us  [call(): pl.pallas_call(kernel, out_shape=out_shape, in_specs=specs or [VMEM] * le...]
    unnamed x17 -> x11, local copies, waits for them, and re-layouts: 0.77 us -> 0.05 us
  transfers between devices with their start and end apart: 10 -> 10, of which waited for: 5 -> 5; matrix products, arithmetic and copies ran while one was open for 0% -> 0% of each run, Pallas kernels for 13% -> 14%
where the time goes in v3:
time: 33.8 us; the launch traced here: 33.6 us
  starting transfers between devices  12.3 us (36%)
  Pallas kernels  11.3 us (33%)
  waiting for transfers between devices  9.88 us (29%)
    pallas_call x6, Pallas kernels, call(): pl.pallas_call(kernel, out_shape=out_shape, in_specs=specs or [VMEM] * le...  11.3 us
    ppermute x6, waiting for transfers between devices, swapped(): lax.ppermute(block, axis, [(i, i ^ mask) for i in range(lax.axis_size(axi...  8.5 us
    ppermute x4, starting transfers between devices, neighbour_swap(): lax.ppermute(block, ('stn', 'tchunk'), part)  6.31 us
    ppermute x6, starting transfers between devices, swapped(): lax.ppermute(block, axis, [(i, i ^ mask) for i in range(lax.axis_size(axi...  5.95 us
    ppermute x4, waiting for transfers between devices, neighbour_swap(): lax.ppermute(block, ('stn', 'tchunk'), part)  1.38 us
  transfers between devices with their start and end apart: 10, of which 5 were waited for; matrix products, arithmetic and copies ran while one was open for 0% of the time, Pallas kernels for 14%

profile of v3, /device:TPU:0, one launch (start us, length us, event | category | flops | bytes accessed | tf_op | source)
XLA Modules:
  0.0 33.6 jit_solution(818012814259419278)
XLA Ops:
  0.0 2.1 %shard_map.73 = (f32[144,4096]{1,0:T(8,128)S(1)}, f32[144,32]{1,0:T(8,128)S(1)}, f32[16,144]{1,0:T(8,128)S(1)}, f32[16,144]{1,0:T(8,128)S(1)}, f32[2,2048]{1,0:T(2,128)S(1)}) custom-call(f32[144,4096]{1,0:T(8,128)} %source.2, f32[2,2048]{1,0:T(2,128)} %constant.9.clone.taper_source), custom_call_target="tpu_custom_call" | custom-call | flops 1179648 | bytes 4788224 | tf_op jit(solution)/shard_map/pallas_call | solution.py:69
  2.1 3.1 %collective-permute-start = (f32[16,144]{1,0:T(8,128)S(1)}, f32[16,144]{1,0:T(8,128)S(1)}, u32[]{:S(2)}, u32[]{:S(2)}) collective-permute-start(f32[16,144]{1,0:T(8,128)S(1)} %get-tuple-element.25), channel_id=1, source_target_pairs={{0,1},{1,0},{2,3},{3,2},{4,5},{5,4},{6,7},{7,6},{8,9},{9,8},{10,11... | collective-permute-start | bytes 27656 | tf_op jit(solution)/shard_map/ppermute | solution.py:59
  5.2 0.0 collective-permute-start.1
  5.2 3.0 %shard_map.74 = (bf16[2048,1024]{1,0:T(8,128)(2,1)S(1)}, bf16[144,1664]{1,0:T(8,128)(2,1)S(1)}, f32[144,1024]{1,0:T(8,128)S(1)}, f32[144,1024]{1,0:T(8,128)S(1)}) custom-call(f32[144,4096]{1,0:T(8,128)S(1)} %get-tuple-element.23.raw, f32[144,32]{1,0:T(8,128)S(1)} %get-tuple-element.24.sums, bf16[2048,1024]{1,0:T(8,128)(2,1)} %constant.8.clone.source, ...), custom_call_target="tpu_custom_call" | custom-call | flops 490733568 | bytes 12441600 | tf_op jit(solution)/shard_map/pallas_call | solution.py:69
  8.1 0.0 copy-start
  8.2 0.0 copy-start.1
  8.2 0.0 copy-start.2
  8.2 0.0 collective-permute-done.from_even
  8.2 0.0 collective-permute-done.1.from_odd
  8.2 2.0 %shard_map.75 = (bf16[144,2432]{1,0:T(8,128)(2,1)S(1)}, bf16[72,1024]{1,0:T(8,128)(2,1)S(1)}, bf16[72,1024]{1,0:T(8,128)(2,1)S(1)}, f32[72,1024]{1,0:T(8,128)S(1)}, f32[72,1024]{1,0:T(8,128)S(1)}) custom-call(f32[144,4096]{1,0:T(8,128)S(1)} %get-tuple-element.23.raw, f32[144,32]{1,0:T(8,128)S(1)} %get-tuple-element.24.sums, ...), custom_call_target="tpu_custom_call" | custom-call | flops 1207959552 | bytes 9371648 | tf_op jit(solution)/shard_map/pallas_call | solution.py:69
  10.2 0.0 copy-start.3
  10.2 3.2 %collective-permute-start.2 = (bf16[72,1024]{1,0:T(8,128)(2,1)S(1)}, bf16[72,1024]{1,0:T(8,128)(2,1)S(1)}, u32[]{:S(2)}, u32[]{:S(2)}) collective-permute-start(bf16[72,1024]{1,0:T(8,128)(2,1)S(1)} %get-tuple-element.33), channel_id=1, source_target_pairs={{0,1},{1,0},{2,3},{3,2},{4,5},{5,4},{6,7},{7,6},{8,9},{9,8},{10,11... | collective-permute-start | bytes 442376 | tf_op jit(solution)/shard_map/ppermute | solution.py:59
  13.5 0.0 collective-permute-start.3
  13.5 0.0 copy-done.1
  13.5 0.0 copy-done.2
  13.5 1.9 %shard_map.76.own = bf16[32,512]{1,0:T(8,128)(2,1)S(1)} custom-call(bf16[144,2432]{1,0:T(8,128)(2,1)S(1)} %get-tuple-element.35.outer, bf16[144,1664]{1,0:T(8,128)(2,1)S(1)} %get-tuple-element.36.middle, bf16[2048,1024]{1,0:T(8,128)(2,1)S(1)} %get-tuple-element.28.table, f32[2,2048]{1,0:T(2,128)S(1)} %get-tuple-element.27.taper, s32[1,144]{1,0:T(1,128)S(1)} %bitcast.2, ...), custom_call_target="tpu_custom_call" | custom-call | flops 1207959552 | bytes 5950016 | tf_op jit(solution)/shard_map/pallas_call | solution.py:69
  15.4 1.4 %collective-permute-done.2.from_even = bf16[72,1024]{1,0:T(8,128)(2,1)S(1)} collective-permute-done((bf16[72,1024]{1,0:T(8,128)(2,1)S(1)}, bf16[72,1024]{1,0:T(8,128)(2,1)S(1)}, u32[]{:S(2)}, u32[]{:S(2)}) %collective-permute-start.2) | collective-permute-done | bytes 147488 | tf_op jit(solution)/shard_map/ppermute | solution.py:59
  16.8 0.0 collective-permute-done.3.from_odd
  16.8 0.6 %shard_map.77 = (bf16[96,128]{1,0:T(8,128)(2,1)S(1)}, bf16[96,128]{1,0:T(8,128)(2,1)S(1)}, bf16[96,128]{1,0:T(8,128)(2,1)S(1)}, bf16[96,128]{1,0:T(8,128)(2,1)S(1)}) custom-call(f32[72,1024]{1,0:T(8,128)S(1)} %get-tuple-element.31.keep_right, f32[72,1024]{1,0:T(8,128)S(1)} %get-tuple-element.32.keep_left, ...), custom_call_target="tpu_custom_call" | custom-call | flops 301989888 | bytes 1542720 | tf_op jit(solution)/shard_map/pallas_call | solution.py:69
  17.4 2.0 %collective-permute-start.4 = (bf16[96,128]{1,0:T(8,128)(2,1)S(1)}, bf16[96,128]{1,0:T(8,128)(2,1)S(1)}, u32[]{:S(2)}, u32[]{:S(2)}) collective-permute-start(bf16[96,128]{1,0:T(8,128)(2,1)S(1)} %get-tuple-element.38), channel_id=1, source_target_pairs={{0,1},{1,0},{2,3},{3,2},{4,5},{5,4},{6,7},{7,6},{8,9},{9,8},{10,11... | collective-permute-start | bytes 73736 | tf_op jit(solution)/shard_map/ppermute | solution.py:63
  19.4 0.9 %collective-permute-start.5 = (bf16[96,128]{1,0:T(8,128)(2,1)S(1)}, bf16[96,128]{1,0:T(8,128)(2,1)S(1)}, u32[]{:S(2)}, u32[]{:S(2)}) collective-permute-start(bf16[96,128]{1,0:T(8,128)(2,1)S(1)} %get-tuple-element.39), channel_id=1, source_target_pairs={{0,2},{1,3},{2,0},{3,1},{4,6},{5,7},{6,4},{7,5},{8,10},{9,11},{10,... | collective-permute-start | bytes 73736 | tf_op jit(solution)/shard_map/ppermute | solution.py:63
  20.3 1.5 %collective-permute-start.6 = (bf16[96,128]{1,0:T(8,128)(2,1)S(1)}, bf16[96,128]{1,0:T(8,128)(2,1)S(1)}, u32[]{:S(2)}, u32[]{:S(2)}) collective-permute-start(bf16[96,128]{1,0:T(8,128)(2,1)S(1)} %get-tuple-element.40), channel_id=1, source_target_pairs={{0,3},{1,2},{2,1},{3,0},{4,7},{5,6},{6,5},{7,4},{8,11},{9,10},{10,... | collective-permute-start | bytes 73736 | tf_op jit(solution)/shard_map/ppermute | solution.py:63
  21.8 0.0 collective-permute-done.4
  21.8 2.3 %collective-permute-done.5 = bf16[96,128]{1,0:T(8,128)(2,1)S(1)} collective-permute-done((bf16[96,128]{1,0:T(8,128)(2,1)S(1)}, bf16[96,128]{1,0:T(8,128)(2,1)S(1)}, u32[]{:S(2)}, u32[]{:S(2)}) %collective-permute-start.5) | collective-permute-done | bytes 24608 | tf_op jit(solution)/shard_map/ppermute | solution.py:63
  24.1 1.8 %collective-permute-done.6 = bf16[96,128]{1,0:T(8,128)(2,1)S(1)} collective-permute-done((bf16[96,128]{1,0:T(8,128)(2,1)S(1)}, bf16[96,128]{1,0:T(8,128)(2,1)S(1)}, u32[]{:S(2)}, u32[]{:S(2)}) %collective-permute-start.6) | collective-permute-done | bytes 24608 | tf_op jit(solution)/shard_map/ppermute | solution.py:63
  25.9 1.5 %collective-permute-start.8 = (bf16[384,128]{1,0:T(8,128)(2,1)S(1)}, bf16[384,128]{1,0:T(8,128)(2,1)S(1)}, u32[]{:S(2)}, u32[]{:S(2)}) collective-permute-start(bf16[384,128]{1,0:T(8,128)(2,1)S(1)} %constant_dynamic-update-slice_fusion.refs_0_), channel_id=1, source_target_pairs={{0,8},{4,12},{8,0},{12,4},{1,9},{5,13},{9,1},{13,5},{2,10},{6,14},... | collective-permute-start | bytes 294920 | tf_op jit(solution)/shard_map/ppermute | solution.py:63
  27.4 0.0 collective-permute-start.7
  27.4 3.1 %collective-permute-done.8.refs_2_ = bf16[384,128]{1,0:T(8,128)(2,1)S(1)} collective-permute-done((bf16[384,128]{1,0:T(8,128)(2,1)S(1)}, bf16[384,128]{1,0:T(8,128)(2,1)S(1)}, u32[]{:S(2)}, u32[]{:S(2)}) %collective-permute-start.8) | collective-permute-done | bytes 98336 | tf_op jit(solution)/shard_map/ppermute | solution.py:63
  30.5 0.0 collective-permute-start.9
  30.5 0.0 collective-permute-done.7.refs_1_
  30.5 1.3 %collective-permute-done.9.refs_3_ = bf16[384,128]{1,0:T(8,128)(2,1)S(1)} collective-permute-done((bf16[384,128]{1,0:T(8,128)(2,1)S(1)}, bf16[384,128]{1,0:T(8,128)(2,1)S(1)}, u32[]{:S(2)}, u32[]{:S(2)}) %collective-permute-start.9) | collective-permute-done | bytes 98336 | tf_op jit(solution)/shard_map/ppermute | solution.py:63
  31.8 1.7 %shard_map.78 = f32[3,128,512]{2,1,0:T(8,128)} custom-call(s32[1,3]{1,0:T(1,128)S(1)} %copy-done.3, bf16[384,128]{1,0:T(8,128)(2,1)S(1)} %constant_dynamic-update-slice_fusion.refs_0_, bf16[384,128]{1,0:T(8,128)(2,1)S(1)} %collective-permute-done.7.refs_1_, bf16[384,128]{1,0:T(8,128)(2,1)S(1)} %collective-permute-done.8.refs_2_, ...), custom_call_target="tpu_custom_call" | custom-call | flops 5505024 | bytes 1179660 | tf_op jit(solution)/shard_map/pallas_call | solution.py:69
  (6 shorter events, 0.0 us)
Async XLA Ops:
  2.1 6.1 %collective-permute-start = (f32[16,144]{1,0:T(8,128)S(1)}, f32[16,144]{1,0:T(8,128)S(1)}, u32[]{:S(2)}, u32[]{:S(2)}) collective-permute-start(f32[16,144]{1,0:T(8,128)S(1)} %get-tuple-element.25), channel_id=1, source_target_pairs={{0,1},{1,0},{2,3},{3,2},{4,5},{5,4},{6,7},{7,6},{8,9},{9,8},{10,11... | collective-permute-start | bytes 27656 | tf_op jit(solution)/shard_map/ppermute | solution.py:59
  5.2 3.0 %collective-permute-start.1 = (f32[16,144]{1,0:T(8,128)S(1)}, f32[16,144]{1,0:T(8,128)S(1)}, u32[]{:S(2)}, u32[]{:S(2)}) collective-permute-start(f32[16,144]{1,0:T(8,128)S(1)} %get-tuple-element.26), channel_id=1, source_target_pairs={{1,2},{2,1},{5,6},{6,5},{9,10},{10,9},{13,14},{14,13},{0,4},{3,7},... | collective-permute-start | bytes 27656 | tf_op jit(solution)/shard_map/ppermute | solution.py:59
  8.1 5.3 %copy-start = (bf16[512,512]{1,0:T(8,128)(2,1)S(1)}, bf16[512,512]{1,0:T(8,128)(2,1)}, u32[]{:S(2)}) copy-start(bf16[512,512]{1,0:T(8,128)(2,1)} %constant.10.clone.nearby) | copy-start | bytes 1572868
  8.2 5.3 %copy-start.1 = (f32[1,512]{1,0:T(1,128)S(1)}, f32[1,512]{1,0:T(1,128)}, u32[]{:S(2)}) copy-start(f32[1,512]{1,0:T(1,128)} %constant.11.clone.scale) | copy-start | bytes 6148
  8.2 5.3 %copy-start.2 = (s32[144]{0:T(256)S(1)}, s32[144]{0:T(256)}, u32[]{:S(2)}) copy-start(s32[144]{0:T(256)} %param.8) | copy-start | bytes 1732
  10.2 21.6 %copy-start.3 = (s32[1,3]{1,0:T(1,128)S(1)}, s32[1,3]{1,0:T(1,128)}, u32[]{:S(2)}) copy-start(s32[1,3]{1,0:T(1,128)} %partners.1) | copy-start | bytes 40
  10.2 6.5 %collective-permute-start.2 = (bf16[72,1024]{1,0:T(8,128)(2,1)S(1)}, bf16[72,1024]{1,0:T(8,128)(2,1)S(1)}, u32[]{:S(2)}, u32[]{:S(2)}) collective-permute-start(bf16[72,1024]{1,0:T(8,128)(2,1)S(1)} %get-tuple-element.33), channel_id=1, source_target_pairs={{0,1},{1,0},{2,3},{3,2},{4,5},{5,4},{6,7},{7,6},{8,9},{9,8},{10,11... | collective-permute-start | bytes 442376 | tf_op jit(solution)/shard_map/ppermute | solution.py:59
  13.5 3.3 %collective-permute-start.3 = (bf16[72,1024]{1,0:T(8,128)(2,1)S(1)}, bf16[72,1024]{1,0:T(8,128)(2,1)S(1)}, u32[]{:S(2)}, u32[]{:S(2)}) collective-permute-start(bf16[72,1024]{1,0:T(8,128)(2,1)S(1)} %get-tuple-element.34), channel_id=1, source_target_pairs={{1,2},{2,1},{5,6},{6,5},{9,10},{10,9},{13,14},{14,13},{0,4},{3,7},... | collective-permute-start | bytes 442376 | tf_op jit(solution)/shard_map/ppermute | solution.py:59
  17.4 4.5 %collective-permute-start.4 = (bf16[96,128]{1,0:T(8,128)(2,1)S(1)}, bf16[96,128]{1,0:T(8,128)(2,1)S(1)}, u32[]{:S(2)}, u32[]{:S(2)}) collective-permute-start(bf16[96,128]{1,0:T(8,128)(2,1)S(1)} %get-tuple-element.38), channel_id=1, source_target_pairs={{0,1},{1,0},{2,3},{3,2},{4,5},{5,4},{6,7},{7,6},{8,9},{9,8},{10,11... | collective-permute-start | bytes 73736 | tf_op jit(solution)/shard_map/ppermute | solution.py:63
  19.4 4.8 %collective-permute-start.5 = (bf16[96,128]{1,0:T(8,128)(2,1)S(1)}, bf16[96,128]{1,0:T(8,128)(2,1)S(1)}, u32[]{:S(2)}, u32[]{:S(2)}) collective-permute-start(bf16[96,128]{1,0:T(8,128)(2,1)S(1)} %get-tuple-element.39), channel_id=1, source_target_pairs={{0,2},{1,3},{2,0},{3,1},{4,6},{5,7},{6,4},{7,5},{8,10},{9,11},{10,... | collective-permute-start | bytes 73736 | tf_op jit(solution)/shard_map/ppermute | solution.py:63
  20.3 5.6 %collective-permute-start.6 = (bf16[96,128]{1,0:T(8,128)(2,1)S(1)}, bf16[96,128]{1,0:T(8,128)(2,1)S(1)}, u32[]{:S(2)}, u32[]{:S(2)}) collective-permute-start(bf16[96,128]{1,0:T(8,128)(2,1)S(1)} %get-tuple-element.40), channel_id=1, source_target_pairs={{0,3},{1,2},{2,1},{3,0},{4,7},{5,6},{6,5},{7,4},{8,11},{9,10},{10,... | collective-permute-start | bytes 73736 | tf_op jit(solution)/shard_map/ppermute | solution.py:63
  25.9 4.6 %collective-permute-start.8 = (bf16[384,128]{1,0:T(8,128)(2,1)S(1)}, bf16[384,128]{1,0:T(8,128)(2,1)S(1)}, u32[]{:S(2)}, u32[]{:S(2)}) collective-permute-start(bf16[384,128]{1,0:T(8,128)(2,1)S(1)} %constant_dynamic-update-slice_fusion.refs_0_), channel_id=1, source_target_pairs={{0,8},{4,12},{8,0},{12,4},{1,9},{5,13},{9,1},{13,5},{2,10},{6,14},... | collective-permute-start | bytes 294920 | tf_op jit(solution)/shard_map/ppermute | solution.py:63
  27.4 3.1 %collective-permute-start.7 = (bf16[384,128]{1,0:T(8,128)(2,1)S(1)}, bf16[384,128]{1,0:T(8,128)(2,1)S(1)}, u32[]{:S(2)}, u32[]{:S(2)}) collective-permute-start(bf16[384,128]{1,0:T(8,128)(2,1)S(1)} %constant_dynamic-update-slice_fusion.refs_0_), channel_id=1, source_target_pairs={{0,4},{4,0},{8,12},{12,8},{1,5},{5,1},{9,13},{13,9},{2,6},{6,2},{1... | collective-permute-start | bytes 294920 | tf_op jit(solution)/shard_map/ppermute | solution.py:63
  30.5 1.3 %collective-permute-start.9 = (bf16[384,128]{1,0:T(8,128)(2,1)S(1)}, bf16[384,128]{1,0:T(8,128)(2,1)S(1)}, u32[]{:S(2)}, u32[]{:S(2)}) collective-permute-start(bf16[384,128]{1,0:T(8,128)(2,1)S(1)} %collective-permute-done.8.refs_2_), channel_id=1, source_target_pairs={{0,4},{4,0},{8,12},{12,8},{1,5},{5,1},{9,13},{13,9},{2,6},{6,2},{1... | collective-permute-start | bytes 294920 | tf_op jit(solution)/shard_map/ppermute | solution.py:63

commit v4 on v3

v4 whole, which is shorter than its diff:
```python
import functools
import math

import jax
import jax.numpy as jnp
import ml_dtypes
import numpy as np
from jax import lax
from jax.experimental import pallas as pl
from jax.experimental.pallas import tpu as pltpu
from jax.sharding import PartitionSpec as P

SEG_DEV = 2
SEGLEN = 4096
HOP = 2048
NBIN = 512
RB = 128
RAMH = 10
SMOOTH = 8
SUB = 16
MAXP = 3

EPS_MEAN = 1e-06
LEVEL = 0.05

BF16 = jnp.bfloat16
F32 = jnp.float32
VMEM = pl.BlockSpec(memory_space=pltpu.VMEM)
HBM = pl.BlockSpec(memory_space=pltpu.HBM)
MIB = 1 << 20


def dft_tables():
    sample = np.arange(HOP, dtype=np.int32)
    frequency = np.arange(1, NBIN + 1, dtype=np.int32)
    turn = np.arange(SEGLEN, dtype=np.float64) * (2.0 * math.pi / SEGLEN)
    phases = sample[:, None] * frequency[None, :] % SEGLEN
    matrix = np.concatenate([np.cos(turn)[phases], -np.sin(turn)[phases]], axis=1)
    taper = (0.5 - 0.5 * np.cos(turn)).reshape(2, HOP)
    matrix = matrix.astype(np.float32).astype(ml_dtypes.bfloat16)
    return matrix, taper.astype(np.float32)


def smooth_tables():
    bin_index = np.arange(NBIN)
    nearby = np.abs(bin_index[:, None] - bin_index[None, :]) <= SMOOTH
    scale = 1.0 / np.sum(nearby, axis=0, keepdims=True)
    return nearby.astype(ml_dtypes.bfloat16), scale.astype(np.float32)


def neighbour_swap(first, second, outer_first):
    blocks, slabs = lax.axis_size("stn"), lax.axis_size("tchunk")
    inner = [(i, i ^ 1) for i in range(slabs - slabs % 2)]
    outer = [(i, i + 1) for i in range(1, slabs - 1, 2)]
    outer += [(j, i) for i, j in outer]
    pairs = [[(b * slabs + i, b * slabs + j) for b in range(blocks) for i, j in part] for part in (inner, outer)]
    if blocks % 2 == 0 and slabs % 2 == 0:
        pairs[1] += [(b * slabs + i, (b ^ 1) * slabs + i) for b in range(blocks) for i in (0, slabs - 1)]
    sent = {}
    for i in (1, 0) if outer_first else (0, 1):
        sent[i] = lax.ppermute((first, second)[i], ("stn", "tchunk"), pairs[i])
    return sent[0], sent[1]


def swapped(block, axis, mask):
    return lax.ppermute(block, axis, [(i, i ^ mask) for i in range(lax.axis_size(axis))])


def call(kernel, out_shape, operands, specs=None, flops=0, limit=16, **more):
    moved = sum(math.prod(a.shape) * a.dtype.itemsize for a in list(operands) + jax.tree.leaves(out_shape))
    more.setdefault("out_specs", jax.tree.map(lambda _: VMEM, out_shape))
    return pl.pallas_call(
        kernel,
        out_shape=out_shape,
        in_specs=specs or [VMEM] * len(operands),
        compiler_params=pltpu.CompilerParams(vmem_limit_bytes=limit * MIB),
        cost_estimate=pl.CostEstimate(flops=flops, bytes_accessed=moved, transcendentals=0),
        **more,
    )(*operands)


def sums_kernel(source, taper_source, raw, sums, to_even, to_odd, taper, held, arrived):
    chunks = arrived.shape[0] - 1
    stations, samples = raw.shape
    blocks = samples // RB
    ends = [stations * n // 9 // 8 * 8 for n in (0, 3, 6, 9)]
    copies = []
    for step in range(chunks):
        rows = ends[step + 1] - ends[step]
        here = pl.ds(ends[step], rows)
        copies.append(pltpu.make_async_copy(source.at[here], raw.at[here], arrived.at[step]))
        copies[-1].start()
    copies.append(pltpu.make_async_copy(taper_source, taper, arrived.at[chunks]))
    copies[-1].start()
    for step in range(chunks):
        copies[step].wait()
        rows = ends[step + 1] - ends[step]
        here = pl.ds(ends[step], rows)
        lane = lax.broadcasted_iota(jnp.int32, (rows, RB), 1)
        total = jnp.zeros((rows, RB), F32)
        for b in range(blocks):
            amount = jnp.sum(jnp.abs(raw[here, b * RB : (b + 1) * RB]), axis=1, keepdims=True)
            total = jnp.where(lane == b, amount, total)
        held[here, :] = total
    whole = held[...]
    sums[...] = whole[:, :blocks]
    flipped = jnp.transpose(whole)
    head = flipped[: blocks // 2]
    tail = flipped[blocks // 2 : blocks]
    even = lax.axis_index("tchunk") % 2 == 0
    to_even[...] = jnp.where(even, tail, head)
    to_odd[...] = jnp.where(even, head, tail)
    copies[-1].wait()


def split_dot(left, right, axis):
    high = left.astype(BF16)
    rest = left - high.astype(F32)
    middle = rest.astype(BF16)
    low = (rest - middle.astype(F32)).astype(BF16)
    parts = jnp.concatenate([high, middle, low], axis=axis)
    return lax.dot_general(
        parts, jnp.concatenate([right] * 3, axis=0), (((axis,), (0,)), ((), ())), preferred_element_type=F32
    )


def band(rows, blocks, first):
    source = lax.broadcasted_iota(jnp.int32, (rows, blocks), 0) + first
    target = lax.broadcasted_iota(jnp.int32, (rows, blocks), 1)
    return ((source >= target - RAMH) & (source < target + RAMH)).astype(BF16)


def alternating():
    column = lax.broadcasted_iota(jnp.int32, (1, 2 * NBIN), 1)
    return jnp.where(column % 2 == 0, -1.0, 1.0)


def windowed_blocks(raw, factor, taper, rows, some, normal, windowed):
    for place, b in enumerate(some):
        here = pl.ds(place * RB, RB)
        scaled = (raw[rows, b * RB : (b + 1) * RB] * factor[rows, b : b + 1]).astype(BF16)
        if normal is not None:
            normal[:, here] = scaled
        hop, inside = divmod(b * RB, HOP)
        weight = taper[1 - hop : 2 - hop, inside : inside + RB]
        windowed[:, here] = (scaled.astype(F32) * weight).astype(BF16)


def middle_kernel(raw, sums, table, taper, normal, ahead, behind, window, windowed):
    blocks = sums.shape[1]
    window[...] = split_dot(sums[...], band(blocks, blocks, 0), 1)
    factor = 1.0 / (window[...] * (1.0 / (2 * RAMH * RB)) + EPS_MEAN)
    windowed_blocks(raw, factor, taper, slice(None), range(RAMH, blocks - RAMH + 1), normal, windowed)
    split = HOP - RAMH * RB
    rest = windowed.shape[1] - split
    ahead[...] = jnp.dot(windowed[:, split:], table[:rest, :], preferred_element_type=F32)
    behind[...] = jnp.dot(windowed[:, :split], table[HOP - split :, :], preferred_element_type=F32)


def send_kernel(
    slabs, raw, window, from_odd, from_even, table, taper, ahead, behind,
    to_even, to_odd, factor, first, last,
):
    stations, blocks = window.shape
    half_blocks = from_even.shape[0]
    half = stations // 2
    me = lax.axis_index("tchunk")
    even = me % 2 == 0
    left = jnp.where(even, from_odd[...], from_even[...])
    right = jnp.where(even, from_even[...], from_odd[...])
    left = jnp.where(me > 0, left, 0.0)
    right = jnp.where(me < slabs - 1, right, 0.0)
    near = jnp.concatenate([left, right], axis=0)
    bands = jnp.concatenate([band(half_blocks, blocks, -half_blocks), band(half_blocks, blocks, blocks)], axis=0)
    total = window[...] + split_dot(near, bands, 0)
    block = lax.broadcasted_iota(jnp.int32, (stations, blocks), 1) + me * blocks
    counted = jnp.minimum(block + RAMH, slabs * blocks) - jnp.maximum(block - RAMH, 0)
    factor[...] = 1.0 / (total / (RB * counted.astype(F32)) + EPS_MEAN)
    windowed_blocks(raw, factor, taper, slice(half, stations), range(blocks - RAMH + 1, blocks), None, last)
    windowed_blocks(raw, factor, taper, slice(0, half), range(RAMH), None, first)
    sign = alternating()
    width = NBIN // 2

    def fill(to_right, to_left):
        for n in range(table.shape[1] // width):
            here = slice(n * width, (n + 1) * width)
            part = jnp.dot(last[...], table[HOP - last.shape[1] :, here], preferred_element_type=F32)
            to_right[:, here] = (part + ahead[half:, here]).astype(BF16)
            part = jnp.dot(first[...], table[: first.shape[1], here], preferred_element_type=F32)
            to_left[:, here] = ((part + behind[:half, here]) * sign[:, here]).astype(BF16)

    @pl.when(even)
    def _():
        fill(to_even, to_odd)

    @pl.when(jnp.logical_not(even))
    def _():
        fill(to_odd, to_even)


def whiten(spectra, nearby, scale):
    real_part = spectra[:, :NBIN]
    imag_part = spectra[:, NBIN:]
    powers = real_part * real_part + imag_part * imag_part
    high = powers.astype(BF16)
    low = (powers - high.astype(F32)).astype(BF16)
    smooth = jnp.dot(high, nearby, preferred_element_type=F32) + jnp.dot(low, nearby, preferred_element_type=F32)
    floor_level = jnp.sum(powers, axis=1, keepdims=True) * (1.0 / NBIN) + 1e-06
    inverse = lax.rsqrt(smooth * scale + LEVEL * floor_level)
    return (real_part * inverse).astype(BF16), (imag_part * inverse).astype(BF16)


def members(group, count):
    shape = (count, group.shape[1])
    return (lax.broadcasted_iota(jnp.int32, shape, 0) == group).astype(BF16)


def own_kernel(
    raw, factor, middle, table, taper, ahead, behind, group, nearby, scale,
    beams, keep_right, keep_left, windowed, first, last,
):
    stations, blocks = factor.shape
    half = stations // 2
    windowed_blocks(raw, factor, taper, slice(0, half), range(blocks - RAMH + 1, blocks), None, last)
    windowed_blocks(raw, factor, taper, slice(half, stations), range(RAMH), None, first)
    part = jnp.dot(last[...], table[HOP - last.shape[1] :, :], preferred_element_type=F32)
    keep_right[...] = part + ahead[:half]
    part = jnp.dot(first[...], table[: first.shape[1], :], preferred_element_type=F32)
    keep_left[...] = (part + behind[half:]) * alternating()

    for b in range(blocks):
        hop, inside = divmod(b * RB, HOP)
        if RAMH <= b <= blocks - RAMH:
            scaled = middle[:, (b - RAMH) * RB : (b - RAMH + 1) * RB]
        else:
            scaled = (raw[:, b * RB : (b + 1) * RB] * factor[:, b : b + 1]).astype(BF16)
        weight = taper[hop : hop + 1, inside : inside + RB]
        rows = slice(hop * stations, (hop + 1) * stations)
        windowed[rows, inside : inside + RB] = (scaled.astype(F32) * weight).astype(BF16)
    both = jnp.dot(windowed[...], table[...], preferred_element_type=F32)
    spectra = both[:stations] + both[stations:] * alternating()
    member = members(group[...], SUB)
    for part, white in enumerate(whiten(spectra, nearby[...], scale[...])):
        beams[part * SUB : (part + 1) * SUB, :] = jnp.dot(member, white, preferred_element_type=F32).astype(BF16)


def crossing_kernel(keep_right, keep_left, from_even, from_odd, own, group, nearby, scale, *out):
    half = keep_right.shape[0]
    held = out[-1]
    me = lax.axis_index("tchunk")
    even = me % 2 == 0
    got_even = from_even[...].astype(F32)
    got_odd = from_odd[...].astype(F32)
    ahead = keep_right[...] + jnp.where(even, got_even, got_odd)
    behind = keep_left[...] + jnp.where(even, got_odd, got_even)
    spectra = jnp.concatenate([ahead, behind], axis=0)
    station = lax.broadcasted_iota(jnp.int32, group.shape, 1)
    member = members(group[...] + jnp.where(station < half, 0, SUB), 2 * SUB)
    held[: 2 * SUB, :] = own[...]
    for part, white in enumerate(whiten(spectra, nearby[...], scale[...])):
        sums = jnp.dot(member, white, preferred_element_type=F32).astype(BF16)
        for side in range(2):
            row = (2 + 2 * side + part) * SUB
            held[row : row + SUB, :] = sums[side * SUB : (side + 1) * SUB]
    pieces = len(out) - 1
    if pieces > 1:
        width = NBIN // pieces
        for mask in range(pieces):
            start = pl.multiple_of((me ^ mask) * width, width)
            out[mask][...] = held[:, pl.ds(start, width)]
    else:
        out[0][...] = held[...]


def far_first(slabs):
    return [0, *range(slabs - 1, 0, -1)]


def combine_kernel(segments, slabs, *refs):
    pieces, (out, held) = refs[:-2], refs[-2:]
    me = lax.axis_index("tchunk")
    side = 2 * SUB
    order = far_first(slabs)
    for m in range(slabs):
        if len(pieces) == slabs:
            held[me ^ order[m]] = pieces[m][...].astype(F32)
        else:
            held[m] = pieces[0][m].astype(F32)
    for s in range(segments):
        here = held[s // 2, :side, :]
        if s % 2 == 1:
            here = held[s // 2, side : 2 * side, :] + held[s // 2 + 1, 2 * side :, :]
        out[s * side : (s + 1) * side, :] = here.astype(BF16)


def cross_terms(segments, mine, others, out):
    side = 2 * SUB
    real, imag = [], []
    for q in range(SUB):
        real_sum = jnp.zeros((SUB, mine.shape[1]), F32)
        imag_sum = jnp.zeros((SUB, mine.shape[1]), F32)
        for s in range(segments):
            first = s * side
            a, b = mine[first + q : first + q + 1, :], mine[first + SUB + q : first + SUB + q + 1, :]
            c, d = others[first : first + SUB, :], others[first + SUB : first + side, :]
            real_sum += a * c + b * d
            imag_sum += b * c - a * d
        real.append(real_sum * (1.0 / segments))
        imag.append(imag_sum * (1.0 / segments))
    half = SUB * SUB
    out[:, :half] = jnp.transpose(jnp.concatenate(real, axis=0))
    out[:, half:] = jnp.transpose(jnp.concatenate(imag, axis=0))


def near_kernel(segments, own, *refs):
    blocks, (products, mine, others) = refs[:-3], refs[-3:]
    mine[...] = own[...].astype(F32)
    products[0] = jnp.zeros(products.shape[1:], F32)
    for index, block in enumerate(blocks):
        others[...] = block[...].astype(F32)
        cross_terms(segments, mine, others, products.at[index + 1])


def last_kernel(segments, partners, own, block, products, out, mine, others, last, finished):
    home = lax.axis_index("stn")
    count = products.shape[0]
    which = []
    for slot in range(MAXP):
        partner = jnp.max(partners[0:1, slot : slot + 1])
        which.append(jnp.where(partner < 0, 0, partner ^ home))

    def copy(slot, source):
        return pltpu.make_async_copy(source, out.at[slot], finished.at[slot])

    for slot in range(MAXP):
        @pl.when(which[slot] < count)
        def _(slot=slot):
            copy(slot, products.at[jnp.minimum(which[slot], count - 1)]).start()

    mine[...] = own[...].astype(F32)
    others[...] = block[...].astype(F32)
    cross_terms(segments, mine, others, last)
    for slot in range(MAXP):
        @pl.when(which[slot] >= count)
        def _(slot=slot):
            copy(slot, last).start()

    for slot in range(MAXP):
        copy(slot, last).wait()


def cross_kernel(segments, partners, *refs):
    blocks, (out, mine, others, done, finished) = refs[:-5], refs[-5:]
    home = lax.axis_index("stn")
    mine[...] = blocks[0][...].astype(F32)
    copies = []
    for slot in range(MAXP):
        partner = partners[0:1, slot : slot + 1]
        chosen = jnp.zeros(mine.shape, F32)
        for index in range(1, len(blocks)):
            chosen = jnp.where(partner == home ^ index, blocks[index][...].astype(F32), chosen)
        others[...] = chosen
        cross_terms(segments, mine, others, done.at[slot])
        copies.append(pltpu.make_async_copy(done.at[slot], out.at[slot], finished.at[slot]))
        copies[-1].start()
    for copy in copies:
        copy.wait()


def body(raw_data, station_group, partner_blocks):
    stations, samples = raw_data.shape
    slabs = lax.axis_size("tchunk")
    count_blocks = lax.axis_size("stn")
    me, home = lax.axis_index("tchunk"), lax.axis_index("stn")
    blocks = samples // RB
    half = stations // 2
    table, taper = (jnp.asarray(t) for t in dft_tables())
    nearby, scale = (jnp.asarray(t) for t in smooth_tables())
    group = station_group[None, :]
    shape = jax.ShapeDtypeStruct

    halo = shape((blocks // 2, stations), F32)
    in_hbm = [pltpu.with_memory_space_constraint(a, pltpu.HBM) for a in (raw_data, taper, table)]
    raw, sums, even, odd, taper = call(
        sums_kernel,
        (shape(raw_data.shape, F32), shape((stations, blocks), F32), halo, halo, shape(taper.shape, F32)),
        in_hbm[:2],
        specs=[HBM, HBM],
        scratch_shapes=[pltpu.VMEM((stations, RB), F32), pltpu.SemaphoreType.DMA((4,))],
        flops=10**10,
    )
    even, odd = neighbour_swap(even, odd, True)
    sent = shape((half, 2 * NBIN), BF16)
    kept = shape((half, 2 * NBIN), F32)
    inner = (blocks - 2 * RAMH + 1) * RB
    partial = shape((stations, 2 * NBIN), F32)
    middle, ahead, behind, window = call(
        middle_kernel,
        (shape((stations, inner), BF16), partial, partial, shape((stations, blocks), F32)),
        (raw, sums, table, taper),
        scratch_shapes=[pltpu.VMEM((stations, inner), BF16)],
        flops=4 * stations * inner * NBIN,
    )
    edges = [pltpu.VMEM((half, RAMH * RB), BF16), pltpu.VMEM((half, (RAMH - 1) * RB), BF16)]
    even, odd, factor = call(
        functools.partial(send_kernel, slabs),
        (sent, sent, shape((stations, blocks), F32)),
        (raw, window, odd, even, table, taper, ahead, behind),
        scratch_shapes=edges,
        flops=2 * stations * samples * NBIN,
    )
    even, odd = neighbour_swap(even, odd, False)
    own, keep_right, keep_left = call(
        own_kernel,
        (shape((2 * SUB, NBIN), BF16), kept, kept),
        (raw, factor, middle, table, taper, ahead, behind, group, nearby, scale),
        scratch_shapes=[pltpu.VMEM((2 * stations, HOP), BF16), *edges],
        flops=6 * stations * samples * NBIN,
    )
    direct = slabs <= 8 and slabs & (slabs - 1) == 0 and NBIN // slabs % 128 == 0
    width = NBIN // slabs
    rows = 6 * SUB
    pieces = call(
        crossing_kernel,
        tuple([shape((rows, width), BF16)] * slabs) if direct else (shape((rows, NBIN), BF16),),
        (keep_right, keep_left, even, odd, own, group, nearby, scale),
        scratch_shapes=[pltpu.VMEM((rows, NBIN), BF16)],
        flops=8 * stations * NBIN * NBIN,
        limit=32,
    )
    if direct:
        order = far_first(slabs)[1:]
        received = {m: swapped(pieces[m], "tchunk", m) for m in order}
        received = [pieces[0]] + [received[m] for m in far_first(slabs)[1:]]
    else:
        received = pieces[0].reshape(rows, slabs, width).swapaxes(0, 1)
        received = [lax.all_to_all(received, "tchunk", split_axis=0, concat_axis=0, tiled=True)]
    segments = SEG_DEV * slabs - 1
    mine = call(
        functools.partial(combine_kernel, segments, slabs),
        shape((segments * 2 * SUB, width), BF16),
        received,
        scratch_shapes=[pltpu.VMEM((slabs, rows, width), F32)],
    )
    result = (MAXP, width, 2 * SUB * SUB)
    floats = [pltpu.VMEM(mine.shape, F32)] * 2
    flops = segments * width * SUB * SUB * 8
    if count_blocks == 4:
        across = swapped(mine, "stn", 2)
        beside = swapped(mine, "stn", 1)
        last = swapped(across, "stn", 1)
        products = call(
            functools.partial(near_kernel, segments),
            shape(result, F32),
            (mine, beside, across),
            scratch_shapes=floats,
            flops=2 * flops,
        )
        out = call(
            functools.partial(last_kernel, segments),
            shape(result, F32),
            (partner_blocks, mine, last, products),
            out_specs=HBM,
            scratch_shapes=floats + [pltpu.VMEM(result[1:], F32), pltpu.SemaphoreType.DMA((MAXP,))],
            flops=flops,
        )
    else:
        gathered = lax.all_gather(mine, "stn", axis=0)
        others = [lax.dynamic_index_in_dim(gathered, home ^ m, 0, keepdims=False) for m in range(count_blocks)]
        out = call(
            functools.partial(cross_kernel, segments),
            shape(result, F32),
            (partner_blocks, *others),
            out_specs=HBM,
            scratch_shapes=floats + [pltpu.VMEM(result, F32), pltpu.SemaphoreType.DMA((MAXP,))],
            flops=MAXP * flops,
            limit=32,
        )
    return out[None]


def solution(mesh):
    placed = (P("stn", ("hour", "tchunk")), P("stn"), P("stn", None))
    return jax.shard_map(
        body,
        mesh=mesh,
        in_specs=placed,
        out_specs=P(("hour", "stn"), None, "tchunk", None),
        check_vma=False,
    )
```

time: 33.8 us -> 30.3 us (0.90)
  waiting for transfers between devices: 9.88 us -> 7.26 us
  Pallas kernels: 11.3 us -> 10 us
  starting transfers between devices: 12.3 us -> 12.8 us
    ppermute x6, waiting for transfers between devices: 8.5 us -> 6.5 us  [swapped(): lax.ppermute(block, axis, [(i, i ^ mask) for i in range(lax.axis_size(axi...]
    pallas_call x6 -> x8, Pallas kernels: 11.3 us -> 10 us  [call(): pl.pallas_call(kernel, out_shape=out_shape, in_specs=specs or [VMEM] * le...]
    ppermute x4, waiting for transfers between devices: 1.38 us -> 0.75 us  [neighbour_swap(): sent[i] = lax.ppermute((first, second)[i], ('stn', 'tchunk'), pairs[i])]
    ppermute x4, starting transfers between devices: 6.31 us -> 6.75 us  [neighbour_swap(): sent[i] = lax.ppermute((first, second)[i], ('stn', 'tchunk'), pairs[i])]
  transfers between devices with their start and end apart: 10 -> 10, of which waited for: 5 -> 7; matrix products, arithmetic and copies ran while one was open for 0% -> 0% of each run, Pallas kernels for 14% -> 15%
where the time goes in v4:
time: 30.3 us; the launch traced here: 30.1 us
  starting transfers between devices  12.8 us (42%)
  Pallas kernels  10 us (33%)
  waiting for transfers between devices  7.26 us (24%)
    pallas_call x8, Pallas kernels, call(): pl.pallas_call(kernel, out_shape=out_shape, in_specs=specs or [VMEM] * le...  10 us
    ppermute x4, starting transfers between devices, neighbour_swap(): sent[i] = lax.ppermute((first, second)[i], ('stn', 'tchunk'), pairs[i])  6.75 us
    ppermute x6, waiting for transfers between devices, swapped(): lax.ppermute(block, axis, [(i, i ^ mask) for i in range(lax.axis_size(axi...  6.5 us
    ppermute x6, starting transfers between devices, swapped(): lax.ppermute(block, axis, [(i, i ^ mask) for i in range(lax.axis_size(axi...  6.01 us
    ppermute x4, waiting for transfers between devices, neighbour_swap(): sent[i] = lax.ppermute((first, second)[i], ('stn', 'tchunk'), pairs[i])  0.75 us
  transfers between devices with their start and end apart: 10, of which 7 were waited for; matrix products, arithmetic and copies ran while one was open for 0% of the time, Pallas kernels for 15%

profile of v4, /device:TPU:0, one launch (start us, length us, event | category | flops | bytes accessed | tf_op | source)
XLA Modules:
  0.0 30.1 jit_solution(4250293629187774431)
XLA Ops:
  0.0 2.2 %shard_map.73 = (f32[144,4096]{1,0:T(8,128)S(1)}, f32[144,32]{1,0:T(8,128)S(1)}, f32[16,144]{1,0:T(8,128)S(1)}, f32[16,144]{1,0:T(8,128)S(1)}, f32[2,2048]{1,0:T(2,128)S(1)}) custom-call(f32[144,4096]{1,0:T(8,128)} %source.1, f32[2,2048]{1,0:T(2,128)} %constant.9.clone.taper_source), custom_call_target="tpu_custom_call" | custom-call | flops 10000000000 | bytes 4788224 | tf_op jit(solution)/shard_map/pallas_call | solution.py:72
  2.2 0.5 %collective-permute-start = (f32[16,144]{1,0:T(8,128)S(1)}, f32[16,144]{1,0:T(8,128)S(1)}, u32[]{:S(2)}, u32[]{:S(2)}) collective-permute-start(f32[16,144]{1,0:T(8,128)S(1)} %get-tuple-element.28), channel_id=1, source_target_pairs={{1,2},{2,1},{5,6},{6,5},{9,10},{10,9},{13,14},{14,13},{0,4},{3,7},... | collective-permute-start | bytes 27656 | tf_op jit(solution)/shard_map/ppermute | solution.py:61
  2.8 4.1 %collective-permute-start.1 = (f32[16,144]{1,0:T(8,128)S(1)}, f32[16,144]{1,0:T(8,128)S(1)}, u32[]{:S(2)}, u32[]{:S(2)}) collective-permute-start(f32[16,144]{1,0:T(8,128)S(1)} %get-tuple-element.29), channel_id=1, source_target_pairs={{0,1},{1,0},{2,3},{3,2},{4,5},{5,4},{6,7},{7,6},{8,9},{9,8},{10,11... | collective-permute-start | bytes 27656 | tf_op jit(solution)/shard_map/ppermute | solution.py:61
  6.9 0.0 copy-done
  6.9 1.1 %shard_map.74 = (bf16[144,1664]{1,0:T(8,128)(2,1)S(1)}, f32[144,1024]{1,0:T(8,128)S(1)}, f32[144,1024]{1,0:T(8,128)S(1)}, f32[144,32]{1,0:T(8,128)S(1)}) custom-call(f32[144,4096]{1,0:T(8,128)S(1)} %get-tuple-element.24.raw, f32[144,32]{1,0:T(8,128)S(1)} %get-tuple-element.25.sums, bf16[2048,1024]{1,0:T(8,128)(2,1)S(1)} %copy-done, ...), custom_call_target="tpu_custom_call" | custom-call | flops 490733568 | bytes 8265728 | tf_op jit(solution)/shard_map/pallas_call | solution.py:72
  8.0 0.0 collective-permute-done.from_odd
  8.0 0.6 %collective-permute-done.1.from_even = f32[16,144]{1,0:T(8,128)S(1)} collective-permute-done((f32[16,144]{1,0:T(8,128)S(1)}, f32[16,144]{1,0:T(8,128)S(1)}, u32[]{:S(2)}, u32[]{:S(2)}) %collective-permute-start.1) | collective-permute-done | bytes 9248 | tf_op jit(solution)/shard_map/ppermute | solution.py:61
  8.6 1.5 %shard_map.75 = (bf16[72,1024]{1,0:T(8,128)(2,1)S(1)}, bf16[72,1024]{1,0:T(8,128)(2,1)S(1)}, f32[144,32]{1,0:T(8,128)S(1)}) custom-call(f32[144,4096]{1,0:T(8,128)S(1)} %get-tuple-element.24.raw, f32[144,32]{1,0:T(8,128)S(1)} %get-tuple-element.27.window, f32[16,144]{1,0:T(8,128)S(1)} %collective-permute-done.from_odd, ...), custom_call_target="tpu_custom_call" | custom-call | flops 603979776 | bytes 8099840 | tf_op jit(solution)/shard_map/pallas_call | solution.py:72
  10.1 2.1 %collective-permute-start.2 = (bf16[72,1024]{1,0:T(8,128)(2,1)S(1)}, bf16[72,1024]{1,0:T(8,128)(2,1)S(1)}, u32[]{:S(2)}, u32[]{:S(2)}) collective-permute-start(bf16[72,1024]{1,0:T(8,128)(2,1)S(1)} %get-tuple-element.36), channel_id=1, source_target_pairs={{0,1},{1,0},{2,3},{3,2},{4,5},{5,4},{6,7},{7,6},{8,9},{9,8},{10,11... | collective-permute-start | bytes 442376 | tf_op jit(solution)/shard_map/ppermute | solution.py:61
  12.2 0.0 collective-permute-start.3
  12.2 0.0 copy-done.1
  12.2 0.0 copy-done.2
  12.2 0.0 copy-done.3
  12.2 2.9 %shard_map.76 = (bf16[32,512]{1,0:T(8,128)(2,1)S(1)}, f32[72,1024]{1,0:T(8,128)S(1)}, f32[72,1024]{1,0:T(8,128)S(1)}) custom-call(f32[144,4096]{1,0:T(8,128)S(1)} %get-tuple-element.24.raw, f32[144,32]{1,0:T(8,128)S(1)} %get-tuple-element.32.factor, bf16[144,1664]{1,0:T(8,128)(2,1)S(1)} %get-tuple-element.33.middle, bf16[2048,1024]{1,0:T(8,128)(2,1)S(1)} %copy-done, ...), custom_call_target="tpu_custom_call" | custom-call | flops 1811939328 | bytes 9396800 | tf_op jit(solution)/shard_map/pallas_call | solution.py:72
  15.2 0.2 collective-permute-done.2.from_even
  15.4 0.0 collective-permute-done.3.from_odd
  15.4 0.6 %shard_map.77 = (bf16[96,128]{1,0:T(8,128)(2,1)S(1)}, bf16[96,128]{1,0:T(8,128)(2,1)S(1)}, bf16[96,128]{1,0:T(8,128)(2,1)S(1)}, bf16[96,128]{1,0:T(8,128)(2,1)S(1)}) custom-call(f32[72,1024]{1,0:T(8,128)S(1)} %get-tuple-element.34.keep_right, f32[72,1024]{1,0:T(8,128)S(1)} %get-tuple-element.35.keep_left, ...), custom_call_target="tpu_custom_call" | custom-call | flops 301989888 | bytes 1542720 | tf_op jit(solution)/shard_map/pallas_call | solution.py:72
  15.9 2.6 %collective-permute-start.4 = (bf16[96,128]{1,0:T(8,128)(2,1)S(1)}, bf16[96,128]{1,0:T(8,128)(2,1)S(1)}, u32[]{:S(2)}, u32[]{:S(2)}) collective-permute-start(bf16[96,128]{1,0:T(8,128)(2,1)S(1)} %get-tuple-element.40), channel_id=1, source_target_pairs={{0,3},{1,2},{2,1},{3,0},{4,7},{5,6},{6,5},{7,4},{8,11},{9,10},{10,... | collective-permute-start | bytes 73736 | tf_op jit(solution)/shard_map/ppermute | solution.py:66
  18.6 1.0 %collective-permute-start.5 = (bf16[96,128]{1,0:T(8,128)(2,1)S(1)}, bf16[96,128]{1,0:T(8,128)(2,1)S(1)}, u32[]{:S(2)}, u32[]{:S(2)}) collective-permute-start(bf16[96,128]{1,0:T(8,128)(2,1)S(1)} %get-tuple-element.41), channel_id=1, source_target_pairs={{0,2},{1,3},{2,0},{3,1},{4,6},{5,7},{6,4},{7,5},{8,10},{9,11},{10,... | collective-permute-start | bytes 73736 | tf_op jit(solution)/shard_map/ppermute | solution.py:66
  19.6 0.8 %collective-permute-start.6 = (bf16[96,128]{1,0:T(8,128)(2,1)S(1)}, bf16[96,128]{1,0:T(8,128)(2,1)S(1)}, u32[]{:S(2)}, u32[]{:S(2)}) collective-permute-start(bf16[96,128]{1,0:T(8,128)(2,1)S(1)} %get-tuple-element.42), channel_id=1, source_target_pairs={{0,1},{1,0},{2,3},{3,2},{4,5},{5,4},{6,7},{7,6},{8,9},{9,8},{10,11... | collective-permute-start | bytes 73736 | tf_op jit(solution)/shard_map/ppermute | solution.py:66
  20.4 1.2 %collective-permute-done.4.refs_1_ = bf16[96,128]{1,0:T(8,128)(2,1)S(1)} collective-permute-done((bf16[96,128]{1,0:T(8,128)(2,1)S(1)}, bf16[96,128]{1,0:T(8,128)(2,1)S(1)}, u32[]{:S(2)}, u32[]{:S(2)}) %collective-permute-start.4) | collective-permute-done | bytes 24608 | tf_op jit(solution)/shard_map/ppermute | solution.py:66
  21.6 1.7 %collective-permute-done.5.refs_2_ = bf16[96,128]{1,0:T(8,128)(2,1)S(1)} collective-permute-done((bf16[96,128]{1,0:T(8,128)(2,1)S(1)}, bf16[96,128]{1,0:T(8,128)(2,1)S(1)}, u32[]{:S(2)}, u32[]{:S(2)}) %collective-permute-start.5) | collective-permute-done | bytes 24608 | tf_op jit(solution)/shard_map/ppermute | solution.py:66
  23.3 0.3 collective-permute-done.6.refs_3_
  23.6 1.6 %collective-permute-start.7 = (bf16[224,128]{1,0:T(8,128)(2,1)S(1)}, bf16[224,128]{1,0:T(8,128)(2,1)S(1)}, u32[]{:S(2)}, u32[]{:S(2)}) collective-permute-start(bf16[224,128]{1,0:T(8,128)(2,1)S(1)} %shard_map.78.own), channel_id=1, source_target_pairs={{0,8},{4,12},{8,0},{12,4},{1,9},{5,13},{9,1},{13,5},{2,10},{6,14},... | collective-permute-start | bytes 172040 | tf_op jit(solution)/shard_map/ppermute | solution.py:66
  25.1 0.0 collective-permute-start.9
  25.1 2.7 %collective-permute-done.7.refs_1_ = bf16[224,128]{1,0:T(8,128)(2,1)S(1)} collective-permute-done((bf16[224,128]{1,0:T(8,128)(2,1)S(1)}, bf16[224,128]{1,0:T(8,128)(2,1)S(1)}, u32[]{:S(2)}, u32[]{:S(2)}) %collective-permute-start.7) | collective-permute-done | bytes 57376 | tf_op jit(solution)/shard_map/ppermute | solution.py:66
  27.8 0.0 collective-permute-start.8
  27.8 0.0 collective-permute-done.9.refs_0_
  27.8 0.6 %shard_map.79.products = f32[3,128,512]{2,1,0:T(8,128)S(1)} custom-call(bf16[224,128]{1,0:T(8,128)(2,1)S(1)} %shard_map.78.own, bf16[224,128]{1,0:T(8,128)(2,1)S(1)} %collective-permute-done.9.refs_0_, bf16[224,128]{1,0:T(8,128)(2,1)S(1)} %collective-permute-done.7.refs_1_), custom_call_target="tpu_custom_call" | custom-call | flops 3670016 | bytes 958464 | tf_op jit(solution)/shard_map/pallas_call | solution.py:72
  28.4 0.7 %collective-permute-done.8.block = bf16[224,128]{1,0:T(8,128)(2,1)S(1)} collective-permute-done((bf16[224,128]{1,0:T(8,128)(2,1)S(1)}, bf16[224,128]{1,0:T(8,128)(2,1)S(1)}, u32[]{:S(2)}, u32[]{:S(2)}) %collective-permute-start.8) | collective-permute-done | bytes 57376 | tf_op jit(solution)/shard_map/ppermute | solution.py:66
  29.1 0.0 copy-done.4
  29.1 1.1 %shard_map.80 = f32[3,128,512]{2,1,0:T(8,128)} custom-call(s32[1,3]{1,0:T(1,128)S(1)} %copy-done.4, bf16[224,128]{1,0:T(8,128)(2,1)S(1)} %shard_map.78.own, bf16[224,128]{1,0:T(8,128)(2,1)S(1)} %collective-permute-done.8.block, f32[3,128,512]{2,1,0:T(8,128)S(1)} %shard_map.79.products), custom_call_target="tpu_custom_call" | custom-call | flops 1835008 | bytes 1687564 | tf_op jit(solution)/shard_map/pallas_call | solution.py:72
  (6 shorter events, 0.0 us)
Async XLA Ops:
  0.0 6.9 %copy-start = (bf16[2048,1024]{1,0:T(8,128)(2,1)S(1)}, bf16[2048,1024]{1,0:T(8,128)(2,1)}, u32[]{:S(2)}) copy-start(bf16[2048,1024]{1,0:T(8,128)(2,1)} %constant.8.clone.table) | copy-start | bytes 12582916
  2.2 5.8 %collective-permute-start = (f32[16,144]{1,0:T(8,128)S(1)}, f32[16,144]{1,0:T(8,128)S(1)}, u32[]{:S(2)}, u32[]{:S(2)}) collective-permute-start(f32[16,144]{1,0:T(8,128)S(1)} %get-tuple-element.28), channel_id=1, source_target_pairs={{1,2},{2,1},{5,6},{6,5},{9,10},{10,9},{13,14},{14,13},{0,4},{3,7},... | collective-permute-start | bytes 27656 | tf_op jit(solution)/shard_map/ppermute | solution.py:61
  2.8 5.9 %collective-permute-start.1 = (f32[16,144]{1,0:T(8,128)S(1)}, f32[16,144]{1,0:T(8,128)S(1)}, u32[]{:S(2)}, u32[]{:S(2)}) collective-permute-start(f32[16,144]{1,0:T(8,128)S(1)} %get-tuple-element.29), channel_id=1, source_target_pairs={{0,1},{1,0},{2,3},{3,2},{4,5},{5,4},{6,7},{7,6},{8,9},{9,8},{10,11... | collective-permute-start | bytes 27656 | tf_op jit(solution)/shard_map/ppermute | solution.py:61
  8.6 3.6 %copy-start.1 = (bf16[512,512]{1,0:T(8,128)(2,1)S(1)}, bf16[512,512]{1,0:T(8,128)(2,1)}, u32[]{:S(2)}) copy-start(bf16[512,512]{1,0:T(8,128)(2,1)} %constant.10.clone.nearby) | copy-start | bytes 1572868
  8.6 3.6 %copy-start.2 = (f32[1,512]{1,0:T(1,128)S(1)}, f32[1,512]{1,0:T(1,128)}, u32[]{:S(2)}) copy-start(f32[1,512]{1,0:T(1,128)} %constant.11.clone.scale) | copy-start | bytes 6148
  8.6 3.6 %copy-start.3 = (s32[144]{0:T(256)S(1)}, s32[144]{0:T(256)}, u32[]{:S(2)}) copy-start(s32[144]{0:T(256)} %param.8) | copy-start | bytes 1732
  10.1 5.2 %collective-permute-start.2 = (bf16[72,1024]{1,0:T(8,128)(2,1)S(1)}, bf16[72,1024]{1,0:T(8,128)(2,1)S(1)}, u32[]{:S(2)}, u32[]{:S(2)}) collective-permute-start(bf16[72,1024]{1,0:T(8,128)(2,1)S(1)} %get-tuple-element.36), channel_id=1, source_target_pairs={{0,1},{1,0},{2,3},{3,2},{4,5},{5,4},{6,7},{7,6},{8,9},{9,8},{10,11... | collective-permute-start | bytes 442376 | tf_op jit(solution)/shard_map/ppermute | solution.py:61
  12.2 3.1 %collective-permute-start.3 = (bf16[72,1024]{1,0:T(8,128)(2,1)S(1)}, bf16[72,1024]{1,0:T(8,128)(2,1)S(1)}, u32[]{:S(2)}, u32[]{:S(2)}) collective-permute-start(bf16[72,1024]{1,0:T(8,128)(2,1)S(1)} %get-tuple-element.37), channel_id=1, source_target_pairs={{1,2},{2,1},{5,6},{6,5},{9,10},{10,9},{13,14},{14,13},{0,4},{3,7},... | collective-permute-start | bytes 442376 | tf_op jit(solution)/shard_map/ppermute | solution.py:61
  15.2 13.9 %copy-start.4 = (s32[1,3]{1,0:T(1,128)S(1)}, s32[1,3]{1,0:T(1,128)}, u32[]{:S(2)}) copy-start(s32[1,3]{1,0:T(1,128)} %partners.1) | copy-start | bytes 40
  15.9 5.7 %collective-permute-start.4 = (bf16[96,128]{1,0:T(8,128)(2,1)S(1)}, bf16[96,128]{1,0:T(8,128)(2,1)S(1)}, u32[]{:S(2)}, u32[]{:S(2)}) collective-permute-start(bf16[96,128]{1,0:T(8,128)(2,1)S(1)} %get-tuple-element.40), channel_id=1, source_target_pairs={{0,3},{1,2},{2,1},{3,0},{4,7},{5,6},{6,5},{7,4},{8,11},{9,10},{10,... | collective-permute-start | bytes 73736 | tf_op jit(solution)/shard_map/ppermute | solution.py:66
  18.6 4.7 %collective-permute-start.5 = (bf16[96,128]{1,0:T(8,128)(2,1)S(1)}, bf16[96,128]{1,0:T(8,128)(2,1)S(1)}, u32[]{:S(2)}, u32[]{:S(2)}) collective-permute-start(bf16[96,128]{1,0:T(8,128)(2,1)S(1)} %get-tuple-element.41), channel_id=1, source_target_pairs={{0,2},{1,3},{2,0},{3,1},{4,6},{5,7},{6,4},{7,5},{8,10},{9,11},{10,... | collective-permute-start | bytes 73736 | tf_op jit(solution)/shard_map/ppermute | solution.py:66
  19.6 4.0 %collective-permute-start.6 = (bf16[96,128]{1,0:T(8,128)(2,1)S(1)}, bf16[96,128]{1,0:T(8,128)(2,1)S(1)}, u32[]{:S(2)}, u32[]{:S(2)}) collective-permute-start(bf16[96,128]{1,0:T(8,128)(2,1)S(1)} %get-tuple-element.42), channel_id=1, source_target_pairs={{0,1},{1,0},{2,3},{3,2},{4,5},{5,4},{6,7},{7,6},{8,9},{9,8},{10,11... | collective-permute-start | bytes 73736 | tf_op jit(solution)/shard_map/ppermute | solution.py:66
  23.6 4.2 %collective-permute-start.7 = (bf16[224,128]{1,0:T(8,128)(2,1)S(1)}, bf16[224,128]{1,0:T(8,128)(2,1)S(1)}, u32[]{:S(2)}, u32[]{:S(2)}) collective-permute-start(bf16[224,128]{1,0:T(8,128)(2,1)S(1)} %shard_map.78.own), channel_id=1, source_target_pairs={{0,8},{4,12},{8,0},{12,4},{1,9},{5,13},{9,1},{13,5},{2,10},{6,14},... | collective-permute-start | bytes 172040 | tf_op jit(solution)/shard_map/ppermute | solution.py:66
  25.1 2.7 %collective-permute-start.9 = (bf16[224,128]{1,0:T(8,128)(2,1)S(1)}, bf16[224,128]{1,0:T(8,128)(2,1)S(1)}, u32[]{:S(2)}, u32[]{:S(2)}) collective-permute-start(bf16[224,128]{1,0:T(8,128)(2,1)S(1)} %shard_map.78.own), channel_id=1, source_target_pairs={{0,4},{4,0},{8,12},{12,8},{1,5},{5,1},{9,13},{13,9},{2,6},{6,2},{1... | collective-permute-start | bytes 172040 | tf_op jit(solution)/shard_map/ppermute | solution.py:66
  27.8 1.2 %collective-permute-start.8 = (bf16[224,128]{1,0:T(8,128)(2,1)S(1)}, bf16[224,128]{1,0:T(8,128)(2,1)S(1)}, u32[]{:S(2)}, u32[]{:S(2)}) collective-permute-start(bf16[224,128]{1,0:T(8,128)(2,1)S(1)} %collective-permute-done.7.refs_1_), channel_id=1, source_target_pairs={{0,4},{4,0},{8,12},{12,8},{1,5},{5,1},{9,13},{13,9},{2,6},{6,2},{1... | collective-permute-start | bytes 172040 | tf_op jit(solution)/shard_map/ppermute | solution.py:66

commit v5 on v4

--- a/solution.py
+++ b/solution.py
@@ -37,8 +37,10 @@
     phases = sample[:, None] * frequency[None, :] % SEGLEN
     matrix = np.concatenate([np.cos(turn)[phases], -np.sin(turn)[phases]], axis=1)
     taper = (0.5 - 0.5 * np.cos(turn)).reshape(2, HOP)
+    repeated = np.concatenate([matrix, matrix * np.concatenate([(-1.0) ** frequency] * 2)], axis=0)
+    tapered = (taper.reshape(-1, 1) * repeated).astype(np.float32).astype(ml_dtypes.bfloat16)
     matrix = matrix.astype(np.float32).astype(ml_dtypes.bfloat16)
-    return matrix, taper.astype(np.float32)
+    return tapered, matrix, taper.astype(np.float32)
 
 
 def smooth_tables():
@@ -146,8 +148,19 @@
         windowed[:, here] = (scaled.astype(F32) * weight).astype(BF16)
 
 
-def middle_kernel(raw, sums, table, taper, normal, ahead, behind, window, windowed):
+def middle_kernel(raw, sums, table, taper, normal, ahead, behind, window, last, first, windowed, bare):
     blocks = sums.shape[1]
+    half = raw.shape[0] // 2
+    for source, rows, some, out in (
+        (raw, slice(half, None), range(blocks - RAMH + 1, blocks), last),
+        (raw, slice(0, half), range(RAMH), first),
+    ):
+        for place, b in enumerate(some):
+            hop, inside = divmod(b * RB, HOP)
+            weight = taper[1 - hop : 2 - hop, inside : inside + RB]
+            bare[place] = (source[rows, b * RB : (b + 1) * RB] * weight).astype(BF16)
+            out[place] = jnp.dot(bare[place], table[inside : inside + RB, :], preferred_element_type=F32)
+
     window[...] = split_dot(sums[...], band(blocks, blocks, 0), 1)
     factor = 1.0 / (window[...] * (1.0 / (2 * RAMH * RB)) + EPS_MEAN)
     windowed_blocks(raw, factor, taper, slice(None), range(RAMH, blocks - RAMH + 1), normal, windowed)
@@ -157,10 +170,7 @@
     behind[...] = jnp.dot(windowed[:, :split], table[HOP - split :, :], preferred_element_type=F32)
 
 
-def send_kernel(
-    slabs, raw, window, from_odd, from_even, table, taper, ahead, behind,
-    to_even, to_odd, factor, first, last,
-):
+def send_kernel(slabs, window, from_odd, from_even, ahead, behind, last, first, to_even, to_odd, factor):
     stations, blocks = window.shape
     half_blocks = from_even.shape[0]
     half = stations // 2
@@ -176,18 +186,21 @@
     block = lax.broadcasted_iota(jnp.int32, (stations, blocks), 1) + me * blocks
     counted = jnp.minimum(block + RAMH, slabs * blocks) - jnp.maximum(block - RAMH, 0)
     factor[...] = 1.0 / (total / (RB * counted.astype(F32)) + EPS_MEAN)
-    windowed_blocks(raw, factor, taper, slice(half, stations), range(blocks - RAMH + 1, blocks), None, last)
-    windowed_blocks(raw, factor, taper, slice(0, half), range(RAMH), None, first)
     sign = alternating()
-    width = NBIN // 2
+    width = NBIN
 
     def fill(to_right, to_left):
-        for n in range(table.shape[1] // width):
+        for n in range(ahead.shape[1] // width):
             here = slice(n * width, (n + 1) * width)
-            part = jnp.dot(last[...], table[HOP - last.shape[1] :, here], preferred_element_type=F32)
-            to_right[:, here] = (part + ahead[half:, here]).astype(BF16)
-            part = jnp.dot(first[...], table[: first.shape[1], here], preferred_element_type=F32)
-            to_left[:, here] = ((part + behind[:half, here]) * sign[:, here]).astype(BF16)
+            part = ahead[half:, here]
+            for place in range(RAMH - 1):
+                b = blocks - RAMH + 1 + place
+                part += factor[half:, b : b + 1] * last[place, :, here]
+            to_right[:, here] = part.astype(BF16)
+            part = behind[:half, here]
+            for b in range(RAMH):
+                part += factor[:half, b : b + 1] * first[b, :, here]
+            to_left[:, here] = (part * sign[:, here]).astype(BF16)
 
     @pl.when(even)
     def _():
@@ -216,8 +229,8 @@
 
 
 def own_kernel(
-    raw, factor, middle, table, taper, ahead, behind, group, nearby, scale,
-    beams, keep_right, keep_left, windowed, first, last,
+    raw, factor, middle, table, tapered, taper, ahead, behind, group, nearby, scale,
+    beams, keep_right, keep_left, normal, first, last,
 ):
     stations, blocks = factor.shape
     half = stations // 2
@@ -228,17 +241,11 @@
     part = jnp.dot(first[...], table[: first.shape[1], :], preferred_element_type=F32)
     keep_left[...] = (part + behind[half:]) * alternating()
 
-    for b in range(blocks):
-        hop, inside = divmod(b * RB, HOP)
-        if RAMH <= b <= blocks - RAMH:
-            scaled = middle[:, (b - RAMH) * RB : (b - RAMH + 1) * RB]
-        else:
-            scaled = (raw[:, b * RB : (b + 1) * RB] * factor[:, b : b + 1]).astype(BF16)
-        weight = taper[hop : hop + 1, inside : inside + RB]
-        rows = slice(hop * stations, (hop + 1) * stations)
-        windowed[rows, inside : inside + RB] = (scaled.astype(F32) * weight).astype(BF16)
-    both = jnp.dot(windowed[...], table[...], preferred_element_type=F32)
-    spectra = both[:stations] + both[stations:] * alternating()
+    for b in [*range(RAMH), *range(blocks - RAMH + 1, blocks)]:
+        here = pl.ds(b * RB, RB)
+        normal[:, here] = (raw[:, here] * factor[:, b : b + 1]).astype(BF16)
+    normal[:, RAMH * RB : RAMH * RB + middle.shape[1]] = middle[...]
+    spectra = jnp.dot(normal[...], tapered[...], preferred_element_type=F32)
     member = members(group[...], SUB)
     for part, white in enumerate(whiten(spectra, nearby[...], scale[...])):
         beams[part * SUB : (part + 1) * SUB, :] = jnp.dot(member, white, preferred_element_type=F32).astype(BF16)
@@ -374,7 +381,7 @@
     me, home = lax.axis_index("tchunk"), lax.axis_index("stn")
     blocks = samples // RB
     half = stations // 2
-    table, taper = (jnp.asarray(t) for t in dft_tables())
+    tapered, table, taper = (jnp.asarray(t) for t in dft_tables())
     nearby, scale = (jnp.asarray(t) for t in smooth_tables())
     group = station_group[None, :]
     shape = jax.ShapeDtypeStruct
@@ -394,27 +401,30 @@
     kept = shape((half, 2 * NBIN), F32)
     inner = (blocks - 2 * RAMH + 1) * RB
     partial = shape((stations, 2 * NBIN), F32)
-    middle, ahead, behind, window = call(
+    edges = [shape((RAMH - 1, half, 2 * NBIN), F32), shape((RAMH, half, 2 * NBIN), F32)]
+    middle, ahead, behind, window, last, first = call(
         middle_kernel,
-        (shape((stations, inner), BF16), partial, partial, shape((stations, blocks), F32)),
+        (shape((stations, inner), BF16), partial, partial, shape((stations, blocks), F32), *edges),
         (raw, sums, table, taper),
-        scratch_shapes=[pltpu.VMEM((stations, inner), BF16)],
+        scratch_shapes=[pltpu.VMEM((stations, inner), BF16), pltpu.VMEM((RAMH, half, RB), BF16)],
         flops=4 * stations * inner * NBIN,
     )
-    edges = [pltpu.VMEM((half, RAMH * RB), BF16), pltpu.VMEM((half, (RAMH - 1) * RB), BF16)]
     even, odd, factor = call(
         functools.partial(send_kernel, slabs),
         (sent, sent, shape((stations, blocks), F32)),
-        (raw, window, odd, even, table, taper, ahead, behind),
-        scratch_shapes=edges,
-        flops=2 * stations * samples * NBIN,
+        (window, odd, even, ahead, behind, last, first),
+        flops=4 * stations * RAMH * NBIN,
     )
     even, odd = neighbour_swap(even, odd, False)
     own, keep_right, keep_left = call(
         own_kernel,
         (shape((2 * SUB, NBIN), BF16), kept, kept),
-        (raw, factor, middle, table, taper, ahead, behind, group, nearby, scale),
-        scratch_shapes=[pltpu.VMEM((2 * stations, HOP), BF16), *edges],
+        (raw, factor, middle, table, tapered, taper, ahead, behind, group, nearby, scale),
+        scratch_shapes=[
+            pltpu.VMEM((stations, samples), BF16),
+            pltpu.VMEM((half, RAMH * RB), BF16),
+            pltpu.VMEM((half, (RAMH - 1) * RB), BF16),
+        ],
         flops=6 * stations * samples * NBIN,
     )
     direct = slabs <= 8 and slabs & (slabs - 1) == 0 and NBIN // slabs % 128 == 0

time: 30.3 us -> 29.6 us (0.977)
  waiting for transfers between devices: 7.26 us -> 6.74 us
  transfers between devices with their start and end apart: 10 -> 10, of which waited for: 7 -> 6; matrix products, arithmetic and copies ran while one was open for 0% -> 0% of each run, Pallas kernels for 15% -> 18%
where the time goes in v5:
time: 29.6 us; the launch traced here: 29.5 us
  starting transfers between devices  12.5 us (42%)
  Pallas kernels  10.1 us (34%)
  waiting for transfers between devices  6.74 us (23%)
    pallas_call x8, Pallas kernels, call(): pl.pallas_call(kernel, out_shape=out_shape, in_specs=specs or [VMEM] * le...  10.1 us
    ppermute x4, starting transfers between devices, neighbour_swap(): sent[i] = lax.ppermute((first, second)[i], ('stn', 'tchunk'), pairs[i])  6.52 us
    ppermute x6, waiting for transfers between devices, swapped(): lax.ppermute(block, axis, [(i, i ^ mask) for i in range(lax.axis_size(axi...  6.28 us
    ppermute x6, starting transfers between devices, swapped(): lax.ppermute(block, axis, [(i, i ^ mask) for i in range(lax.axis_size(axi...  6.01 us
  transfers between devices with their start and end apart: 10, of which 6 were waited for; matrix products, arithmetic and copies ran while one was open for 0% of the time, Pallas kernels for 18%

profile of v5, /device:TPU:0, one launch (start us, length us, event | category | flops | bytes accessed | tf_op | source)
XLA Modules:
  0.0 29.5 jit_solution(2145576793126330548)
XLA Ops:
  0.0 2.2 %shard_map.82 = (f32[144,4096]{1,0:T(8,128)S(1)}, f32[144,32]{1,0:T(8,128)S(1)}, f32[16,144]{1,0:T(8,128)S(1)}, f32[16,144]{1,0:T(8,128)S(1)}, f32[2,2048]{1,0:T(2,128)S(1)}) custom-call(f32[144,4096]{1,0:T(8,128)} %source.1, f32[2,2048]{1,0:T(2,128)} %constant.12.clone.taper_source), custom_call_target="tpu_custom_call" | custom-call | flops 10000000000 | bytes 4788224 | tf_op jit(solution)/shard_map/pallas_call | solution.py:74
  2.2 0.5 %collective-permute-start = (f32[16,144]{1,0:T(8,128)S(1)}, f32[16,144]{1,0:T(8,128)S(1)}, u32[]{:S(2)}, u32[]{:S(2)}) collective-permute-start(f32[16,144]{1,0:T(8,128)S(1)} %get-tuple-element.30), channel_id=1, source_target_pairs={{1,2},{2,1},{5,6},{6,5},{9,10},{10,9},{13,14},{14,13},{0,4},{3,7},... | collective-permute-start | bytes 27656 | tf_op jit(solution)/shard_map/ppermute | solution.py:63
  2.8 4.1 %collective-permute-start.1 = (f32[16,144]{1,0:T(8,128)S(1)}, f32[16,144]{1,0:T(8,128)S(1)}, u32[]{:S(2)}, u32[]{:S(2)}) collective-permute-start(f32[16,144]{1,0:T(8,128)S(1)} %get-tuple-element.31), channel_id=1, source_target_pairs={{0,1},{1,0},{2,3},{3,2},{4,5},{5,4},{6,7},{7,6},{8,9},{9,8},{10,11... | collective-permute-start | bytes 27656 | tf_op jit(solution)/shard_map/ppermute | solution.py:63
  6.9 0.0 copy-done
  6.9 1.9 %shard_map.83 = (bf16[144,1664]{1,0:T(8,128)(2,1)S(1)}, f32[144,1024]{1,0:T(8,128)S(1)}, f32[144,1024]{1,0:T(8,128)S(1)}, f32[144,32]{1,0:T(8,128)S(1)}, f32[9,7...) custom-call(f32[144,4096]{1,0:T(8,128)S(1)} %get-tuple-element.26.raw, f32[144,32]{1,0:T(8,128)S(1)} %get-tuple-element.27.sums, ...), custom_call_target="tpu_custom_call" | custom-call | flops 490733568 | bytes 13869056 | tf_op jit(solution)/shard_map/pallas_call | solution.py:74
  8.8 0.0 collective-permute-done.from_odd
  8.8 0.0 collective-permute-done.1.from_even
  8.8 0.0 copy-start.2
  8.8 0.0 copy-start.3
  8.9 0.0 copy-start.4
  8.9 0.8 %shard_map.84 = (bf16[72,1024]{1,0:T(8,128)(2,1)S(1)}, bf16[72,1024]{1,0:T(8,128)(2,1)S(1)}, f32[144,32]{1,0:T(8,128)S(1)}) custom-call(f32[144,32]{1,0:T(8,128)S(1)} %get-tuple-element.29.window, f32[16,144]{1,0:T(8,128)S(1)} %collective-permute-done.from_odd, f32[16,144]{1,0:T(8,128)S(1)} %collective-permute-done.1.from_even, ...), custom_call_target="tpu_custom_call" | custom-call | flops 2949120 | bytes 7133184 | tf_op jit(solution)/shard_map/pallas_call | solution.py:74
  9.7 1.8 %collective-permute-start.2 = (bf16[72,1024]{1,0:T(8,128)(2,1)S(1)}, bf16[72,1024]{1,0:T(8,128)(2,1)S(1)}, u32[]{:S(2)}, u32[]{:S(2)}) collective-permute-start(bf16[72,1024]{1,0:T(8,128)(2,1)S(1)} %get-tuple-element.40), channel_id=1, source_target_pairs={{0,1},{1,0},{2,3},{3,2},{4,5},{5,4},{6,7},{7,6},{8,9},{9,8},{10,11... | collective-permute-start | bytes 442376 | tf_op jit(solution)/shard_map/ppermute | solution.py:63
  11.6 0.0 collective-permute-start.3
  11.6 0.0 copy-start.5
  11.6 2.9 %shard_map.85 = (bf16[32,512]{1,0:T(8,128)(2,1)S(1)}, f32[72,1024]{1,0:T(8,128)S(1)}, f32[72,1024]{1,0:T(8,128)S(1)}) custom-call(f32[144,4096]{1,0:T(8,128)S(1)} %get-tuple-element.26.raw, f32[144,32]{1,0:T(8,128)S(1)} %get-tuple-element.36.factor, bf16[144,1664]{1,0:T(8,128)(2,1)S(1)} %get-tuple-element.37.middle, bf16[2048,1024]{1,0:T(8,128)(2,1)S(1)} %copy-done, ...), custom_call_target="tpu_custom_call" | custom-call | flops 1811939328 | bytes 17785408 | tf_op jit(solution)/shard_map/pallas_call | solution.py:74
  14.5 0.5 %collective-permute-done.2.from_even = bf16[72,1024]{1,0:T(8,128)(2,1)S(1)} collective-permute-done((bf16[72,1024]{1,0:T(8,128)(2,1)S(1)}, bf16[72,1024]{1,0:T(8,128)(2,1)S(1)}, u32[]{:S(2)}, u32[]{:S(2)}) %collective-permute-start.2) | collective-permute-done | bytes 147488 | tf_op jit(solution)/shard_map/ppermute | solution.py:63
  14.9 0.0 collective-permute-done.3.from_odd
  14.9 0.6 %shard_map.86 = (bf16[96,128]{1,0:T(8,128)(2,1)S(1)}, bf16[96,128]{1,0:T(8,128)(2,1)S(1)}, bf16[96,128]{1,0:T(8,128)(2,1)S(1)}, bf16[96,128]{1,0:T(8,128)(2,1)S(1)}) custom-call(f32[72,1024]{1,0:T(8,128)S(1)} %get-tuple-element.38.keep_right, f32[72,1024]{1,0:T(8,128)S(1)} %get-tuple-element.39.keep_left, ...), custom_call_target="tpu_custom_call" | custom-call | flops 301989888 | bytes 1542720 | tf_op jit(solution)/shard_map/pallas_call | solution.py:74
  15.5 2.4 %collective-permute-start.4 = (bf16[96,128]{1,0:T(8,128)(2,1)S(1)}, bf16[96,128]{1,0:T(8,128)(2,1)S(1)}, u32[]{:S(2)}, u32[]{:S(2)}) collective-permute-start(bf16[96,128]{1,0:T(8,128)(2,1)S(1)} %get-tuple-element.44), channel_id=1, source_target_pairs={{0,3},{1,2},{2,1},{3,0},{4,7},{5,6},{6,5},{7,4},{8,11},{9,10},{10,... | collective-permute-start | bytes 73736 | tf_op jit(solution)/shard_map/ppermute | solution.py:68
  17.9 1.2 %collective-permute-start.5 = (bf16[96,128]{1,0:T(8,128)(2,1)S(1)}, bf16[96,128]{1,0:T(8,128)(2,1)S(1)}, u32[]{:S(2)}, u32[]{:S(2)}) collective-permute-start(bf16[96,128]{1,0:T(8,128)(2,1)S(1)} %get-tuple-element.45), channel_id=1, source_target_pairs={{0,2},{1,3},{2,0},{3,1},{4,6},{5,7},{6,4},{7,5},{8,10},{9,11},{10,... | collective-permute-start | bytes 73736 | tf_op jit(solution)/shard_map/ppermute | solution.py:68
  19.1 0.9 %collective-permute-start.6 = (bf16[96,128]{1,0:T(8,128)(2,1)S(1)}, bf16[96,128]{1,0:T(8,128)(2,1)S(1)}, u32[]{:S(2)}, u32[]{:S(2)}) collective-permute-start(bf16[96,128]{1,0:T(8,128)(2,1)S(1)} %get-tuple-element.46), channel_id=1, source_target_pairs={{0,1},{1,0},{2,3},{3,2},{4,5},{5,4},{6,7},{7,6},{8,9},{9,8},{10,11... | collective-permute-start | bytes 73736 | tf_op jit(solution)/shard_map/ppermute | solution.py:68
  20.0 1.2 %collective-permute-done.4.refs_1_ = bf16[96,128]{1,0:T(8,128)(2,1)S(1)} collective-permute-done((bf16[96,128]{1,0:T(8,128)(2,1)S(1)}, bf16[96,128]{1,0:T(8,128)(2,1)S(1)}, u32[]{:S(2)}, u32[]{:S(2)}) %collective-permute-start.4) | collective-permute-done | bytes 24608 | tf_op jit(solution)/shard_map/ppermute | solution.py:68
  21.2 1.4 %collective-permute-done.5.refs_2_ = bf16[96,128]{1,0:T(8,128)(2,1)S(1)} collective-permute-done((bf16[96,128]{1,0:T(8,128)(2,1)S(1)}, bf16[96,128]{1,0:T(8,128)(2,1)S(1)}, u32[]{:S(2)}, u32[]{:S(2)}) %collective-permute-start.5) | collective-permute-done | bytes 24608 | tf_op jit(solution)/shard_map/ppermute | solution.py:68
  22.6 0.3 collective-permute-done.6.refs_3_
  22.9 1.6 %collective-permute-start.7 = (bf16[224,128]{1,0:T(8,128)(2,1)S(1)}, bf16[224,128]{1,0:T(8,128)(2,1)S(1)}, u32[]{:S(2)}, u32[]{:S(2)}) collective-permute-start(bf16[224,128]{1,0:T(8,128)(2,1)S(1)} %shard_map.87.own), channel_id=1, source_target_pairs={{0,8},{4,12},{8,0},{12,4},{1,9},{5,13},{9,1},{13,5},{2,10},{6,14},... | collective-permute-start | bytes 172040 | tf_op jit(solution)/shard_map/ppermute | solution.py:68
  24.5 0.0 collective-permute-start.9
  24.5 2.7 %collective-permute-done.7.refs_1_ = bf16[224,128]{1,0:T(8,128)(2,1)S(1)} collective-permute-done((bf16[224,128]{1,0:T(8,128)(2,1)S(1)}, bf16[224,128]{1,0:T(8,128)(2,1)S(1)}, u32[]{:S(2)}, u32[]{:S(2)}) %collective-permute-start.7) | collective-permute-done | bytes 57376 | tf_op jit(solution)/shard_map/ppermute | solution.py:68
  27.2 0.0 collective-permute-start.8
  27.2 0.0 collective-permute-done.9.refs_0_
  27.2 0.6 %shard_map.88.products = f32[3,128,512]{2,1,0:T(8,128)S(1)} custom-call(bf16[224,128]{1,0:T(8,128)(2,1)S(1)} %shard_map.87.own, bf16[224,128]{1,0:T(8,128)(2,1)S(1)} %collective-permute-done.9.refs_0_, bf16[224,128]{1,0:T(8,128)(2,1)S(1)} %collective-permute-done.7.refs_1_), custom_call_target="tpu_custom_call" | custom-call | flops 3670016 | bytes 958464 | tf_op jit(solution)/shard_map/pallas_call | solution.py:74
  27.7 0.7 %collective-permute-done.8.block = bf16[224,128]{1,0:T(8,128)(2,1)S(1)} collective-permute-done((bf16[224,128]{1,0:T(8,128)(2,1)S(1)}, bf16[224,128]{1,0:T(8,128)(2,1)S(1)}, u32[]{:S(2)}, u32[]{:S(2)}) %collective-permute-start.8) | collective-permute-done | bytes 57376 | tf_op jit(solution)/shard_map/ppermute | solution.py:68
  28.4 1.1 %shard_map.89 = f32[3,128,512]{2,1,0:T(8,128)} custom-call(s32[1,3]{1,0:T(1,128)S(1)} %copy-done.5, bf16[224,128]{1,0:T(8,128)(2,1)S(1)} %shard_map.87.own, bf16[224,128]{1,0:T(8,128)(2,1)S(1)} %collective-permute-done.8.block, f32[3,128,512]{2,1,0:T(8,128)S(1)} %shard_map.88.products), custom_call_target="tpu_custom_call" | custom-call | flops 1835008 | bytes 1687564 | tf_op jit(solution)/shard_map/pallas_call | solution.py:74
  (8 shorter events, 0.0 us)
Async XLA Ops:
  0.0 6.9 %copy-start = (bf16[2048,1024]{1,0:T(8,128)(2,1)S(1)}, bf16[2048,1024]{1,0:T(8,128)(2,1)}, u32[]{:S(2)}) copy-start(bf16[2048,1024]{1,0:T(8,128)(2,1)} %constant.11.clone.table) | copy-start | bytes 12582916
  2.2 6.6 %collective-permute-start = (f32[16,144]{1,0:T(8,128)S(1)}, f32[16,144]{1,0:T(8,128)S(1)}, u32[]{:S(2)}, u32[]{:S(2)}) collective-permute-start(f32[16,144]{1,0:T(8,128)S(1)} %get-tuple-element.30), channel_id=1, source_target_pairs={{1,2},{2,1},{5,6},{6,5},{9,10},{10,9},{13,14},{14,13},{0,4},{3,7},... | collective-permute-start | bytes 27656 | tf_op jit(solution)/shard_map/ppermute | solution.py:63
  2.8 6.1 %collective-permute-start.1 = (f32[16,144]{1,0:T(8,128)S(1)}, f32[16,144]{1,0:T(8,128)S(1)}, u32[]{:S(2)}, u32[]{:S(2)}) collective-permute-start(f32[16,144]{1,0:T(8,128)S(1)} %get-tuple-element.31), channel_id=1, source_target_pairs={{0,1},{1,0},{2,3},{3,2},{4,5},{5,4},{6,7},{7,6},{8,9},{9,8},{10,11... | collective-permute-start | bytes 27656 | tf_op jit(solution)/shard_map/ppermute | solution.py:63
  6.9 4.7 %copy-start.1 = (bf16[4096,1024]{1,0:T(8,128)(2,1)S(1)}, bf16[4096,1024]{1,0:T(8,128)(2,1)}, u32[]{:S(2)}) copy-start(bf16[4096,1024]{1,0:T(8,128)(2,1)} %constant.10.clone.tapered) | copy-start | bytes 25165828
  8.8 2.7 %copy-start.2 = (bf16[512,512]{1,0:T(8,128)(2,1)S(1)}, bf16[512,512]{1,0:T(8,128)(2,1)}, u32[]{:S(2)}) copy-start(bf16[512,512]{1,0:T(8,128)(2,1)} %constant.13.clone.nearby) | copy-start | bytes 1572868
  8.8 2.7 %copy-start.3 = (f32[1,512]{1,0:T(1,128)S(1)}, f32[1,512]{1,0:T(1,128)}, u32[]{:S(2)}) copy-start(f32[1,512]{1,0:T(1,128)} %constant.14.clone.scale) | copy-start | bytes 6148
  8.9 2.7 %copy-start.4 = (s32[144]{0:T(256)S(1)}, s32[144]{0:T(256)}, u32[]{:S(2)}) copy-start(s32[144]{0:T(256)} %param.9) | copy-start | bytes 1732
  9.7 5.2 %collective-permute-start.2 = (bf16[72,1024]{1,0:T(8,128)(2,1)S(1)}, bf16[72,1024]{1,0:T(8,128)(2,1)S(1)}, u32[]{:S(2)}, u32[]{:S(2)}) collective-permute-start(bf16[72,1024]{1,0:T(8,128)(2,1)S(1)} %get-tuple-element.40), channel_id=1, source_target_pairs={{0,1},{1,0},{2,3},{3,2},{4,5},{5,4},{6,7},{7,6},{8,9},{9,8},{10,11... | collective-permute-start | bytes 442376 | tf_op jit(solution)/shard_map/ppermute | solution.py:63
  11.6 3.4 %collective-permute-start.3 = (bf16[72,1024]{1,0:T(8,128)(2,1)S(1)}, bf16[72,1024]{1,0:T(8,128)(2,1)S(1)}, u32[]{:S(2)}, u32[]{:S(2)}) collective-permute-start(bf16[72,1024]{1,0:T(8,128)(2,1)S(1)} %get-tuple-element.41), channel_id=1, source_target_pairs={{1,2},{2,1},{5,6},{6,5},{9,10},{10,9},{13,14},{14,13},{0,4},{3,7},... | collective-permute-start | bytes 442376 | tf_op jit(solution)/shard_map/ppermute | solution.py:63
  11.6 16.8 %copy-start.5 = (s32[1,3]{1,0:T(1,128)S(1)}, s32[1,3]{1,0:T(1,128)}, u32[]{:S(2)}) copy-start(s32[1,3]{1,0:T(1,128)} %partners.1) | copy-start | bytes 40
  15.5 5.7 %collective-permute-start.4 = (bf16[96,128]{1,0:T(8,128)(2,1)S(1)}, bf16[96,128]{1,0:T(8,128)(2,1)S(1)}, u32[]{:S(2)}, u32[]{:S(2)}) collective-permute-start(bf16[96,128]{1,0:T(8,128)(2,1)S(1)} %get-tuple-element.44), channel_id=1, source_target_pairs={{0,3},{1,2},{2,1},{3,0},{4,7},{5,6},{6,5},{7,4},{8,11},{9,10},{10,... | collective-permute-start | bytes 73736 | tf_op jit(solution)/shard_map/ppermute | solution.py:68
  17.9 4.7 %collective-permute-start.5 = (bf16[96,128]{1,0:T(8,128)(2,1)S(1)}, bf16[96,128]{1,0:T(8,128)(2,1)S(1)}, u32[]{:S(2)}, u32[]{:S(2)}) collective-permute-start(bf16[96,128]{1,0:T(8,128)(2,1)S(1)} %get-tuple-element.45), channel_id=1, source_target_pairs={{0,2},{1,3},{2,0},{3,1},{4,6},{5,7},{6,4},{7,5},{8,10},{9,11},{10,... | collective-permute-start | bytes 73736 | tf_op jit(solution)/shard_map/ppermute | solution.py:68
  19.1 3.8 %collective-permute-start.6 = (bf16[96,128]{1,0:T(8,128)(2,1)S(1)}, bf16[96,128]{1,0:T(8,128)(2,1)S(1)}, u32[]{:S(2)}, u32[]{:S(2)}) collective-permute-start(bf16[96,128]{1,0:T(8,128)(2,1)S(1)} %get-tuple-element.46), channel_id=1, source_target_pairs={{0,1},{1,0},{2,3},{3,2},{4,5},{5,4},{6,7},{7,6},{8,9},{9,8},{10,11... | collective-permute-start | bytes 73736 | tf_op jit(solution)/shard_map/ppermute | solution.py:68
  22.9 4.2 %collective-permute-start.7 = (bf16[224,128]{1,0:T(8,128)(2,1)S(1)}, bf16[224,128]{1,0:T(8,128)(2,1)S(1)}, u32[]{:S(2)}, u32[]{:S(2)}) collective-permute-start(bf16[224,128]{1,0:T(8,128)(2,1)S(1)} %shard_map.87.own), channel_id=1, source_target_pairs={{0,8},{4,12},{8,0},{12,4},{1,9},{5,13},{9,1},{13,5},{2,10},{6,14},... | collective-permute-start | bytes 172040 | tf_op jit(solution)/shard_map/ppermute | solution.py:68
  24.5 2.7 %collective-permute-start.9 = (bf16[224,128]{1,0:T(8,128)(2,1)S(1)}, bf16[224,128]{1,0:T(8,128)(2,1)S(1)}, u32[]{:S(2)}, u32[]{:S(2)}) collective-permute-start(bf16[224,128]{1,0:T(8,128)(2,1)S(1)} %shard_map.87.own), channel_id=1, source_target_pairs={{0,4},{4,0},{8,12},{12,8},{1,5},{5,1},{9,13},{13,9},{2,6},{6,2},{1... | collective-permute-start | bytes 172040 | tf_op jit(solution)/shard_map/ppermute | solution.py:68
  27.2 1.2 %collective-permute-start.8 = (bf16[224,128]{1,0:T(8,128)(2,1)S(1)}, bf16[224,128]{1,0:T(8,128)(2,1)S(1)}, u32[]{:S(2)}, u32[]{:S(2)}) collective-permute-start(bf16[224,128]{1,0:T(8,128)(2,1)S(1)} %collective-permute-done.7.refs_1_), channel_id=1, source_target_pairs={{0,4},{4,0},{8,12},{12,8},{1,5},{5,1},{9,13},{13,9},{2,6},{6,2},{1... | collective-permute-start | bytes 172040 | tf_op jit(solution)/shard_map/ppermute | solution.py:68

commit v6 on v5

--- a/solution.py
+++ b/solution.py
@@ -187,20 +187,21 @@
     counted = jnp.minimum(block + RAMH, slabs * blocks) - jnp.maximum(block - RAMH, 0)
     factor[...] = 1.0 / (total / (RB * counted.astype(F32)) + EPS_MEAN)
     sign = alternating()
-    width = NBIN
+
+    def weighted(base, products, start, first):
+        sums = []
+        for row in range(0, half, 8):
+            here = slice(start + row, start + row + 8)
+            total = base[here, :]
+            for place in range(products.shape[0]):
+                b = first + place
+                total += factor[here, b : b + 1] * products[place, row : row + 8, :]
+            sums.append(total)
+        return jnp.concatenate(sums, axis=0)
 
     def fill(to_right, to_left):
-        for n in range(ahead.shape[1] // width):
-            here = slice(n * width, (n + 1) * width)
-            part = ahead[half:, here]
-            for place in range(RAMH - 1):
-                b = blocks - RAMH + 1 + place
-                part += factor[half:, b : b + 1] * last[place, :, here]
-            to_right[:, here] = part.astype(BF16)
-            part = behind[:half, here]
-            for b in range(RAMH):
-                part += factor[:half, b : b + 1] * first[b, :, here]
-            to_left[:, here] = (part * sign[:, here]).astype(BF16)
+        to_right[...] = weighted(ahead, last, half, blocks - RAMH + 1).astype(BF16)
+        to_left[...] = (weighted(behind, first, 0, 0) * sign).astype(BF16)
 
     @pl.when(even)
     def _():
@@ -212,12 +213,14 @@
 
 
 def whiten(spectra, nearby, scale):
+    rows = spectra.shape[0]
     real_part = spectra[:, :NBIN]
     imag_part = spectra[:, NBIN:]
     powers = real_part * real_part + imag_part * imag_part
     high = powers.astype(BF16)
     low = (powers - high.astype(F32)).astype(BF16)
-    smooth = jnp.dot(high, nearby, preferred_element_type=F32) + jnp.dot(low, nearby, preferred_element_type=F32)
+    both = jnp.dot(jnp.concatenate([high, low], axis=0), nearby, preferred_element_type=F32)
+    smooth = both[:rows] + both[rows:]
     floor_level = jnp.sum(powers, axis=1, keepdims=True) * (1.0 / NBIN) + 1e-06
     inverse = lax.rsqrt(smooth * scale + LEVEL * floor_level)
     return (real_part * inverse).astype(BF16), (imag_part * inverse).astype(BF16)
@@ -256,10 +259,9 @@
     held = out[-1]
     me = lax.axis_index("tchunk")
     even = me % 2 == 0
-    got_even = from_even[...].astype(F32)
-    got_odd = from_odd[...].astype(F32)
-    ahead = keep_right[...] + jnp.where(even, got_even, got_odd)
-    behind = keep_left[...] + jnp.where(even, got_odd, got_even)
+    got_even, got_odd = from_even[...], from_odd[...]
+    ahead = keep_right[...] + jnp.where(even, got_even, got_odd).astype(F32)
+    behind = keep_left[...] + jnp.where(even, got_odd, got_even).astype(F32)
     spectra = jnp.concatenate([ahead, behind], axis=0)
     station = lax.broadcasted_iota(jnp.int32, group.shape, 1)
     member = members(group[...] + jnp.where(station < half, 0, SUB), 2 * SUB)

time: 29.6 us -> 29.5 us (level)
  no operation moved by 1% of the time
where the time goes in v6:
time: 29.5 us; the launch traced here: 29.4 us
  starting transfers between devices  12.5 us (42%)
  Pallas kernels  9.94 us (34%)
  waiting for transfers between devices  6.75 us (23%)
    pallas_call x8, Pallas kernels, call(): pl.pallas_call(kernel, out_shape=out_shape, in_specs=specs or [VMEM] * le...  9.94 us
    ppermute x4, starting transfers between devices, neighbour_swap(): sent[i] = lax.ppermute((first, second)[i], ('stn', 'tchunk'), pairs[i])  6.51 us
    ppermute x6, waiting for transfers between devices, swapped(): lax.ppermute(block, axis, [(i, i ^ mask) for i in range(lax.axis_size(axi...  6.28 us
    ppermute x6, starting transfers between devices, swapped(): lax.ppermute(block, axis, [(i, i ^ mask) for i in range(lax.axis_size(axi...  6.01 us
  transfers between devices with their start and end apart: 10, of which 6 were waited for; matrix products, arithmetic and copies ran while one was open for 0% of the time, Pallas kernels for 18%

profile of v6, /device:TPU:0, one launch (start us, length us, event | category | flops | bytes accessed | tf_op | source)
XLA Modules:
  0.0 29.4 jit_solution(4127342730487757880)
XLA Ops:
  0.0 2.2 %shard_map.82 = (f32[144,4096]{1,0:T(8,128)S(1)}, f32[144,32]{1,0:T(8,128)S(1)}, f32[16,144]{1,0:T(8,128)S(1)}, f32[16,144]{1,0:T(8,128)S(1)}, f32[2,2048]{1,0:T(2,128)S(1)}) custom-call(f32[144,4096]{1,0:T(8,128)} %source.1, f32[2,2048]{1,0:T(2,128)} %constant.12.clone.taper_source), custom_call_target="tpu_custom_call" | custom-call | flops 10000000000 | bytes 4788224 | tf_op jit(solution)/shard_map/pallas_call | solution.py:74
  2.2 0.5 %collective-permute-start = (f32[16,144]{1,0:T(8,128)S(1)}, f32[16,144]{1,0:T(8,128)S(1)}, u32[]{:S(2)}, u32[]{:S(2)}) collective-permute-start(f32[16,144]{1,0:T(8,128)S(1)} %get-tuple-element.30), channel_id=1, source_target_pairs={{1,2},{2,1},{5,6},{6,5},{9,10},{10,9},{13,14},{14,13},{0,4},{3,7},... | collective-permute-start | bytes 27656 | tf_op jit(solution)/shard_map/ppermute | solution.py:63
  2.8 4.1 %collective-permute-start.1 = (f32[16,144]{1,0:T(8,128)S(1)}, f32[16,144]{1,0:T(8,128)S(1)}, u32[]{:S(2)}, u32[]{:S(2)}) collective-permute-start(f32[16,144]{1,0:T(8,128)S(1)} %get-tuple-element.31), channel_id=1, source_target_pairs={{0,1},{1,0},{2,3},{3,2},{4,5},{5,4},{6,7},{7,6},{8,9},{9,8},{10,11... | collective-permute-start | bytes 27656 | tf_op jit(solution)/shard_map/ppermute | solution.py:63
  6.9 1.9 %shard_map.83 = (bf16[144,1664]{1,0:T(8,128)(2,1)S(1)}, f32[144,1024]{1,0:T(8,128)S(1)}, f32[144,1024]{1,0:T(8,128)S(1)}, f32[144,32]{1,0:T(8,128)S(1)}, f32[9,7...) custom-call(f32[144,4096]{1,0:T(8,128)S(1)} %get-tuple-element.26.raw, f32[144,32]{1,0:T(8,128)S(1)} %get-tuple-element.27.sums, ...), custom_call_target="tpu_custom_call" | custom-call | flops 490733568 | bytes 13869056 | tf_op jit(solution)/shard_map/pallas_call | solution.py:74
  8.8 0.0 collective-permute-done.from_odd
  8.8 0.0 collective-permute-done.1.from_even
  8.8 0.0 copy-start.2
  8.8 0.0 copy-start.3
  8.9 0.0 copy-start.4
  8.9 0.8 %shard_map.84 = (bf16[72,1024]{1,0:T(8,128)(2,1)S(1)}, bf16[72,1024]{1,0:T(8,128)(2,1)S(1)}, f32[144,32]{1,0:T(8,128)S(1)}) custom-call(f32[144,32]{1,0:T(8,128)S(1)} %get-tuple-element.29.window, f32[16,144]{1,0:T(8,128)S(1)} %collective-permute-done.from_odd, f32[16,144]{1,0:T(8,128)S(1)} %collective-permute-done.1.from_even, ...), custom_call_target="tpu_custom_call" | custom-call | flops 2949120 | bytes 7133184 | tf_op jit(solution)/shard_map/pallas_call | solution.py:74
  9.6 1.8 %collective-permute-start.2 = (bf16[72,1024]{1,0:T(8,128)(2,1)S(1)}, bf16[72,1024]{1,0:T(8,128)(2,1)S(1)}, u32[]{:S(2)}, u32[]{:S(2)}) collective-permute-start(bf16[72,1024]{1,0:T(8,128)(2,1)S(1)} %get-tuple-element.40), channel_id=1, source_target_pairs={{0,1},{1,0},{2,3},{3,2},{4,5},{5,4},{6,7},{7,6},{8,9},{9,8},{10,11... | collective-permute-start | bytes 442376 | tf_op jit(solution)/shard_map/ppermute | solution.py:63
  11.5 0.0 collective-permute-start.3
  11.5 0.0 copy-done.1
  11.5 0.0 copy-start.5
  11.5 2.9 %shard_map.85 = (bf16[32,512]{1,0:T(8,128)(2,1)S(1)}, f32[72,1024]{1,0:T(8,128)S(1)}, f32[72,1024]{1,0:T(8,128)S(1)}) custom-call(f32[144,4096]{1,0:T(8,128)S(1)} %get-tuple-element.26.raw, f32[144,32]{1,0:T(8,128)S(1)} %get-tuple-element.36.factor, bf16[144,1664]{1,0:T(8,128)(2,1)S(1)} %get-tuple-element.37.middle, bf16[2048,1024]{1,0:T(8,128)(2,1)S(1)} %copy-done, ...), custom_call_target="tpu_custom_call" | custom-call | flops 1811939328 | bytes 17785408 | tf_op jit(solution)/shard_map/pallas_call | solution.py:74
  14.4 0.5 %collective-permute-done.2.from_even = bf16[72,1024]{1,0:T(8,128)(2,1)S(1)} collective-permute-done((bf16[72,1024]{1,0:T(8,128)(2,1)S(1)}, bf16[72,1024]{1,0:T(8,128)(2,1)S(1)}, u32[]{:S(2)}, u32[]{:S(2)}) %collective-permute-start.2) | collective-permute-done | bytes 147488 | tf_op jit(solution)/shard_map/ppermute | solution.py:63
  14.8 0.0 collective-permute-done.3.from_odd
  14.8 0.5 %shard_map.86 = (bf16[96,128]{1,0:T(8,128)(2,1)S(1)}, bf16[96,128]{1,0:T(8,128)(2,1)S(1)}, bf16[96,128]{1,0:T(8,128)(2,1)S(1)}, bf16[96,128]{1,0:T(8,128)(2,1)S(1)}) custom-call(f32[72,1024]{1,0:T(8,128)S(1)} %get-tuple-element.38.keep_right, f32[72,1024]{1,0:T(8,128)S(1)} %get-tuple-element.39.keep_left, ...), custom_call_target="tpu_custom_call" | custom-call | flops 301989888 | bytes 1542720 | tf_op jit(solution)/shard_map/pallas_call | solution.py:74
  15.4 2.4 %collective-permute-start.4 = (bf16[96,128]{1,0:T(8,128)(2,1)S(1)}, bf16[96,128]{1,0:T(8,128)(2,1)S(1)}, u32[]{:S(2)}, u32[]{:S(2)}) collective-permute-start(bf16[96,128]{1,0:T(8,128)(2,1)S(1)} %get-tuple-element.44), channel_id=1, source_target_pairs={{0,3},{1,2},{2,1},{3,0},{4,7},{5,6},{6,5},{7,4},{8,11},{9,10},{10,... | collective-permute-start | bytes 73736 | tf_op jit(solution)/shard_map/ppermute | solution.py:68
  17.8 1.2 %collective-permute-start.5 = (bf16[96,128]{1,0:T(8,128)(2,1)S(1)}, bf16[96,128]{1,0:T(8,128)(2,1)S(1)}, u32[]{:S(2)}, u32[]{:S(2)}) collective-permute-start(bf16[96,128]{1,0:T(8,128)(2,1)S(1)} %get-tuple-element.45), channel_id=1, source_target_pairs={{0,2},{1,3},{2,0},{3,1},{4,6},{5,7},{6,4},{7,5},{8,10},{9,11},{10,... | collective-permute-start | bytes 73736 | tf_op jit(solution)/shard_map/ppermute | solution.py:68
  18.9 0.9 %collective-permute-start.6 = (bf16[96,128]{1,0:T(8,128)(2,1)S(1)}, bf16[96,128]{1,0:T(8,128)(2,1)S(1)}, u32[]{:S(2)}, u32[]{:S(2)}) collective-permute-start(bf16[96,128]{1,0:T(8,128)(2,1)S(1)} %get-tuple-element.46), channel_id=1, source_target_pairs={{0,1},{1,0},{2,3},{3,2},{4,5},{5,4},{6,7},{7,6},{8,9},{9,8},{10,11... | collective-permute-start | bytes 73736 | tf_op jit(solution)/shard_map/ppermute | solution.py:68
  19.8 1.2 %collective-permute-done.4.refs_1_ = bf16[96,128]{1,0:T(8,128)(2,1)S(1)} collective-permute-done((bf16[96,128]{1,0:T(8,128)(2,1)S(1)}, bf16[96,128]{1,0:T(8,128)(2,1)S(1)}, u32[]{:S(2)}, u32[]{:S(2)}) %collective-permute-start.4) | collective-permute-done | bytes 24608 | tf_op jit(solution)/shard_map/ppermute | solution.py:68
  21.1 1.4 %collective-permute-done.5.refs_2_ = bf16[96,128]{1,0:T(8,128)(2,1)S(1)} collective-permute-done((bf16[96,128]{1,0:T(8,128)(2,1)S(1)}, bf16[96,128]{1,0:T(8,128)(2,1)S(1)}, u32[]{:S(2)}, u32[]{:S(2)}) %collective-permute-start.5) | collective-permute-done | bytes 24608 | tf_op jit(solution)/shard_map/ppermute | solution.py:68
  22.5 0.3 collective-permute-done.6.refs_3_
  22.8 1.6 %collective-permute-start.7 = (bf16[224,128]{1,0:T(8,128)(2,1)S(1)}, bf16[224,128]{1,0:T(8,128)(2,1)S(1)}, u32[]{:S(2)}, u32[]{:S(2)}) collective-permute-start(bf16[224,128]{1,0:T(8,128)(2,1)S(1)} %shard_map.87.own), channel_id=1, source_target_pairs={{0,8},{4,12},{8,0},{12,4},{1,9},{5,13},{9,1},{13,5},{2,10},{6,14},... | collective-permute-start | bytes 172040 | tf_op jit(solution)/shard_map/ppermute | solution.py:68
  24.4 0.0 collective-permute-start.9
  24.4 2.7 %collective-permute-done.7.refs_1_ = bf16[224,128]{1,0:T(8,128)(2,1)S(1)} collective-permute-done((bf16[224,128]{1,0:T(8,128)(2,1)S(1)}, bf16[224,128]{1,0:T(8,128)(2,1)S(1)}, u32[]{:S(2)}, u32[]{:S(2)}) %collective-permute-start.7) | collective-permute-done | bytes 57376 | tf_op jit(solution)/shard_map/ppermute | solution.py:68
  27.0 0.0 collective-permute-start.8
  27.0 0.0 collective-permute-done.9.refs_0_
  27.0 0.6 %shard_map.88.products = f32[3,128,512]{2,1,0:T(8,128)S(1)} custom-call(bf16[224,128]{1,0:T(8,128)(2,1)S(1)} %shard_map.87.own, bf16[224,128]{1,0:T(8,128)(2,1)S(1)} %collective-permute-done.9.refs_0_, bf16[224,128]{1,0:T(8,128)(2,1)S(1)} %collective-permute-done.7.refs_1_), custom_call_target="tpu_custom_call" | custom-call | flops 3670016 | bytes 958464 | tf_op jit(solution)/shard_map/pallas_call | solution.py:74
  27.6 0.7 %collective-permute-done.8.block = bf16[224,128]{1,0:T(8,128)(2,1)S(1)} collective-permute-done((bf16[224,128]{1,0:T(8,128)(2,1)S(1)}, bf16[224,128]{1,0:T(8,128)(2,1)S(1)}, u32[]{:S(2)}, u32[]{:S(2)}) %collective-permute-start.8) | collective-permute-done | bytes 57376 | tf_op jit(solution)/shard_map/ppermute | solution.py:68
  28.3 1.1 %shard_map.89 = f32[3,128,512]{2,1,0:T(8,128)} custom-call(s32[1,3]{1,0:T(1,128)S(1)} %copy-done.5, bf16[224,128]{1,0:T(8,128)(2,1)S(1)} %shard_map.87.own, bf16[224,128]{1,0:T(8,128)(2,1)S(1)} %collective-permute-done.8.block, f32[3,128,512]{2,1,0:T(8,128)S(1)} %shard_map.88.products), custom_call_target="tpu_custom_call" | custom-call | flops 1835008 | bytes 1687564 | tf_op jit(solution)/shard_map/pallas_call | solution.py:74
  (8 shorter events, 0.0 us)
Async XLA Ops:
  0.0 6.9 %copy-start = (bf16[2048,1024]{1,0:T(8,128)(2,1)S(1)}, bf16[2048,1024]{1,0:T(8,128)(2,1)}, u32[]{:S(2)}) copy-start(bf16[2048,1024]{1,0:T(8,128)(2,1)} %constant.11.clone.table) | copy-start | bytes 12582916
  2.2 6.6 %collective-permute-start = (f32[16,144]{1,0:T(8,128)S(1)}, f32[16,144]{1,0:T(8,128)S(1)}, u32[]{:S(2)}, u32[]{:S(2)}) collective-permute-start(f32[16,144]{1,0:T(8,128)S(1)} %get-tuple-element.30), channel_id=1, source_target_pairs={{1,2},{2,1},{5,6},{6,5},{9,10},{10,9},{13,14},{14,13},{0,4},{3,7},... | collective-permute-start | bytes 27656 | tf_op jit(solution)/shard_map/ppermute | solution.py:63
  2.8 6.1 %collective-permute-start.1 = (f32[16,144]{1,0:T(8,128)S(1)}, f32[16,144]{1,0:T(8,128)S(1)}, u32[]{:S(2)}, u32[]{:S(2)}) collective-permute-start(f32[16,144]{1,0:T(8,128)S(1)} %get-tuple-element.31), channel_id=1, source_target_pairs={{0,1},{1,0},{2,3},{3,2},{4,5},{5,4},{6,7},{7,6},{8,9},{9,8},{10,11... | collective-permute-start | bytes 27656 | tf_op jit(solution)/shard_map/ppermute | solution.py:63
  6.9 4.6 %copy-start.1 = (bf16[4096,1024]{1,0:T(8,128)(2,1)S(1)}, bf16[4096,1024]{1,0:T(8,128)(2,1)}, u32[]{:S(2)}) copy-start(bf16[4096,1024]{1,0:T(8,128)(2,1)} %constant.10.clone.tapered) | copy-start | bytes 25165828
  8.8 2.7 %copy-start.2 = (bf16[512,512]{1,0:T(8,128)(2,1)S(1)}, bf16[512,512]{1,0:T(8,128)(2,1)}, u32[]{:S(2)}) copy-start(bf16[512,512]{1,0:T(8,128)(2,1)} %constant.13.clone.nearby) | copy-start | bytes 1572868
  8.8 2.7 %copy-start.3 = (f32[1,512]{1,0:T(1,128)S(1)}, f32[1,512]{1,0:T(1,128)}, u32[]{:S(2)}) copy-start(f32[1,512]{1,0:T(1,128)} %constant.14.clone.scale) | copy-start | bytes 6148
  8.9 2.7 %copy-start.4 = (s32[144]{0:T(256)S(1)}, s32[144]{0:T(256)}, u32[]{:S(2)}) copy-start(s32[144]{0:T(256)} %param.9) | copy-start | bytes 1732
  9.6 5.2 %collective-permute-start.2 = (bf16[72,1024]{1,0:T(8,128)(2,1)S(1)}, bf16[72,1024]{1,0:T(8,128)(2,1)S(1)}, u32[]{:S(2)}, u32[]{:S(2)}) collective-permute-start(bf16[72,1024]{1,0:T(8,128)(2,1)S(1)} %get-tuple-element.40), channel_id=1, source_target_pairs={{0,1},{1,0},{2,3},{3,2},{4,5},{5,4},{6,7},{7,6},{8,9},{9,8},{10,11... | collective-permute-start | bytes 442376 | tf_op jit(solution)/shard_map/ppermute | solution.py:63
  11.5 3.4 %collective-permute-start.3 = (bf16[72,1024]{1,0:T(8,128)(2,1)S(1)}, bf16[72,1024]{1,0:T(8,128)(2,1)S(1)}, u32[]{:S(2)}, u32[]{:S(2)}) collective-permute-start(bf16[72,1024]{1,0:T(8,128)(2,1)S(1)} %get-tuple-element.41), channel_id=1, source_target_pairs={{1,2},{2,1},{5,6},{6,5},{9,10},{10,9},{13,14},{14,13},{0,4},{3,7},... | collective-permute-start | bytes 442376 | tf_op jit(solution)/shard_map/ppermute | solution.py:63
  11.5 16.8 %copy-start.5 = (s32[1,3]{1,0:T(1,128)S(1)}, s32[1,3]{1,0:T(1,128)}, u32[]{:S(2)}) copy-start(s32[1,3]{1,0:T(1,128)} %partners.1) | copy-start | bytes 40
  15.4 5.7 %collective-permute-start.4 = (bf16[96,128]{1,0:T(8,128)(2,1)S(1)}, bf16[96,128]{1,0:T(8,128)(2,1)S(1)}, u32[]{:S(2)}, u32[]{:S(2)}) collective-permute-start(bf16[96,128]{1,0:T(8,128)(2,1)S(1)} %get-tuple-element.44), channel_id=1, source_target_pairs={{0,3},{1,2},{2,1},{3,0},{4,7},{5,6},{6,5},{7,4},{8,11},{9,10},{10,... | collective-permute-start | bytes 73736 | tf_op jit(solution)/shard_map/ppermute | solution.py:68
  17.8 4.7 %collective-permute-start.5 = (bf16[96,128]{1,0:T(8,128)(2,1)S(1)}, bf16[96,128]{1,0:T(8,128)(2,1)S(1)}, u32[]{:S(2)}, u32[]{:S(2)}) collective-permute-start(bf16[96,128]{1,0:T(8,128)(2,1)S(1)} %get-tuple-element.45), channel_id=1, source_target_pairs={{0,2},{1,3},{2,0},{3,1},{4,6},{5,7},{6,4},{7,5},{8,10},{9,11},{10,... | collective-permute-start | bytes 73736 | tf_op jit(solution)/shard_map/ppermute | solution.py:68
  18.9 3.8 %collective-permute-start.6 = (bf16[96,128]{1,0:T(8,128)(2,1)S(1)}, bf16[96,128]{1,0:T(8,128)(2,1)S(1)}, u32[]{:S(2)}, u32[]{:S(2)}) collective-permute-start(bf16[96,128]{1,0:T(8,128)(2,1)S(1)} %get-tuple-element.46), channel_id=1, source_target_pairs={{0,1},{1,0},{2,3},{3,2},{4,5},{5,4},{6,7},{7,6},{8,9},{9,8},{10,11... | collective-permute-start | bytes 73736 | tf_op jit(solution)/shard_map/ppermute | solution.py:68
  22.8 4.2 %collective-permute-start.7 = (bf16[224,128]{1,0:T(8,128)(2,1)S(1)}, bf16[224,128]{1,0:T(8,128)(2,1)S(1)}, u32[]{:S(2)}, u32[]{:S(2)}) collective-permute-start(bf16[224,128]{1,0:T(8,128)(2,1)S(1)} %shard_map.87.own), channel_id=1, source_target_pairs={{0,8},{4,12},{8,0},{12,4},{1,9},{5,13},{9,1},{13,5},{2,10},{6,14},... | collective-permute-start | bytes 172040 | tf_op jit(solution)/shard_map/ppermute | solution.py:68
  24.4 2.7 %collective-permute-start.9 = (bf16[224,128]{1,0:T(8,128)(2,1)S(1)}, bf16[224,128]{1,0:T(8,128)(2,1)S(1)}, u32[]{:S(2)}, u32[]{:S(2)}) collective-permute-start(bf16[224,128]{1,0:T(8,128)(2,1)S(1)} %shard_map.87.own), channel_id=1, source_target_pairs={{0,4},{4,0},{8,12},{12,8},{1,5},{5,1},{9,13},{13,9},{2,6},{6,2},{1... | collective-permute-start | bytes 172040 | tf_op jit(solution)/shard_map/ppermute | solution.py:68
  27.0 1.2 %collective-permute-start.8 = (bf16[224,128]{1,0:T(8,128)(2,1)S(1)}, bf16[224,128]{1,0:T(8,128)(2,1)S(1)}, u32[]{:S(2)}, u32[]{:S(2)}) collective-permute-start(bf16[224,128]{1,0:T(8,128)(2,1)S(1)} %collective-permute-done.7.refs_1_), channel_id=1, source_target_pairs={{0,4},{4,0},{8,12},{12,8},{1,5},{5,1},{9,13},{13,9},{2,6},{6,2},{1... | collective-permute-start | bytes 172040 | tf_op jit(solution)/shard_map/ppermute | solution.py:68

commit v7 on v6

--- a/solution.py
+++ b/solution.py
@@ -170,7 +170,7 @@
     behind[...] = jnp.dot(windowed[:, :split], table[HOP - split :, :], preferred_element_type=F32)
 
 
-def send_kernel(slabs, window, from_odd, from_even, ahead, behind, last, first, to_even, to_odd, factor):
+def send_kernel(slabs, window, from_even, from_odd, ahead, behind, last, first, to_even, to_odd, factor):
     stations, blocks = window.shape
     half_blocks = from_even.shape[0]
     half = stations // 2
@@ -414,7 +414,7 @@
     even, odd, factor = call(
         functools.partial(send_kernel, slabs),
         (sent, sent, shape((stations, blocks), F32)),
-        (window, odd, even, ahead, behind, last, first),
+        (window, even, odd, ahead, behind, last, first),
         flops=4 * stations * RAMH * NBIN,
     )
     even, odd = neighbour_swap(even, odd, False)

time: 29.5 us -> 29.4 us (level)
  no operation moved by 1% of the time
where the time goes in v7:
time: 29.4 us; the launch traced here: 29.2 us
  starting transfers between devices  12.3 us (42%)
  Pallas kernels  9.93 us (34%)
  waiting for transfers between devices  6.84 us (23%)
    pallas_call x8, Pallas kernels, call(): pl.pallas_call(kernel, out_shape=out_shape, in_specs=specs or [VMEM] * le...  9.93 us
    ppermute x6, waiting for transfers between devices, swapped(): lax.ppermute(block, axis, [(i, i ^ mask) for i in range(lax.axis_size(axi...  6.45 us
    ppermute x4, starting transfers between devices, neighbour_swap(): sent[i] = lax.ppermute((first, second)[i], ('stn', 'tchunk'), pairs[i])  6.31 us
    ppermute x6, starting transfers between devices, swapped(): lax.ppermute(block, axis, [(i, i ^ mask) for i in range(lax.axis_size(axi...  6.01 us
  transfers between devices with their start and end apart: 10, of which 6 were waited for; matrix products, arithmetic and copies ran while one was open for 0% of the time, Pallas kernels for 18%

profile of v7, /device:TPU:0, one launch (start us, length us, event | category | flops | bytes accessed | tf_op | source)
XLA Modules:
  0.0 29.2 jit_solution(853509298804649350)
XLA Ops:
  0.0 2.2 %shard_map.82 = (f32[144,4096]{1,0:T(8,128)S(1)}, f32[144,32]{1,0:T(8,128)S(1)}, f32[16,144]{1,0:T(8,128)S(1)}, f32[16,144]{1,0:T(8,128)S(1)}, f32[2,2048]{1,0:T(2,128)S(1)}) custom-call(f32[144,4096]{1,0:T(8,128)} %source.1, f32[2,2048]{1,0:T(2,128)} %constant.12.clone.taper_source), custom_call_target="tpu_custom_call" | custom-call | flops 10000000000 | bytes 4788224 | tf_op jit(solution)/shard_map/pallas_call | solution.py:74
  2.2 3.1 %collective-permute-start = (f32[16,144]{1,0:T(8,128)S(1)}, f32[16,144]{1,0:T(8,128)S(1)}, u32[]{:S(2)}, u32[]{:S(2)}) collective-permute-start(f32[16,144]{1,0:T(8,128)S(1)} %get-tuple-element.30), channel_id=1, source_target_pairs={{0,1},{1,0},{2,3},{3,2},{4,5},{5,4},{6,7},{7,6},{8,9},{9,8},{10,11... | collective-permute-start | bytes 27656 | tf_op jit(solution)/shard_map/ppermute | solution.py:63
  5.3 0.0 collective-permute-start.1
  5.3 1.9 %shard_map.83 = (bf16[144,1664]{1,0:T(8,128)(2,1)S(1)}, f32[144,1024]{1,0:T(8,128)S(1)}, f32[144,1024]{1,0:T(8,128)S(1)}, f32[144,32]{1,0:T(8,128)S(1)}, f32[9,7...) custom-call(f32[144,4096]{1,0:T(8,128)S(1)} %get-tuple-element.26.raw, f32[144,32]{1,0:T(8,128)S(1)} %get-tuple-element.27.sums, ...), custom_call_target="tpu_custom_call" | custom-call | flops 490733568 | bytes 13869056 | tf_op jit(solution)/shard_map/pallas_call | solution.py:74
  7.2 0.0 collective-permute-done.from_even
  7.2 0.0 collective-permute-done.1.from_odd
  7.3 0.0 copy-start.2
  7.3 0.0 copy-start.3
  7.3 0.0 copy-start.4
  7.3 0.8 %shard_map.84 = (bf16[72,1024]{1,0:T(8,128)(2,1)S(1)}, bf16[72,1024]{1,0:T(8,128)(2,1)S(1)}, f32[144,32]{1,0:T(8,128)S(1)}) custom-call(f32[144,32]{1,0:T(8,128)S(1)} %get-tuple-element.29.window, f32[16,144]{1,0:T(8,128)S(1)} %collective-permute-done.from_even, f32[16,144]{1,0:T(8,128)S(1)} %collective-permute-done.1.from_odd, ...), custom_call_target="tpu_custom_call" | custom-call | flops 2949120 | bytes 7133184 | tf_op jit(solution)/shard_map/pallas_call | solution.py:74
  8.1 3.2 %collective-permute-start.2 = (bf16[72,1024]{1,0:T(8,128)(2,1)S(1)}, bf16[72,1024]{1,0:T(8,128)(2,1)S(1)}, u32[]{:S(2)}, u32[]{:S(2)}) collective-permute-start(bf16[72,1024]{1,0:T(8,128)(2,1)S(1)} %get-tuple-element.40), channel_id=1, source_target_pairs={{0,1},{1,0},{2,3},{3,2},{4,5},{5,4},{6,7},{7,6},{8,9},{9,8},{10,11... | collective-permute-start | bytes 442376 | tf_op jit(solution)/shard_map/ppermute | solution.py:63
  11.3 0.0 collective-permute-start.3
  11.3 0.0 copy-done.3
  11.3 0.0 copy-start.5
  11.3 2.9 %shard_map.85 = (bf16[32,512]{1,0:T(8,128)(2,1)S(1)}, f32[72,1024]{1,0:T(8,128)S(1)}, f32[72,1024]{1,0:T(8,128)S(1)}) custom-call(f32[144,4096]{1,0:T(8,128)S(1)} %get-tuple-element.26.raw, f32[144,32]{1,0:T(8,128)S(1)} %get-tuple-element.36.factor, bf16[144,1664]{1,0:T(8,128)(2,1)S(1)} %get-tuple-element.37.middle, bf16[2048,1024]{1,0:T(8,128)(2,1)S(1)} %copy-done, ...), custom_call_target="tpu_custom_call" | custom-call | flops 1811939328 | bytes 17785408 | tf_op jit(solution)/shard_map/pallas_call | solution.py:74
  14.2 0.4 %collective-permute-done.2.from_even = bf16[72,1024]{1,0:T(8,128)(2,1)S(1)} collective-permute-done((bf16[72,1024]{1,0:T(8,128)(2,1)S(1)}, bf16[72,1024]{1,0:T(8,128)(2,1)S(1)}, u32[]{:S(2)}, u32[]{:S(2)}) %collective-permute-start.2) | collective-permute-done | bytes 147488 | tf_op jit(solution)/shard_map/ppermute | solution.py:63
  14.6 0.0 collective-permute-done.3.from_odd
  14.6 0.5 %shard_map.86 = (bf16[96,128]{1,0:T(8,128)(2,1)S(1)}, bf16[96,128]{1,0:T(8,128)(2,1)S(1)}, bf16[96,128]{1,0:T(8,128)(2,1)S(1)}, bf16[96,128]{1,0:T(8,128)(2,1)S(1)}) custom-call(f32[72,1024]{1,0:T(8,128)S(1)} %get-tuple-element.38.keep_right, f32[72,1024]{1,0:T(8,128)S(1)} %get-tuple-element.39.keep_left, ...), custom_call_target="tpu_custom_call" | custom-call | flops 301989888 | bytes 1542720 | tf_op jit(solution)/shard_map/pallas_call | solution.py:74
  15.1 2.6 %collective-permute-start.4 = (bf16[96,128]{1,0:T(8,128)(2,1)S(1)}, bf16[96,128]{1,0:T(8,128)(2,1)S(1)}, u32[]{:S(2)}, u32[]{:S(2)}) collective-permute-start(bf16[96,128]{1,0:T(8,128)(2,1)S(1)} %get-tuple-element.44), channel_id=1, source_target_pairs={{0,3},{1,2},{2,1},{3,0},{4,7},{5,6},{6,5},{7,4},{8,11},{9,10},{10,... | collective-permute-start | bytes 73736 | tf_op jit(solution)/shard_map/ppermute | solution.py:68
  17.7 0.9 %collective-permute-start.5 = (bf16[96,128]{1,0:T(8,128)(2,1)S(1)}, bf16[96,128]{1,0:T(8,128)(2,1)S(1)}, u32[]{:S(2)}, u32[]{:S(2)}) collective-permute-start(bf16[96,128]{1,0:T(8,128)(2,1)S(1)} %get-tuple-element.45), channel_id=1, source_target_pairs={{0,2},{1,3},{2,0},{3,1},{4,6},{5,7},{6,4},{7,5},{8,10},{9,11},{10,... | collective-permute-start | bytes 73736 | tf_op jit(solution)/shard_map/ppermute | solution.py:68
  18.6 1.0 %collective-permute-start.6 = (bf16[96,128]{1,0:T(8,128)(2,1)S(1)}, bf16[96,128]{1,0:T(8,128)(2,1)S(1)}, u32[]{:S(2)}, u32[]{:S(2)}) collective-permute-start(bf16[96,128]{1,0:T(8,128)(2,1)S(1)} %get-tuple-element.46), channel_id=1, source_target_pairs={{0,1},{1,0},{2,3},{3,2},{4,5},{5,4},{6,7},{7,6},{8,9},{9,8},{10,11... | collective-permute-start | bytes 73736 | tf_op jit(solution)/shard_map/ppermute | solution.py:68
  19.6 1.3 %collective-permute-done.4.refs_1_ = bf16[96,128]{1,0:T(8,128)(2,1)S(1)} collective-permute-done((bf16[96,128]{1,0:T(8,128)(2,1)S(1)}, bf16[96,128]{1,0:T(8,128)(2,1)S(1)}, u32[]{:S(2)}, u32[]{:S(2)}) %collective-permute-start.4) | collective-permute-done | bytes 24608 | tf_op jit(solution)/shard_map/ppermute | solution.py:68
  20.8 1.7 %collective-permute-done.5.refs_2_ = bf16[96,128]{1,0:T(8,128)(2,1)S(1)} collective-permute-done((bf16[96,128]{1,0:T(8,128)(2,1)S(1)}, bf16[96,128]{1,0:T(8,128)(2,1)S(1)}, u32[]{:S(2)}, u32[]{:S(2)}) %collective-permute-start.5) | collective-permute-done | bytes 24608 | tf_op jit(solution)/shard_map/ppermute | solution.py:68
  22.5 0.1 collective-permute-done.6.refs_3_
  22.7 1.6 %collective-permute-start.7 = (bf16[224,128]{1,0:T(8,128)(2,1)S(1)}, bf16[224,128]{1,0:T(8,128)(2,1)S(1)}, u32[]{:S(2)}, u32[]{:S(2)}) collective-permute-start(bf16[224,128]{1,0:T(8,128)(2,1)S(1)} %shard_map.87.own), channel_id=1, source_target_pairs={{0,8},{4,12},{8,0},{12,4},{1,9},{5,13},{9,1},{13,5},{2,10},{6,14},... | collective-permute-start | bytes 172040 | tf_op jit(solution)/shard_map/ppermute | solution.py:68
  24.2 0.0 collective-permute-start.9
  24.2 2.7 %collective-permute-done.7.refs_1_ = bf16[224,128]{1,0:T(8,128)(2,1)S(1)} collective-permute-done((bf16[224,128]{1,0:T(8,128)(2,1)S(1)}, bf16[224,128]{1,0:T(8,128)(2,1)S(1)}, u32[]{:S(2)}, u32[]{:S(2)}) %collective-permute-start.7) | collective-permute-done | bytes 57376 | tf_op jit(solution)/shard_map/ppermute | solution.py:68
  26.9 0.0 collective-permute-start.8
  26.9 0.0 collective-permute-done.9.refs_0_
  26.9 0.6 %shard_map.88.products = f32[3,128,512]{2,1,0:T(8,128)S(1)} custom-call(bf16[224,128]{1,0:T(8,128)(2,1)S(1)} %shard_map.87.own, bf16[224,128]{1,0:T(8,128)(2,1)S(1)} %collective-permute-done.9.refs_0_, bf16[224,128]{1,0:T(8,128)(2,1)S(1)} %collective-permute-done.7.refs_1_), custom_call_target="tpu_custom_call" | custom-call | flops 3670016 | bytes 958464 | tf_op jit(solution)/shard_map/pallas_call | solution.py:74
  27.5 0.7 %collective-permute-done.8.block = bf16[224,128]{1,0:T(8,128)(2,1)S(1)} collective-permute-done((bf16[224,128]{1,0:T(8,128)(2,1)S(1)}, bf16[224,128]{1,0:T(8,128)(2,1)S(1)}, u32[]{:S(2)}, u32[]{:S(2)}) %collective-permute-start.8) | collective-permute-done | bytes 57376 | tf_op jit(solution)/shard_map/ppermute | solution.py:68
  28.2 1.1 %shard_map.89 = f32[3,128,512]{2,1,0:T(8,128)} custom-call(s32[1,3]{1,0:T(1,128)S(1)} %copy-done.5, bf16[224,128]{1,0:T(8,128)(2,1)S(1)} %shard_map.87.own, bf16[224,128]{1,0:T(8,128)(2,1)S(1)} %collective-permute-done.8.block, f32[3,128,512]{2,1,0:T(8,128)S(1)} %shard_map.88.products), custom_call_target="tpu_custom_call" | custom-call | flops 1835008 | bytes 1687564 | tf_op jit(solution)/shard_map/pallas_call | solution.py:74
  (8 shorter events, 0.0 us)
Async XLA Ops:
  0.0 5.3 %copy-start = (bf16[2048,1024]{1,0:T(8,128)(2,1)S(1)}, bf16[2048,1024]{1,0:T(8,128)(2,1)}, u32[]{:S(2)}) copy-start(bf16[2048,1024]{1,0:T(8,128)(2,1)} %constant.11.clone.table) | copy-start | bytes 12582916
  2.2 5.0 %collective-permute-start = (f32[16,144]{1,0:T(8,128)S(1)}, f32[16,144]{1,0:T(8,128)S(1)}, u32[]{:S(2)}, u32[]{:S(2)}) collective-permute-start(f32[16,144]{1,0:T(8,128)S(1)} %get-tuple-element.30), channel_id=1, source_target_pairs={{0,1},{1,0},{2,3},{3,2},{4,5},{5,4},{6,7},{7,6},{8,9},{9,8},{10,11... | collective-permute-start | bytes 27656 | tf_op jit(solution)/shard_map/ppermute | solution.py:63
  5.3 1.9 %collective-permute-start.1 = (f32[16,144]{1,0:T(8,128)S(1)}, f32[16,144]{1,0:T(8,128)S(1)}, u32[]{:S(2)}, u32[]{:S(2)}) collective-permute-start(f32[16,144]{1,0:T(8,128)S(1)} %get-tuple-element.31), channel_id=1, source_target_pairs={{1,2},{2,1},{5,6},{6,5},{9,10},{10,9},{13,14},{14,13},{0,4},{3,7},... | collective-permute-start | bytes 27656 | tf_op jit(solution)/shard_map/ppermute | solution.py:63
  5.3 6.0 %copy-start.1 = (bf16[4096,1024]{1,0:T(8,128)(2,1)S(1)}, bf16[4096,1024]{1,0:T(8,128)(2,1)}, u32[]{:S(2)}) copy-start(bf16[4096,1024]{1,0:T(8,128)(2,1)} %constant.10.clone.tapered) | copy-start | bytes 25165828
  7.3 4.0 %copy-start.2 = (bf16[512,512]{1,0:T(8,128)(2,1)S(1)}, bf16[512,512]{1,0:T(8,128)(2,1)}, u32[]{:S(2)}) copy-start(bf16[512,512]{1,0:T(8,128)(2,1)} %constant.13.clone.nearby) | copy-start | bytes 1572868
  7.3 4.0 %copy-start.3 = (f32[1,512]{1,0:T(1,128)S(1)}, f32[1,512]{1,0:T(1,128)}, u32[]{:S(2)}) copy-start(f32[1,512]{1,0:T(1,128)} %constant.14.clone.scale) | copy-start | bytes 6148
  7.3 4.0 %copy-start.4 = (s32[144]{0:T(256)S(1)}, s32[144]{0:T(256)}, u32[]{:S(2)}) copy-start(s32[144]{0:T(256)} %param.9) | copy-start | bytes 1732
  8.1 6.5 %collective-permute-start.2 = (bf16[72,1024]{1,0:T(8,128)(2,1)S(1)}, bf16[72,1024]{1,0:T(8,128)(2,1)S(1)}, u32[]{:S(2)}, u32[]{:S(2)}) collective-permute-start(bf16[72,1024]{1,0:T(8,128)(2,1)S(1)} %get-tuple-element.40), channel_id=1, source_target_pairs={{0,1},{1,0},{2,3},{3,2},{4,5},{5,4},{6,7},{7,6},{8,9},{9,8},{10,11... | collective-permute-start | bytes 442376 | tf_op jit(solution)/shard_map/ppermute | solution.py:63
  11.3 3.3 %collective-permute-start.3 = (bf16[72,1024]{1,0:T(8,128)(2,1)S(1)}, bf16[72,1024]{1,0:T(8,128)(2,1)S(1)}, u32[]{:S(2)}, u32[]{:S(2)}) collective-permute-start(bf16[72,1024]{1,0:T(8,128)(2,1)S(1)} %get-tuple-element.41), channel_id=1, source_target_pairs={{1,2},{2,1},{5,6},{6,5},{9,10},{10,9},{13,14},{14,13},{0,4},{3,7},... | collective-permute-start | bytes 442376 | tf_op jit(solution)/shard_map/ppermute | solution.py:63
  11.3 16.9 %copy-start.5 = (s32[1,3]{1,0:T(1,128)S(1)}, s32[1,3]{1,0:T(1,128)}, u32[]{:S(2)}) copy-start(s32[1,3]{1,0:T(1,128)} %partners.1) | copy-start | bytes 40
  15.1 5.7 %collective-permute-start.4 = (bf16[96,128]{1,0:T(8,128)(2,1)S(1)}, bf16[96,128]{1,0:T(8,128)(2,1)S(1)}, u32[]{:S(2)}, u32[]{:S(2)}) collective-permute-start(bf16[96,128]{1,0:T(8,128)(2,1)S(1)} %get-tuple-element.44), channel_id=1, source_target_pairs={{0,3},{1,2},{2,1},{3,0},{4,7},{5,6},{6,5},{7,4},{8,11},{9,10},{10,... | collective-permute-start | bytes 73736 | tf_op jit(solution)/shard_map/ppermute | solution.py:68
  17.7 4.8 %collective-permute-start.5 = (bf16[96,128]{1,0:T(8,128)(2,1)S(1)}, bf16[96,128]{1,0:T(8,128)(2,1)S(1)}, u32[]{:S(2)}, u32[]{:S(2)}) collective-permute-start(bf16[96,128]{1,0:T(8,128)(2,1)S(1)} %get-tuple-element.45), channel_id=1, source_target_pairs={{0,2},{1,3},{2,0},{3,1},{4,6},{5,7},{6,4},{7,5},{8,10},{9,11},{10,... | collective-permute-start | bytes 73736 | tf_op jit(solution)/shard_map/ppermute | solution.py:68
  18.6 4.1 %collective-permute-start.6 = (bf16[96,128]{1,0:T(8,128)(2,1)S(1)}, bf16[96,128]{1,0:T(8,128)(2,1)S(1)}, u32[]{:S(2)}, u32[]{:S(2)}) collective-permute-start(bf16[96,128]{1,0:T(8,128)(2,1)S(1)} %get-tuple-element.46), channel_id=1, source_target_pairs={{0,1},{1,0},{2,3},{3,2},{4,5},{5,4},{6,7},{7,6},{8,9},{9,8},{10,11... | collective-permute-start | bytes 73736 | tf_op jit(solution)/shard_map/ppermute | solution.py:68
  22.7 4.2 %collective-permute-start.7 = (bf16[224,128]{1,0:T(8,128)(2,1)S(1)}, bf16[224,128]{1,0:T(8,128)(2,1)S(1)}, u32[]{:S(2)}, u32[]{:S(2)}) collective-permute-start(bf16[224,128]{1,0:T(8,128)(2,1)S(1)} %shard_map.87.own), channel_id=1, source_target_pairs={{0,8},{4,12},{8,0},{12,4},{1,9},{5,13},{9,1},{13,5},{2,10},{6,14},... | collective-permute-start | bytes 172040 | tf_op jit(solution)/shard_map/ppermute | solution.py:68
  24.2 2.7 %collective-permute-start.9 = (bf16[224,128]{1,0:T(8,128)(2,1)S(1)}, bf16[224,128]{1,0:T(8,128)(2,1)S(1)}, u32[]{:S(2)}, u32[]{:S(2)}) collective-permute-start(bf16[224,128]{1,0:T(8,128)(2,1)S(1)} %shard_map.87.own), channel_id=1, source_target_pairs={{0,4},{4,0},{8,12},{12,8},{1,5},{5,1},{9,13},{13,9},{2,6},{6,2},{1... | collective-permute-start | bytes 172040 | tf_op jit(solution)/shard_map/ppermute | solution.py:68
  26.9 1.2 %collective-permute-start.8 = (bf16[224,128]{1,0:T(8,128)(2,1)S(1)}, bf16[224,128]{1,0:T(8,128)(2,1)S(1)}, u32[]{:S(2)}, u32[]{:S(2)}) collective-permute-start(bf16[224,128]{1,0:T(8,128)(2,1)S(1)} %collective-permute-done.7.refs_1_), channel_id=1, source_target_pairs={{0,4},{4,0},{8,12},{12,8},{1,5},{5,1},{9,13},{13,9},{2,6},{6,2},{1... | collective-permute-start | bytes 172040 | tf_op jit(solution)/shard_map/ppermute | solution.py:68

commit v8 on v7

--- a/solution.py
+++ b/solution.py
@@ -344,7 +344,7 @@
     for slot in range(MAXP):
         @pl.when(which[slot] < count)
         def _(slot=slot):
-            copy(slot, products.at[jnp.minimum(which[slot], count - 1)]).start()
+            copy(slot, products.at[jnp.where(which[slot] == 0, 0, 3 - jnp.minimum(which[slot], count - 1))]).start()
 
     mine[...] = own[...].astype(F32)
     others[...] = block[...].astype(F32)
@@ -464,7 +464,7 @@
         products = call(
             functools.partial(near_kernel, segments),
             shape(result, F32),
-            (mine, beside, across),
+            (mine, across, beside),
             scratch_shapes=floats,
             flops=2 * flops,
         )

time: 29.4 us -> 29.4 us (level)
  no operation moved by 1% of the time
where the time goes in v8:
time: 29.4 us; the launch traced here: 29.3 us
  starting transfers between devices  12.3 us (42%)
  Pallas kernels  9.95 us (34%)
  waiting for transfers between devices  6.84 us (23%)
    pallas_call x8, Pallas kernels, call(): pl.pallas_call(kernel, out_shape=out_shape, in_specs=specs or [VMEM] * le...  9.95 us
    ppermute x6, waiting for transfers between devices, swapped(): lax.ppermute(block, axis, [(i, i ^ mask) for i in range(lax.axis_size(axi...  6.45 us
    ppermute x4, starting transfers between devices, neighbour_swap(): sent[i] = lax.ppermute((first, second)[i], ('stn', 'tchunk'), pairs[i])  6.31 us
    ppermute x6, starting transfers between devices, swapped(): lax.ppermute(block, axis, [(i, i ^ mask) for i in range(lax.axis_size(axi...  6.01 us
  transfers between devices with their start and end apart: 10, of which 6 were waited for; matrix products, arithmetic and copies ran while one was open for 0% of the time, Pallas kernels for 18%

profile of v8, /device:TPU:0, one launch (start us, length us, event | category | flops | bytes accessed | tf_op | source)
XLA Modules:
  0.0 29.3 jit_solution(2341440717128328756)
XLA Ops:
  0.0 2.2 %shard_map.82 = (f32[144,4096]{1,0:T(8,128)S(1)}, f32[144,32]{1,0:T(8,128)S(1)}, f32[16,144]{1,0:T(8,128)S(1)}, f32[16,144]{1,0:T(8,128)S(1)}, f32[2,2048]{1,0:T(2,128)S(1)}) custom-call(f32[144,4096]{1,0:T(8,128)} %source.1, f32[2,2048]{1,0:T(2,128)} %constant.12.clone.taper_source), custom_call_target="tpu_custom_call" | custom-call | flops 10000000000 | bytes 4788224 | tf_op jit(solution)/shard_map/pallas_call | solution.py:74
  2.2 3.1 %collective-permute-start = (f32[16,144]{1,0:T(8,128)S(1)}, f32[16,144]{1,0:T(8,128)S(1)}, u32[]{:S(2)}, u32[]{:S(2)}) collective-permute-start(f32[16,144]{1,0:T(8,128)S(1)} %get-tuple-element.30), channel_id=1, source_target_pairs={{0,1},{1,0},{2,3},{3,2},{4,5},{5,4},{6,7},{7,6},{8,9},{9,8},{10,11... | collective-permute-start | bytes 27656 | tf_op jit(solution)/shard_map/ppermute | solution.py:63
  5.3 0.0 collective-permute-start.1
  5.3 1.9 %shard_map.83 = (bf16[144,1664]{1,0:T(8,128)(2,1)S(1)}, f32[144,1024]{1,0:T(8,128)S(1)}, f32[144,1024]{1,0:T(8,128)S(1)}, f32[144,32]{1,0:T(8,128)S(1)}, f32[9,7...) custom-call(f32[144,4096]{1,0:T(8,128)S(1)} %get-tuple-element.26.raw, f32[144,32]{1,0:T(8,128)S(1)} %get-tuple-element.27.sums, ...), custom_call_target="tpu_custom_call" | custom-call | flops 490733568 | bytes 13869056 | tf_op jit(solution)/shard_map/pallas_call | solution.py:74
  7.2 0.0 collective-permute-done.from_even
  7.2 0.0 collective-permute-done.1.from_odd
  7.3 0.0 copy-start.2
  7.3 0.0 copy-start.3
  7.3 0.0 copy-start.4
  7.3 0.8 %shard_map.84 = (bf16[72,1024]{1,0:T(8,128)(2,1)S(1)}, bf16[72,1024]{1,0:T(8,128)(2,1)S(1)}, f32[144,32]{1,0:T(8,128)S(1)}) custom-call(f32[144,32]{1,0:T(8,128)S(1)} %get-tuple-element.29.window, f32[16,144]{1,0:T(8,128)S(1)} %collective-permute-done.from_even, f32[16,144]{1,0:T(8,128)S(1)} %collective-permute-done.1.from_odd, ...), custom_call_target="tpu_custom_call" | custom-call | flops 2949120 | bytes 7133184 | tf_op jit(solution)/shard_map/pallas_call | solution.py:74
  8.1 3.2 %collective-permute-start.2 = (bf16[72,1024]{1,0:T(8,128)(2,1)S(1)}, bf16[72,1024]{1,0:T(8,128)(2,1)S(1)}, u32[]{:S(2)}, u32[]{:S(2)}) collective-permute-start(bf16[72,1024]{1,0:T(8,128)(2,1)S(1)} %get-tuple-element.40), channel_id=1, source_target_pairs={{0,1},{1,0},{2,3},{3,2},{4,5},{5,4},{6,7},{7,6},{8,9},{9,8},{10,11... | collective-permute-start | bytes 442376 | tf_op jit(solution)/shard_map/ppermute | solution.py:63
  11.3 0.0 collective-permute-start.3
  11.3 0.0 copy-done.1
  11.3 0.0 copy-start.5
  11.3 2.9 %shard_map.85 = (bf16[32,512]{1,0:T(8,128)(2,1)S(1)}, f32[72,1024]{1,0:T(8,128)S(1)}, f32[72,1024]{1,0:T(8,128)S(1)}) custom-call(f32[144,4096]{1,0:T(8,128)S(1)} %get-tuple-element.26.raw, f32[144,32]{1,0:T(8,128)S(1)} %get-tuple-element.36.factor, bf16[144,1664]{1,0:T(8,128)(2,1)S(1)} %get-tuple-element.37.middle, bf16[2048,1024]{1,0:T(8,128)(2,1)S(1)} %copy-done, ...), custom_call_target="tpu_custom_call" | custom-call | flops 1811939328 | bytes 17785408 | tf_op jit(solution)/shard_map/pallas_call | solution.py:74
  14.2 0.4 %collective-permute-done.2.from_even = bf16[72,1024]{1,0:T(8,128)(2,1)S(1)} collective-permute-done((bf16[72,1024]{1,0:T(8,128)(2,1)S(1)}, bf16[72,1024]{1,0:T(8,128)(2,1)S(1)}, u32[]{:S(2)}, u32[]{:S(2)}) %collective-permute-start.2) | collective-permute-done | bytes 147488 | tf_op jit(solution)/shard_map/ppermute | solution.py:63
  14.6 0.0 collective-permute-done.3.from_odd
  14.6 0.5 %shard_map.86 = (bf16[96,128]{1,0:T(8,128)(2,1)S(1)}, bf16[96,128]{1,0:T(8,128)(2,1)S(1)}, bf16[96,128]{1,0:T(8,128)(2,1)S(1)}, bf16[96,128]{1,0:T(8,128)(2,1)S(1)}) custom-call(f32[72,1024]{1,0:T(8,128)S(1)} %get-tuple-element.38.keep_right, f32[72,1024]{1,0:T(8,128)S(1)} %get-tuple-element.39.keep_left, ...), custom_call_target="tpu_custom_call" | custom-call | flops 301989888 | bytes 1542720 | tf_op jit(solution)/shard_map/pallas_call | solution.py:74
  15.1 2.6 %collective-permute-start.4 = (bf16[96,128]{1,0:T(8,128)(2,1)S(1)}, bf16[96,128]{1,0:T(8,128)(2,1)S(1)}, u32[]{:S(2)}, u32[]{:S(2)}) collective-permute-start(bf16[96,128]{1,0:T(8,128)(2,1)S(1)} %get-tuple-element.44), channel_id=1, source_target_pairs={{0,3},{1,2},{2,1},{3,0},{4,7},{5,6},{6,5},{7,4},{8,11},{9,10},{10,... | collective-permute-start | bytes 73736 | tf_op jit(solution)/shard_map/ppermute | solution.py:68
  17.7 0.9 %collective-permute-start.5 = (bf16[96,128]{1,0:T(8,128)(2,1)S(1)}, bf16[96,128]{1,0:T(8,128)(2,1)S(1)}, u32[]{:S(2)}, u32[]{:S(2)}) collective-permute-start(bf16[96,128]{1,0:T(8,128)(2,1)S(1)} %get-tuple-element.45), channel_id=1, source_target_pairs={{0,2},{1,3},{2,0},{3,1},{4,6},{5,7},{6,4},{7,5},{8,10},{9,11},{10,... | collective-permute-start | bytes 73736 | tf_op jit(solution)/shard_map/ppermute | solution.py:68
  18.6 1.0 %collective-permute-start.6 = (bf16[96,128]{1,0:T(8,128)(2,1)S(1)}, bf16[96,128]{1,0:T(8,128)(2,1)S(1)}, u32[]{:S(2)}, u32[]{:S(2)}) collective-permute-start(bf16[96,128]{1,0:T(8,128)(2,1)S(1)} %get-tuple-element.46), channel_id=1, source_target_pairs={{0,1},{1,0},{2,3},{3,2},{4,5},{5,4},{6,7},{7,6},{8,9},{9,8},{10,11... | collective-permute-start | bytes 73736 | tf_op jit(solution)/shard_map/ppermute | solution.py:68
  19.6 1.3 %collective-permute-done.4.refs_1_ = bf16[96,128]{1,0:T(8,128)(2,1)S(1)} collective-permute-done((bf16[96,128]{1,0:T(8,128)(2,1)S(1)}, bf16[96,128]{1,0:T(8,128)(2,1)S(1)}, u32[]{:S(2)}, u32[]{:S(2)}) %collective-permute-start.4) | collective-permute-done | bytes 24608 | tf_op jit(solution)/shard_map/ppermute | solution.py:68
  20.8 1.7 %collective-permute-done.5.refs_2_ = bf16[96,128]{1,0:T(8,128)(2,1)S(1)} collective-permute-done((bf16[96,128]{1,0:T(8,128)(2,1)S(1)}, bf16[96,128]{1,0:T(8,128)(2,1)S(1)}, u32[]{:S(2)}, u32[]{:S(2)}) %collective-permute-start.5) | collective-permute-done | bytes 24608 | tf_op jit(solution)/shard_map/ppermute | solution.py:68
  22.5 0.1 collective-permute-done.6.refs_3_
  22.7 1.6 %collective-permute-start.7 = (bf16[224,128]{1,0:T(8,128)(2,1)S(1)}, bf16[224,128]{1,0:T(8,128)(2,1)S(1)}, u32[]{:S(2)}, u32[]{:S(2)}) collective-permute-start(bf16[224,128]{1,0:T(8,128)(2,1)S(1)} %shard_map.87.own), channel_id=1, source_target_pairs={{0,8},{4,12},{8,0},{12,4},{1,9},{5,13},{9,1},{13,5},{2,10},{6,14},... | collective-permute-start | bytes 172040 | tf_op jit(solution)/shard_map/ppermute | solution.py:68
  24.2 0.0 collective-permute-start.9
  24.2 2.7 %collective-permute-done.7.refs_0_ = bf16[224,128]{1,0:T(8,128)(2,1)S(1)} collective-permute-done((bf16[224,128]{1,0:T(8,128)(2,1)S(1)}, bf16[224,128]{1,0:T(8,128)(2,1)S(1)}, u32[]{:S(2)}, u32[]{:S(2)}) %collective-permute-start.7) | collective-permute-done | bytes 57376 | tf_op jit(solution)/shard_map/ppermute | solution.py:68
  26.9 0.0 collective-permute-start.8
  26.9 0.0 collective-permute-done.9.refs_1_
  26.9 0.6 %shard_map.88.products = f32[3,128,512]{2,1,0:T(8,128)S(1)} custom-call(bf16[224,128]{1,0:T(8,128)(2,1)S(1)} %shard_map.87.own, bf16[224,128]{1,0:T(8,128)(2,1)S(1)} %collective-permute-done.7.refs_0_, bf16[224,128]{1,0:T(8,128)(2,1)S(1)} %collective-permute-done.9.refs_1_), custom_call_target="tpu_custom_call" | custom-call | flops 3670016 | bytes 958464 | tf_op jit(solution)/shard_map/pallas_call | solution.py:74
  27.5 0.7 %collective-permute-done.8.block = bf16[224,128]{1,0:T(8,128)(2,1)S(1)} collective-permute-done((bf16[224,128]{1,0:T(8,128)(2,1)S(1)}, bf16[224,128]{1,0:T(8,128)(2,1)S(1)}, u32[]{:S(2)}, u32[]{:S(2)}) %collective-permute-start.8) | collective-permute-done | bytes 57376 | tf_op jit(solution)/shard_map/ppermute | solution.py:68
  28.2 1.1 %shard_map.89 = f32[3,128,512]{2,1,0:T(8,128)} custom-call(s32[1,3]{1,0:T(1,128)S(1)} %copy-done.5, bf16[224,128]{1,0:T(8,128)(2,1)S(1)} %shard_map.87.own, bf16[224,128]{1,0:T(8,128)(2,1)S(1)} %collective-permute-done.8.block, f32[3,128,512]{2,1,0:T(8,128)S(1)} %shard_map.88.products), custom_call_target="tpu_custom_call" | custom-call | flops 1835008 | bytes 1687564 | tf_op jit(solution)/shard_map/pallas_call | solution.py:74
  (8 shorter events, 0.0 us)
Async XLA Ops:
  0.0 5.3 %copy-start = (bf16[2048,1024]{1,0:T(8,128)(2,1)S(1)}, bf16[2048,1024]{1,0:T(8,128)(2,1)}, u32[]{:S(2)}) copy-start(bf16[2048,1024]{1,0:T(8,128)(2,1)} %constant.11.clone.table) | copy-start | bytes 12582916
  2.2 5.0 %collective-permute-start = (f32[16,144]{1,0:T(8,128)S(1)}, f32[16,144]{1,0:T(8,128)S(1)}, u32[]{:S(2)}, u32[]{:S(2)}) collective-permute-start(f32[16,144]{1,0:T(8,128)S(1)} %get-tuple-element.30), channel_id=1, source_target_pairs={{0,1},{1,0},{2,3},{3,2},{4,5},{5,4},{6,7},{7,6},{8,9},{9,8},{10,11... | collective-permute-start | bytes 27656 | tf_op jit(solution)/shard_map/ppermute | solution.py:63
  5.3 1.9 %collective-permute-start.1 = (f32[16,144]{1,0:T(8,128)S(1)}, f32[16,144]{1,0:T(8,128)S(1)}, u32[]{:S(2)}, u32[]{:S(2)}) collective-permute-start(f32[16,144]{1,0:T(8,128)S(1)} %get-tuple-element.31), channel_id=1, source_target_pairs={{1,2},{2,1},{5,6},{6,5},{9,10},{10,9},{13,14},{14,13},{0,4},{3,7},... | collective-permute-start | bytes 27656 | tf_op jit(solution)/shard_map/ppermute | solution.py:63
  5.3 6.0 %copy-start.1 = (bf16[4096,1024]{1,0:T(8,128)(2,1)S(1)}, bf16[4096,1024]{1,0:T(8,128)(2,1)}, u32[]{:S(2)}) copy-start(bf16[4096,1024]{1,0:T(8,128)(2,1)} %constant.10.clone.tapered) | copy-start | bytes 25165828
  7.3 4.0 %copy-start.2 = (bf16[512,512]{1,0:T(8,128)(2,1)S(1)}, bf16[512,512]{1,0:T(8,128)(2,1)}, u32[]{:S(2)}) copy-start(bf16[512,512]{1,0:T(8,128)(2,1)} %constant.13.clone.nearby) | copy-start | bytes 1572868
  7.3 4.0 %copy-start.3 = (f32[1,512]{1,0:T(1,128)S(1)}, f32[1,512]{1,0:T(1,128)}, u32[]{:S(2)}) copy-start(f32[1,512]{1,0:T(1,128)} %constant.14.clone.scale) | copy-start | bytes 6148
  7.3 4.0 %copy-start.4 = (s32[144]{0:T(256)S(1)}, s32[144]{0:T(256)}, u32[]{:S(2)}) copy-start(s32[144]{0:T(256)} %param.9) | copy-start | bytes 1732
  8.1 6.5 %collective-permute-start.2 = (bf16[72,1024]{1,0:T(8,128)(2,1)S(1)}, bf16[72,1024]{1,0:T(8,128)(2,1)S(1)}, u32[]{:S(2)}, u32[]{:S(2)}) collective-permute-start(bf16[72,1024]{1,0:T(8,128)(2,1)S(1)} %get-tuple-element.40), channel_id=1, source_target_pairs={{0,1},{1,0},{2,3},{3,2},{4,5},{5,4},{6,7},{7,6},{8,9},{9,8},{10,11... | collective-permute-start | bytes 442376 | tf_op jit(solution)/shard_map/ppermute | solution.py:63
  11.3 3.3 %collective-permute-start.3 = (bf16[72,1024]{1,0:T(8,128)(2,1)S(1)}, bf16[72,1024]{1,0:T(8,128)(2,1)S(1)}, u32[]{:S(2)}, u32[]{:S(2)}) collective-permute-start(bf16[72,1024]{1,0:T(8,128)(2,1)S(1)} %get-tuple-element.41), channel_id=1, source_target_pairs={{1,2},{2,1},{5,6},{6,5},{9,10},{10,9},{13,14},{14,13},{0,4},{3,7},... | collective-permute-start | bytes 442376 | tf_op jit(solution)/shard_map/ppermute | solution.py:63
  11.3 16.9 %copy-start.5 = (s32[1,3]{1,0:T(1,128)S(1)}, s32[1,3]{1,0:T(1,128)}, u32[]{:S(2)}) copy-start(s32[1,3]{1,0:T(1,128)} %partners.1) | copy-start | bytes 40
  15.1 5.7 %collective-permute-start.4 = (bf16[96,128]{1,0:T(8,128)(2,1)S(1)}, bf16[96,128]{1,0:T(8,128)(2,1)S(1)}, u32[]{:S(2)}, u32[]{:S(2)}) collective-permute-start(bf16[96,128]{1,0:T(8,128)(2,1)S(1)} %get-tuple-element.44), channel_id=1, source_target_pairs={{0,3},{1,2},{2,1},{3,0},{4,7},{5,6},{6,5},{7,4},{8,11},{9,10},{10,... | collective-permute-start | bytes 73736 | tf_op jit(solution)/shard_map/ppermute | solution.py:68
  17.7 4.8 %collective-permute-start.5 = (bf16[96,128]{1,0:T(8,128)(2,1)S(1)}, bf16[96,128]{1,0:T(8,128)(2,1)S(1)}, u32[]{:S(2)}, u32[]{:S(2)}) collective-permute-start(bf16[96,128]{1,0:T(8,128)(2,1)S(1)} %get-tuple-element.45), channel_id=1, source_target_pairs={{0,2},{1,3},{2,0},{3,1},{4,6},{5,7},{6,4},{7,5},{8,10},{9,11},{10,... | collective-permute-start | bytes 73736 | tf_op jit(solution)/shard_map/ppermute | solution.py:68
  18.6 4.1 %collective-permute-start.6 = (bf16[96,128]{1,0:T(8,128)(2,1)S(1)}, bf16[96,128]{1,0:T(8,128)(2,1)S(1)}, u32[]{:S(2)}, u32[]{:S(2)}) collective-permute-start(bf16[96,128]{1,0:T(8,128)(2,1)S(1)} %get-tuple-element.46), channel_id=1, source_target_pairs={{0,1},{1,0},{2,3},{3,2},{4,5},{5,4},{6,7},{7,6},{8,9},{9,8},{10,11... | collective-permute-start | bytes 73736 | tf_op jit(solution)/shard_map/ppermute | solution.py:68
  22.7 4.2 %collective-permute-start.7 = (bf16[224,128]{1,0:T(8,128)(2,1)S(1)}, bf16[224,128]{1,0:T(8,128)(2,1)S(1)}, u32[]{:S(2)}, u32[]{:S(2)}) collective-permute-start(bf16[224,128]{1,0:T(8,128)(2,1)S(1)} %shard_map.87.own), channel_id=1, source_target_pairs={{0,8},{4,12},{8,0},{12,4},{1,9},{5,13},{9,1},{13,5},{2,10},{6,14},... | collective-permute-start | bytes 172040 | tf_op jit(solution)/shard_map/ppermute | solution.py:68
  24.2 2.7 %collective-permute-start.9 = (bf16[224,128]{1,0:T(8,128)(2,1)S(1)}, bf16[224,128]{1,0:T(8,128)(2,1)S(1)}, u32[]{:S(2)}, u32[]{:S(2)}) collective-permute-start(bf16[224,128]{1,0:T(8,128)(2,1)S(1)} %shard_map.87.own), channel_id=1, source_target_pairs={{0,4},{4,0},{8,12},{12,8},{1,5},{5,1},{9,13},{13,9},{2,6},{6,2},{1... | collective-permute-start | bytes 172040 | tf_op jit(solution)/shard_map/ppermute | solution.py:68
  26.9 1.2 %collective-permute-start.8 = (bf16[224,128]{1,0:T(8,128)(2,1)S(1)}, bf16[224,128]{1,0:T(8,128)(2,1)S(1)}, u32[]{:S(2)}, u32[]{:S(2)}) collective-permute-start(bf16[224,128]{1,0:T(8,128)(2,1)S(1)} %collective-permute-done.7.refs_0_), channel_id=1, source_target_pairs={{0,4},{4,0},{8,12},{12,8},{1,5},{5,1},{9,13},{13,9},{2,6},{6,2},{1... | collective-permute-start | bytes 172040 | tf_op jit(solution)/shard_map/ppermute | solution.py:68

commit v9 on v7

--- a/solution.py
+++ b/solution.py
@@ -304,18 +304,22 @@
 
 def cross_terms(segments, mine, others, out):
     side = 2 * SUB
+    theirs = []
+    for s in range(segments):
+        c, d = others[s * side : s * side + SUB, :], others[s * side + SUB : (s + 1) * side, :]
+        theirs.append((c, c + d, c - d))
     real, imag = [], []
     for q in range(SUB):
-        real_sum = jnp.zeros((SUB, mine.shape[1]), F32)
-        imag_sum = jnp.zeros((SUB, mine.shape[1]), F32)
-        for s in range(segments):
-            first = s * side
-            a, b = mine[first + q : first + q + 1, :], mine[first + SUB + q : first + SUB + q + 1, :]
-            c, d = others[first : first + SUB, :], others[first + SUB : first + side, :]
-            real_sum += a * c + b * d
-            imag_sum += b * c - a * d
-        real.append(real_sum * (1.0 / segments))
-        imag.append(imag_sum * (1.0 / segments))
+        shared = jnp.zeros((SUB, mine.shape[1]), F32)
+        first, second = shared, shared
+        for s, (c, plus, minus) in enumerate(theirs):
+            row = s * side + q
+            a, b = mine[row : row + 1, :], mine[row + SUB : row + SUB + 1, :]
+            shared += (a + b) * c
+            first += b * minus
+            second += a * plus
+        real.append((shared - first) * (1.0 / segments))
+        imag.append((shared - second) * (1.0 / segments))
     half = SUB * SUB
     out[:, :half] = jnp.transpose(jnp.concatenate(real, axis=0))
     out[:, half:] = jnp.transpose(jnp.concatenate(imag, axis=0))

time: 29.4 us -> 29.4 us (level)
  no operation moved by 1% of the time
where the time goes in v9:
time: 29.4 us; the launch traced here: 29.2 us
  starting transfers between devices  12.3 us (42%)
  Pallas kernels  9.9 us (34%)
  waiting for transfers between devices  6.86 us (23%)
    pallas_call x8, Pallas kernels, call(): pl.pallas_call(kernel, out_shape=out_shape, in_specs=specs or [VMEM] * le...  9.9 us
    ppermute x6, waiting for transfers between devices, swapped(): lax.ppermute(block, axis, [(i, i ^ mask) for i in range(lax.axis_size(axi...  6.47 us
    ppermute x4, starting transfers between devices, neighbour_swap(): sent[i] = lax.ppermute((first, second)[i], ('stn', 'tchunk'), pairs[i])  6.31 us
    ppermute x6, starting transfers between devices, swapped(): lax.ppermute(block, axis, [(i, i ^ mask) for i in range(lax.axis_size(axi...  6.01 us
  transfers between devices with their start and end apart: 10, of which 6 were waited for; matrix products, arithmetic and copies ran while one was open for 0% of the time, Pallas kernels for 18%

profile of v9, /device:TPU:0, one launch (start us, length us, event | category | flops | bytes accessed | tf_op | source)
XLA Modules:
  0.0 29.2 jit_solution(38654292843084474)
XLA Ops:
  0.0 2.2 %shard_map.82 = (f32[144,4096]{1,0:T(8,128)S(1)}, f32[144,32]{1,0:T(8,128)S(1)}, f32[16,144]{1,0:T(8,128)S(1)}, f32[16,144]{1,0:T(8,128)S(1)}, f32[2,2048]{1,0:T(2,128)S(1)}) custom-call(f32[144,4096]{1,0:T(8,128)} %source.1, f32[2,2048]{1,0:T(2,128)} %constant.12.clone.taper_source), custom_call_target="tpu_custom_call" | custom-call | flops 10000000000 | bytes 4788224 | tf_op jit(solution)/shard_map/pallas_call | solution.py:74
  2.2 3.1 %collective-permute-start = (f32[16,144]{1,0:T(8,128)S(1)}, f32[16,144]{1,0:T(8,128)S(1)}, u32[]{:S(2)}, u32[]{:S(2)}) collective-permute-start(f32[16,144]{1,0:T(8,128)S(1)} %get-tuple-element.30), channel_id=1, source_target_pairs={{0,1},{1,0},{2,3},{3,2},{4,5},{5,4},{6,7},{7,6},{8,9},{9,8},{10,11... | collective-permute-start | bytes 27656 | tf_op jit(solution)/shard_map/ppermute | solution.py:63
  5.3 0.0 collective-permute-start.1
  5.3 0.0 copy-done
  5.3 1.9 %shard_map.83 = (bf16[144,1664]{1,0:T(8,128)(2,1)S(1)}, f32[144,1024]{1,0:T(8,128)S(1)}, f32[144,1024]{1,0:T(8,128)S(1)}, f32[144,32]{1,0:T(8,128)S(1)}, f32[9,7...) custom-call(f32[144,4096]{1,0:T(8,128)S(1)} %get-tuple-element.26.raw, f32[144,32]{1,0:T(8,128)S(1)} %get-tuple-element.27.sums, ...), custom_call_target="tpu_custom_call" | custom-call | flops 490733568 | bytes 13869056 | tf_op jit(solution)/shard_map/pallas_call | solution.py:74
  7.2 0.0 collective-permute-done.from_even
  7.2 0.0 collective-permute-done.1.from_odd
  7.3 0.0 copy-start.2
  7.3 0.0 copy-start.3
  7.3 0.0 copy-start.4
  7.3 0.8 %shard_map.84 = (bf16[72,1024]{1,0:T(8,128)(2,1)S(1)}, bf16[72,1024]{1,0:T(8,128)(2,1)S(1)}, f32[144,32]{1,0:T(8,128)S(1)}) custom-call(f32[144,32]{1,0:T(8,128)S(1)} %get-tuple-element.29.window, f32[16,144]{1,0:T(8,128)S(1)} %collective-permute-done.from_even, f32[16,144]{1,0:T(8,128)S(1)} %collective-permute-done.1.from_odd, ...), custom_call_target="tpu_custom_call" | custom-call | flops 2949120 | bytes 7133184 | tf_op jit(solution)/shard_map/pallas_call | solution.py:74
  8.1 3.2 %collective-permute-start.2 = (bf16[72,1024]{1,0:T(8,128)(2,1)S(1)}, bf16[72,1024]{1,0:T(8,128)(2,1)S(1)}, u32[]{:S(2)}, u32[]{:S(2)}) collective-permute-start(bf16[72,1024]{1,0:T(8,128)(2,1)S(1)} %get-tuple-element.40), channel_id=1, source_target_pairs={{0,1},{1,0},{2,3},{3,2},{4,5},{5,4},{6,7},{7,6},{8,9},{9,8},{10,11... | collective-permute-start | bytes 442376 | tf_op jit(solution)/shard_map/ppermute | solution.py:63
  11.3 0.0 collective-permute-start.3
  11.3 0.0 copy-start.5
  11.3 2.9 %shard_map.85 = (bf16[32,512]{1,0:T(8,128)(2,1)S(1)}, f32[72,1024]{1,0:T(8,128)S(1)}, f32[72,1024]{1,0:T(8,128)S(1)}) custom-call(f32[144,4096]{1,0:T(8,128)S(1)} %get-tuple-element.26.raw, f32[144,32]{1,0:T(8,128)S(1)} %get-tuple-element.36.factor, bf16[144,1664]{1,0:T(8,128)(2,1)S(1)} %get-tuple-element.37.middle, bf16[2048,1024]{1,0:T(8,128)(2,1)S(1)} %copy-done, ...), custom_call_target="tpu_custom_call" | custom-call | flops 1811939328 | bytes 17785408 | tf_op jit(solution)/shard_map/pallas_call | solution.py:74
  14.2 0.4 %collective-permute-done.2.from_even = bf16[72,1024]{1,0:T(8,128)(2,1)S(1)} collective-permute-done((bf16[72,1024]{1,0:T(8,128)(2,1)S(1)}, bf16[72,1024]{1,0:T(8,128)(2,1)S(1)}, u32[]{:S(2)}, u32[]{:S(2)}) %collective-permute-start.2) | collective-permute-done | bytes 147488 | tf_op jit(solution)/shard_map/ppermute | solution.py:63
  14.6 0.0 collective-permute-done.3.from_odd
  14.6 0.5 %shard_map.86 = (bf16[96,128]{1,0:T(8,128)(2,1)S(1)}, bf16[96,128]{1,0:T(8,128)(2,1)S(1)}, bf16[96,128]{1,0:T(8,128)(2,1)S(1)}, bf16[96,128]{1,0:T(8,128)(2,1)S(1)}) custom-call(f32[72,1024]{1,0:T(8,128)S(1)} %get-tuple-element.38.keep_right, f32[72,1024]{1,0:T(8,128)S(1)} %get-tuple-element.39.keep_left, ...), custom_call_target="tpu_custom_call" | custom-call | flops 301989888 | bytes 1542720 | tf_op jit(solution)/shard_map/pallas_call | solution.py:74
  15.1 2.6 %collective-permute-start.4 = (bf16[96,128]{1,0:T(8,128)(2,1)S(1)}, bf16[96,128]{1,0:T(8,128)(2,1)S(1)}, u32[]{:S(2)}, u32[]{:S(2)}) collective-permute-start(bf16[96,128]{1,0:T(8,128)(2,1)S(1)} %get-tuple-element.44), channel_id=1, source_target_pairs={{0,3},{1,2},{2,1},{3,0},{4,7},{5,6},{6,5},{7,4},{8,11},{9,10},{10,... | collective-permute-start | bytes 73736 | tf_op jit(solution)/shard_map/ppermute | solution.py:68
  17.7 0.9 %collective-permute-start.5 = (bf16[96,128]{1,0:T(8,128)(2,1)S(1)}, bf16[96,128]{1,0:T(8,128)(2,1)S(1)}, u32[]{:S(2)}, u32[]{:S(2)}) collective-permute-start(bf16[96,128]{1,0:T(8,128)(2,1)S(1)} %get-tuple-element.45), channel_id=1, source_target_pairs={{0,2},{1,3},{2,0},{3,1},{4,6},{5,7},{6,4},{7,5},{8,10},{9,11},{10,... | collective-permute-start | bytes 73736 | tf_op jit(solution)/shard_map/ppermute | solution.py:68
  18.6 1.0 %collective-permute-start.6 = (bf16[96,128]{1,0:T(8,128)(2,1)S(1)}, bf16[96,128]{1,0:T(8,128)(2,1)S(1)}, u32[]{:S(2)}, u32[]{:S(2)}) collective-permute-start(bf16[96,128]{1,0:T(8,128)(2,1)S(1)} %get-tuple-element.46), channel_id=1, source_target_pairs={{0,1},{1,0},{2,3},{3,2},{4,5},{5,4},{6,7},{7,6},{8,9},{9,8},{10,11... | collective-permute-start | bytes 73736 | tf_op jit(solution)/shard_map/ppermute | solution.py:68
  19.6 1.3 %collective-permute-done.4.refs_1_ = bf16[96,128]{1,0:T(8,128)(2,1)S(1)} collective-permute-done((bf16[96,128]{1,0:T(8,128)(2,1)S(1)}, bf16[96,128]{1,0:T(8,128)(2,1)S(1)}, u32[]{:S(2)}, u32[]{:S(2)}) %collective-permute-start.4) | collective-permute-done | bytes 24608 | tf_op jit(solution)/shard_map/ppermute | solution.py:68
  20.8 1.7 %collective-permute-done.5.refs_2_ = bf16[96,128]{1,0:T(8,128)(2,1)S(1)} collective-permute-done((bf16[96,128]{1,0:T(8,128)(2,1)S(1)}, bf16[96,128]{1,0:T(8,128)(2,1)S(1)}, u32[]{:S(2)}, u32[]{:S(2)}) %collective-permute-start.5) | collective-permute-done | bytes 24608 | tf_op jit(solution)/shard_map/ppermute | solution.py:68
  22.5 0.1 collective-permute-done.6.refs_3_
  22.7 1.6 %collective-permute-start.7 = (bf16[224,128]{1,0:T(8,128)(2,1)S(1)}, bf16[224,128]{1,0:T(8,128)(2,1)S(1)}, u32[]{:S(2)}, u32[]{:S(2)}) collective-permute-start(bf16[224,128]{1,0:T(8,128)(2,1)S(1)} %shard_map.87.own), channel_id=1, source_target_pairs={{0,8},{4,12},{8,0},{12,4},{1,9},{5,13},{9,1},{13,5},{2,10},{6,14},... | collective-permute-start | bytes 172040 | tf_op jit(solution)/shard_map/ppermute | solution.py:68
  24.2 0.0 collective-permute-start.9
  24.2 2.7 %collective-permute-done.7.refs_1_ = bf16[224,128]{1,0:T(8,128)(2,1)S(1)} collective-permute-done((bf16[224,128]{1,0:T(8,128)(2,1)S(1)}, bf16[224,128]{1,0:T(8,128)(2,1)S(1)}, u32[]{:S(2)}, u32[]{:S(2)}) %collective-permute-start.7) | collective-permute-done | bytes 57376 | tf_op jit(solution)/shard_map/ppermute | solution.py:68
  26.9 0.0 collective-permute-start.8
  26.9 0.0 collective-permute-done.9.refs_0_
  26.9 0.5 %shard_map.88.products = f32[3,128,512]{2,1,0:T(8,128)S(1)} custom-call(bf16[224,128]{1,0:T(8,128)(2,1)S(1)} %shard_map.87.own, bf16[224,128]{1,0:T(8,128)(2,1)S(1)} %collective-permute-done.9.refs_0_, bf16[224,128]{1,0:T(8,128)(2,1)S(1)} %collective-permute-done.7.refs_1_), custom_call_target="tpu_custom_call" | custom-call | flops 3670016 | bytes 958464 | tf_op jit(solution)/shard_map/pallas_call | solution.py:74
  27.5 0.7 %collective-permute-done.8.block = bf16[224,128]{1,0:T(8,128)(2,1)S(1)} collective-permute-done((bf16[224,128]{1,0:T(8,128)(2,1)S(1)}, bf16[224,128]{1,0:T(8,128)(2,1)S(1)}, u32[]{:S(2)}, u32[]{:S(2)}) %collective-permute-start.8) | collective-permute-done | bytes 57376 | tf_op jit(solution)/shard_map/ppermute | solution.py:68
  28.2 1.1 %shard_map.89 = f32[3,128,512]{2,1,0:T(8,128)} custom-call(s32[1,3]{1,0:T(1,128)S(1)} %copy-done.5, bf16[224,128]{1,0:T(8,128)(2,1)S(1)} %shard_map.87.own, bf16[224,128]{1,0:T(8,128)(2,1)S(1)} %collective-permute-done.8.block, f32[3,128,512]{2,1,0:T(8,128)S(1)} %shard_map.88.products), custom_call_target="tpu_custom_call" | custom-call | flops 1835008 | bytes 1687564 | tf_op jit(solution)/shard_map/pallas_call | solution.py:74
  (8 shorter events, 0.0 us)
Async XLA Ops:
  0.0 5.3 %copy-start = (bf16[2048,1024]{1,0:T(8,128)(2,1)S(1)}, bf16[2048,1024]{1,0:T(8,128)(2,1)}, u32[]{:S(2)}) copy-start(bf16[2048,1024]{1,0:T(8,128)(2,1)} %constant.11.clone.table) | copy-start | bytes 12582916
  2.2 5.0 %collective-permute-start = (f32[16,144]{1,0:T(8,128)S(1)}, f32[16,144]{1,0:T(8,128)S(1)}, u32[]{:S(2)}, u32[]{:S(2)}) collective-permute-start(f32[16,144]{1,0:T(8,128)S(1)} %get-tuple-element.30), channel_id=1, source_target_pairs={{0,1},{1,0},{2,3},{3,2},{4,5},{5,4},{6,7},{7,6},{8,9},{9,8},{10,11... | collective-permute-start | bytes 27656 | tf_op jit(solution)/shard_map/ppermute | solution.py:63
  5.3 1.9 %collective-permute-start.1 = (f32[16,144]{1,0:T(8,128)S(1)}, f32[16,144]{1,0:T(8,128)S(1)}, u32[]{:S(2)}, u32[]{:S(2)}) collective-permute-start(f32[16,144]{1,0:T(8,128)S(1)} %get-tuple-element.31), channel_id=1, source_target_pairs={{1,2},{2,1},{5,6},{6,5},{9,10},{10,9},{13,14},{14,13},{0,4},{3,7},... | collective-permute-start | bytes 27656 | tf_op jit(solution)/shard_map/ppermute | solution.py:63
  5.3 6.0 %copy-start.1 = (bf16[4096,1024]{1,0:T(8,128)(2,1)S(1)}, bf16[4096,1024]{1,0:T(8,128)(2,1)}, u32[]{:S(2)}) copy-start(bf16[4096,1024]{1,0:T(8,128)(2,1)} %constant.10.clone.tapered) | copy-start | bytes 25165828
  7.3 4.0 %copy-start.2 = (bf16[512,512]{1,0:T(8,128)(2,1)S(1)}, bf16[512,512]{1,0:T(8,128)(2,1)}, u32[]{:S(2)}) copy-start(bf16[512,512]{1,0:T(8,128)(2,1)} %constant.13.clone.nearby) | copy-start | bytes 1572868
  7.3 4.0 %copy-start.3 = (f32[1,512]{1,0:T(1,128)S(1)}, f32[1,512]{1,0:T(1,128)}, u32[]{:S(2)}) copy-start(f32[1,512]{1,0:T(1,128)} %constant.14.clone.scale) | copy-start | bytes 6148
  7.3 4.0 %copy-start.4 = (s32[144]{0:T(256)S(1)}, s32[144]{0:T(256)}, u32[]{:S(2)}) copy-start(s32[144]{0:T(256)} %param.9) | copy-start | bytes 1732
  8.1 6.5 %collective-permute-start.2 = (bf16[72,1024]{1,0:T(8,128)(2,1)S(1)}, bf16[72,1024]{1,0:T(8,128)(2,1)S(1)}, u32[]{:S(2)}, u32[]{:S(2)}) collective-permute-start(bf16[72,1024]{1,0:T(8,128)(2,1)S(1)} %get-tuple-element.40), channel_id=1, source_target_pairs={{0,1},{1,0},{2,3},{3,2},{4,5},{5,4},{6,7},{7,6},{8,9},{9,8},{10,11... | collective-permute-start | bytes 442376 | tf_op jit(solution)/shard_map/ppermute | solution.py:63
  11.3 3.3 %collective-permute-start.3 = (bf16[72,1024]{1,0:T(8,128)(2,1)S(1)}, bf16[72,1024]{1,0:T(8,128)(2,1)S(1)}, u32[]{:S(2)}, u32[]{:S(2)}) collective-permute-start(bf16[72,1024]{1,0:T(8,128)(2,1)S(1)} %get-tuple-element.41), channel_id=1, source_target_pairs={{1,2},{2,1},{5,6},{6,5},{9,10},{10,9},{13,14},{14,13},{0,4},{3,7},... | collective-permute-start | bytes 442376 | tf_op jit(solution)/shard_map/ppermute | solution.py:63
  11.3 16.9 %copy-start.5 = (s32[1,3]{1,0:T(1,128)S(1)}, s32[1,3]{1,0:T(1,128)}, u32[]{:S(2)}) copy-start(s32[1,3]{1,0:T(1,128)} %partners.1) | copy-start | bytes 40
  15.1 5.7 %collective-permute-start.4 = (bf16[96,128]{1,0:T(8,128)(2,1)S(1)}, bf16[96,128]{1,0:T(8,128)(2,1)S(1)}, u32[]{:S(2)}, u32[]{:S(2)}) collective-permute-start(bf16[96,128]{1,0:T(8,128)(2,1)S(1)} %get-tuple-element.44), channel_id=1, source_target_pairs={{0,3},{1,2},{2,1},{3,0},{4,7},{5,6},{6,5},{7,4},{8,11},{9,10},{10,... | collective-permute-start | bytes 73736 | tf_op jit(solution)/shard_map/ppermute | solution.py:68
  17.7 4.8 %collective-permute-start.5 = (bf16[96,128]{1,0:T(8,128)(2,1)S(1)}, bf16[96,128]{1,0:T(8,128)(2,1)S(1)}, u32[]{:S(2)}, u32[]{:S(2)}) collective-permute-start(bf16[96,128]{1,0:T(8,128)(2,1)S(1)} %get-tuple-element.45), channel_id=1, source_target_pairs={{0,2},{1,3},{2,0},{3,1},{4,6},{5,7},{6,4},{7,5},{8,10},{9,11},{10,... | collective-permute-start | bytes 73736 | tf_op jit(solution)/shard_map/ppermute | solution.py:68
  18.6 4.1 %collective-permute-start.6 = (bf16[96,128]{1,0:T(8,128)(2,1)S(1)}, bf16[96,128]{1,0:T(8,128)(2,1)S(1)}, u32[]{:S(2)}, u32[]{:S(2)}) collective-permute-start(bf16[96,128]{1,0:T(8,128)(2,1)S(1)} %get-tuple-element.46), channel_id=1, source_target_pairs={{0,1},{1,0},{2,3},{3,2},{4,5},{5,4},{6,7},{7,6},{8,9},{9,8},{10,11... | collective-permute-start | bytes 73736 | tf_op jit(solution)/shard_map/ppermute | solution.py:68
  22.7 4.2 %collective-permute-start.7 = (bf16[224,128]{1,0:T(8,128)(2,1)S(1)}, bf16[224,128]{1,0:T(8,128)(2,1)S(1)}, u32[]{:S(2)}, u32[]{:S(2)}) collective-permute-start(bf16[224,128]{1,0:T(8,128)(2,1)S(1)} %shard_map.87.own), channel_id=1, source_target_pairs={{0,8},{4,12},{8,0},{12,4},{1,9},{5,13},{9,1},{13,5},{2,10},{6,14},... | collective-permute-start | bytes 172040 | tf_op jit(solution)/shard_map/ppermute | solution.py:68
  24.2 2.7 %collective-permute-start.9 = (bf16[224,128]{1,0:T(8,128)(2,1)S(1)}, bf16[224,128]{1,0:T(8,128)(2,1)S(1)}, u32[]{:S(2)}, u32[]{:S(2)}) collective-permute-start(bf16[224,128]{1,0:T(8,128)(2,1)S(1)} %shard_map.87.own), channel_id=1, source_target_pairs={{0,4},{4,0},{8,12},{12,8},{1,5},{5,1},{9,13},{13,9},{2,6},{6,2},{1... | collective-permute-start | bytes 172040 | tf_op jit(solution)/shard_map/ppermute | solution.py:68
  26.9 1.2 %collective-permute-start.8 = (bf16[224,128]{1,0:T(8,128)(2,1)S(1)}, bf16[224,128]{1,0:T(8,128)(2,1)S(1)}, u32[]{:S(2)}, u32[]{:S(2)}) collective-permute-start(bf16[224,128]{1,0:T(8,128)(2,1)S(1)} %collective-permute-done.7.refs_1_), channel_id=1, source_target_pairs={{0,4},{4,0},{8,12},{12,8},{1,5},{5,1},{9,13},{13,9},{2,6},{6,2},{1... | collective-permute-start | bytes 172040 | tf_op jit(solution)/shard_map/ppermute | solution.py:68
